TPU v7x, 32 devices: a whole 2x2x4 slice. The times are simulated.
32 devices in a mesh: ctx: 16 (over z, y, x), head: 2 (over core).
Axes of the slice: x: 2, y: 2, z: 4, core: 2. Of those that a mesh axis runs over, the one named last changes fastest.
Arguments:
- queries: bfloat16 [2, 8192, 2, 512], P(None, 'ctx', 'head'), may hold values from -6 to 6
- key_vectors: bfloat16 [2, 8192, 2, 512], P(None, 'ctx', 'head'), may hold values from -6 to 6
- value_vectors: bfloat16 [2, 8192, 2, 512], P(None, 'ctx', 'head'), may hold values from -6 to 6
- token_rates: float32 [2, 8192, 2], P(None, 'ctx', 'head'), may hold values from 0.02 to 0.5
- fast_init: bfloat16 [2, 3, 512, 512], P('head'), may hold values from -0.25 to 0.25
- out_proj: bfloat16 [2, 512, 2048], P('head'), may hold values from -0.1875 to 0.1875
Outputs:
- layer_out: bfloat16 [2, 8192, 2048], P(None, 'ctx', 'head')
All inputs are finite; a program needn't handle non-finite values.
Results may differ from a plain program's by a relative error of at most 0.018.
Values may be sent and summed in bfloat16 or wider, within the bound.
No kernel may reach another device: no remote copies, remote signals or barrier semaphores. Data moves between devices by JAX's collectives and lax.ppermute only.
A program may use at most 128 MiB of HBM per device.

v0:
```python
import jax
import jax.numpy as jnp
from jax import lax
from jax.sharding import PartitionSpec as P

momentum_beta = 0.9
step_size = 0.03


def silu_of(values):
    return values * jax.nn.sigmoid(values)


def fast_grads(weights_bf, key_rows, value_rows, rates):
    gate_pre = jnp.dot(key_rows, weights_bf[0], preferred_element_type=jnp.float32)
    lin_pre = jnp.dot(key_rows, weights_bf[1], preferred_element_type=jnp.float32)
    sig_gate = jax.nn.sigmoid(gate_pre)
    silu_out = gate_pre * sig_gate
    hidden = (silu_out * lin_pre).astype(jnp.bfloat16)
    out_grad = (rates[:, None] * value_rows.astype(jnp.float32)).astype(jnp.bfloat16)
    hid_grad = lax.dot_general(
        out_grad, weights_bf[2], (((1,), (1,)), ((), ())), preferred_element_type=jnp.float32
    )
    gate_grad = (hid_grad * lin_pre * sig_gate * (1.0 + gate_pre * (1.0 - sig_gate))).astype(
        jnp.bfloat16
    )
    lin_grad = (hid_grad * silu_out).astype(jnp.bfloat16)
    contract = (((0,), (0,)), ((), ()))
    grad_gate = lax.dot_general(key_rows, gate_grad, contract, preferred_element_type=jnp.float32)
    grad_lin = lax.dot_general(key_rows, lin_grad, contract, preferred_element_type=jnp.float32)
    grad_out = lax.dot_general(hidden, out_grad, contract, preferred_element_type=jnp.float32)
    return jnp.stack([grad_gate, grad_lin, grad_out])


def fast_apply(weights_bf, query_rows):
    gate_pre = jnp.dot(query_rows, weights_bf[0], preferred_element_type=jnp.float32)
    lin_pre = jnp.dot(query_rows, weights_bf[1], preferred_element_type=jnp.float32)
    hidden = (silu_of(gate_pre) * lin_pre).astype(jnp.bfloat16)
    return jnp.dot(hidden, weights_bf[2], preferred_element_type=jnp.float32).astype(jnp.bfloat16)


def renorm(weights, moment):
    unit_rows = moment * lax.rsqrt(jnp.mean(moment * moment, axis=-1, keepdims=True) + 1e-05)
    moved = weights + step_size * unit_rows
    old_sq = jnp.mean(weights * weights, axis=-1, keepdims=True) + 1e-06
    new_sq = jnp.mean(moved * moved, axis=-1, keepdims=True) + 1e-06
    return moved * jnp.sqrt(old_sq / new_sq)


def on_device(queries, key_vectors, value_vectors, token_rates, fast_init, out_proj):
    blocks, tok_local, heads_local, head_width = queries.shape
    weights_bf = fast_init
    weights = fast_init.astype(jnp.float32)
    moment = jnp.zeros(weights.shape, jnp.float32)
    results = []
    for block_idx in range(blocks):
        local_terms = jnp.stack(
            [
                fast_grads(
                    weights_bf[0],
                    key_vectors[block_idx, :, 0],
                    value_vectors[block_idx, :, 0],
                    token_rates[block_idx, :, 0],
                )
            ]
        )
        grad_total = lax.psum(local_terms, "ctx")
        moment = momentum_beta * moment + grad_total
        weights = renorm(weights, moment)
        weights_bf = weights.astype(jnp.bfloat16)
        head_outs = fast_apply(weights_bf[0], queries[block_idx, :, 0])
        mixed_out = jnp.dot(head_outs, out_proj[0], preferred_element_type=jnp.float32)
        results.append(
            lax.psum_scatter(
                mixed_out.astype(jnp.bfloat16), "head", scatter_dimension=1, tiled=True
            )
        )
    return jnp.stack(results)


def solution(mesh):
    placed = (
        P(None, "ctx", "head", None),
        P(None, "ctx", "head", None),
        P(None, "ctx", "head", None),
        P(None, "ctx", "head"),
        P("head", None, None, None),
        P("head", None, None),
    )
    return jax.shard_map(
        on_device, mesh=mesh, in_specs=placed, out_specs=P(None, "ctx", "head"), check_vma=False
    )
```

profile of v0, /device:TPU:0, one launch (start us, length us, event | category | flops | bytes accessed | tf_op | source)
XLA Modules:
  0.0 359.3 jit_solution(11550558404274977504)
XLA Ops:
  6.6 1.8 fusion.43
  8.3 1.6 fusion.45
  10.0 1.5 fusion.31
  11.6 0.5 convolution_bitcast_fusion.10
  12.1 0.8 convolution_bitcast_fusion.11
  12.8 0.7 convolution_bitcast_fusion.9
  13.5 2.0 maximum_bitcast_fusion
  15.6 2.6 copy.7
  18.2 147.1 %all-reduce.3.cloned.1.call-done = f32[1,3,512,512]{2,3,1,0:T(8,128)} async-done(((f32[1,3,512,512]{2,3,1,0:T(8,128)}), f32[1,3,512,512]{2,3,1,0:T(8,128)}) %all-reduce.3.cloned.1.call-update) | async-done | bytes 3145744 | tf_op jit(solution)/shard_map/psum | solution.py:67
  165.3 2.4 multiply_reduce_fusion.4
  168.1 2.3 fusion
  170.5 0.7 multiply_convert_fusion.1
  171.2 0.5 convolution_bitcast_fusion.5
  171.6 0.5 convolution_bitcast_fusion.6
  172.1 0.8 copy-done.12
  173.0 0.5 fusion.27
  173.4 0.5 convolution_bitcast_fusion.3
  174.0 0.8 convolution_bitcast_fusion.4
  174.7 0.7 convolution_bitcast_fusion.2
  175.4 2.0 maximum_bitcast_fusion.1
  177.5 1.7 convolution_bitcast_fusion.8
  179.2 3.0 convolution_convert_fusion.3
  182.1 3.7 %convolution_convert_fusion.1 = bf16[512,2048]{1,0:T(8,128)(2,1)} fusion(bf16[512,512]{1,0:T(8,128)(2,1)} %convolution_convert_fusion.3, bf16[1,512,2048]{2,1,0:T(8,128)(2,1)S(1)} %copy-done), kind=kOutput, calls=%fused_computation.14 | convolution fusion | flops 1074790400 | bytes 4718592 | tf_op jit(solution)/shard_map/dot_general | solution.py:72
  186.0 137.5 %all-reduce.5.cloned.1.call-done = f32[1,3,512,512]{2,3,1,0:T(8,128)} async-done(((f32[1,3,512,512]{2,3,1,0:T(8,128)}), f32[1,3,512,512]{2,3,1,0:T(8,128)}) %all-reduce.5.cloned.1.call-update) | async-done | bytes 3145744 | tf_op jit(solution)/shard_map/psum | solution.py:67
  323.6 3.8 %multiply_reduce_fusion.2 = f32[3,512]{1,0:T(4,128)S(1)} fusion(f32[1,3,512,512]{2,3,1,0:T(8,128)} %all-reduce.5.cloned.1.call-done, f32[1,3,512,512]{2,3,1,0:T(8,128)} %all-reduce.3.cloned.1.call-done), kind=kLoop, calls=%fused_computation.9 | loop fusion | flops 3144192 | bytes 6297600 | tf_op jit(solution)/shard_map/reduce_sum | solution.py:43
  327.8 3.5 multiply_reduce_fusion.1
  331.3 1.2 multiply_convert_fusion
  332.6 1.1 copy-done.8
  334.2 3.0 convolution_convert_fusion.2
  337.1 3.6 %convolution_convert_fusion = bf16[512,2048]{1,0:T(8,128)(2,1)} fusion(bf16[512,512]{1,0:T(8,128)(2,1)} %convolution_convert_fusion.2, bf16[1,512,2048]{2,1,0:T(8,128)(2,1)S(1)} %copy-done), kind=kOutput, calls=%fused_computation.13 | convolution fusion | flops 1074790400 | bytes 4718592 | tf_op jit(solution)/shard_map/dot_general | solution.py:72
  340.8 8.9 %reduce-scatter.5.cloned.1.call-done = bf16[512,1024]{1,0:T(8,128)(2,1)} async-done(((bf16[512,2048]{1,0:T(8,128)(2,1)}), bf16[512,1024]{1,0:T(8,128)(2,1)}) %reduce-scatter.5.cloned.1.call-update) | async-done | bytes 1048592 | tf_op jit(solution)/shard_map/reduce_scatter | solution.py:74
  349.7 3.1 pad_maximum_fusion
  (39 shorter events, 1.7 us)
Async XLA Ops:
  6.5 175.6 %copy-start = (bf16[1,512,2048]{2,1,0:T(8,128)(2,1)S(1)}, bf16[1,512,2048]{2,1,0:T(8,128)(2,1)}, u32[]{:S(2)}) copy-start(bf16[1,512,2048]{2,1,0:T(8,128)(2,1)} %param.11) | copy-start | bytes 6291460
  6.5 5.0 %copy-start.7 = (bf16[2,512,1,512]{3,1,2,0:T(8,128)(2,1)S(1)}, bf16[2,512,1,512]{3,1,2,0:T(8,128)(2,1)}, u32[]{:S(2)}) copy-start(bf16[2,512,1,512]{3,1,2,0:T(8,128)(2,1)} %param.7) | copy-start | bytes 3145732
  6.5 3.4 copy-start.10
  6.5 158.7 %all-reduce.3.cloned.1.call-start = ((), (), s32[]{:S(2)}) async-start(), calls=%async_computation.2 | async-start | bytes 6291456 | tf_op jit(solution)/shard_map/psum | solution.py:67
  6.5 3.5 copy-start.11
  15.6 308.0 %all-reduce.5.cloned.1.call-start = ((), (), s32[]{:S(2)}) async-start(), calls=%async_computation.4 | async-start | bytes 6291456 | tf_op jit(solution)/shard_map/psum | solution.py:67
  165.3 2.8 copy-start.1
  167.7 2.8 copy-start.3
  171.2 2.3 copy-start.6
  171.2 1.8 copy-start.12
  177.5 163.3 %reduce-scatter.3.cloned.1.call-start = ((), (), s32[]{:S(2)}) async-start(), calls=%async_computation.3 | async-start | bytes 3145728 | tf_op jit(solution)/shard_map/reduce_scatter | solution.py:74
  185.8 163.9 %reduce-scatter.5.cloned.1.call-start = ((), (), s32[]{:S(2)}) async-start(), calls=%async_computation.5 | async-start | bytes 3145728 | tf_op jit(solution)/shard_map/reduce_scatter | solution.py:74
  323.6 3.8 %copy-start.2 = (f32[1,3,512,512]{2,3,1,0:T(8,128)S(1)}, f32[1,3,512,512]{2,3,1,0:T(8,128)}, u32[]{:S(2)}) copy-start(f32[1,3,512,512]{2,3,1,0:T(8,128)} %all-reduce.3.cloned.1.call-done) | copy-start | bytes 9437188
  323.6 4.2 %copy-start.4 = (bf16[1,3,512,512]{2,3,1,0:T(8,128)(2,1)S(1)}, bf16[1,3,512,512]{2,3,1,0:T(8,128)(2,1)}, u32[]{:S(2)}) copy-start(bf16[1,3,512,512]{2,3,1,0:T(8,128)(2,1)} %copy.7) | copy-start | bytes 4718596
  327.8 3.5 copy-start.5
  331.3 2.4 copy-start.9
  332.6 1.1 copy-start.8
Sparse Core Ops, SparseCore 0:
  15.7 149.5 all-reduce.2
  177.6 145.9 all-reduce.4
  325.8 8.6 reduce-scatter.2
  340.9 8.7 reduce-scatter.4
where the time goes:
time: 360 us; the launch traced here: 359 us
  waiting for transfers between devices  294 us (82%)
  matrix products  25.6 us (7%)
  other arithmetic  21.1 us (6%)
  between operations  13.4 us (4%)
  local copies, waits for them, and re-layouts  5.37 us (1%)
    psum x2, waiting for transfers between devices, on_device(): grad_total = lax.psum(local_terms, 'ctx')  285 us
    reduce_scatter x2, waiting for transfers between devices, on_device(): lax.psum_scatter(mixed_out.astype(jnp.bfloat16), 'head', scatter_dimensio...  8.89 us
    dot_general x2, matrix products, on_device(): jnp.dot(head_outs, out_proj[0], preferred_element_type=jnp.float32)  7.27 us
  transfers between devices with their start and end apart: 4, of which 3 were waited for; matrix products, arithmetic and copies ran while one was open for 7% of the time, Pallas kernels for 0%

commit v1 on v0

v1 whole, which is shorter than its diff:
```python
import functools

import jax
import jax.numpy as jnp
from jax import lax
from jax.experimental import pallas as pl
from jax.experimental.pallas import tpu as pltpu
from jax.sharding import PartitionSpec as P

momentum_beta = 0.9
step_size = 0.03
f32 = jnp.float32
bf16 = jnp.bfloat16
VMEM = pl.BlockSpec(memory_space=pltpu.VMEM)
SMEM = pl.BlockSpec(memory_space=pltpu.SMEM)


def params(mib=40):
    return pltpu.CompilerParams(vmem_limit_bytes=mib * 2**20)


def dot(x, y, contract=((1,), (0,))):
    return lax.dot_general(x, y, (contract, ((), ())), preferred_element_type=f32)


def sigmoid(x):
    return 0.5 * jnp.tanh(0.5 * x) + 0.5


def assemble(me, shard_refs, full):
    shards = len(shard_refs)
    rows = full.shape[1] // shards
    for j, ref in enumerate(shard_refs):
        place = pl.ds(pl.multiple_of((me ^ j) * rows, rows), rows)
        for m in range(full.shape[0]):
            full[m, place, :] = ref[m * rows : (m + 1) * rows, :]


def grads_kernel(shards, first, me_ref, k_ref, v_ref, r_ref, *refs):
    n_w = 1 if first else shards
    w_refs, out_refs = refs[:n_w], refs[n_w : n_w + shards]
    scratch = refs[n_w + shards :]
    da_s, db_s, hid_s, dy_s, g_s = scratch[:5]
    me = me_ref[0]
    if first:
        w = w_refs[0]
    else:
        w = scratch[5]
        assemble(me, w_refs, w)
    tok, width = k_ref.shape
    rate_col = jnp.broadcast_to(r_ref[...], (8, tok)).T[:, :1]
    chunk = min(tok, 256)
    for t in range(0, tok, chunk):
        span = slice(t, t + chunk)
        k = k_ref[span, :]
        a = dot(k, w[0])
        b = dot(k, w[1])
        sig = sigmoid(a)
        silu = a * sig
        hid_s[span, :] = (silu * b).astype(bf16)
        dy = (rate_col[span] * v_ref[span, :].astype(f32)).astype(bf16)
        dy_s[span, :] = dy
        dh = dot(dy, w[2], ((1,), (1,)))
        da_s[span, :] = (dh * b * sig * (1.0 + a * (1.0 - sig))).astype(bf16)
        db_s[span, :] = (dh * silu).astype(bf16)
    over_tokens = ((0,), (0,))
    g_s[0] = dot(k_ref[...], da_s[...], over_tokens).astype(bf16)
    g_s[1] = dot(k_ref[...], db_s[...], over_tokens).astype(bf16)
    g_s[2] = dot(hid_s[...], dy_s[...], over_tokens).astype(bf16)
    rows = width // shards
    for j, out in enumerate(out_refs):
        place = pl.ds(pl.multiple_of((me ^ j) * rows, rows), rows)
        for m in range(3):
            out[m * rows : (m + 1) * rows, :] = g_s[m, place, :]


def local_grads(me, k, v, r, w):
    first = len(w) == 1
    tok, width = k.shape
    shards = SHARDS if first else len(w)
    rows = 3 * width // shards
    scratch = [pltpu.VMEM((tok, width), bf16)] * 4 + [pltpu.VMEM((3, width, width), bf16)]
    if not first:
        scratch.append(pltpu.VMEM((3, width, width), bf16))
    return pl.pallas_call(
        functools.partial(grads_kernel, shards, first),
        out_shape=[jax.ShapeDtypeStruct((rows, width), bf16)] * shards,
        in_specs=[SMEM] + [VMEM] * (3 + len(w)),
        out_specs=[VMEM] * shards,
        scratch_shapes=scratch,
        compiler_params=params(),
        name="grads",
    )(me, k, v, r, *w)


def sum_kernel(*refs):
    total = refs[0][...].astype(f32)
    for ref in refs[1:-1]:
        total = total + ref[...].astype(f32)
    refs[-1][...] = total.astype(bf16)


def sum_parts(parts):
    return pl.pallas_call(
        sum_kernel,
        out_shape=jax.ShapeDtypeStruct(parts[0].shape, bf16),
        in_specs=[VMEM] * len(parts),
        out_specs=VMEM,
        compiler_params=params(),
        name="sum_parts",
    )(*parts)


def update_kernel(first, me_ref, p_ref, q_ref, *refs):
    grad = p_ref[...].astype(f32) + q_ref[...].astype(f32)
    if first:
        init_ref, w_out, m_out, wb_out, w_s = refs
        rows = p_ref.shape[0] // 3
        place = pl.ds(pl.multiple_of(me_ref[0] * rows, rows), rows)
        for m in range(3):
            w_s[m * rows : (m + 1) * rows, :] = init_ref[m, place, :]
        weights = w_s[...].astype(f32)
        moment = grad
    else:
        w_ref, m_ref, wb_out = refs
        weights = w_ref[...]
        moment = momentum_beta * m_ref[...] + grad
    unit = moment * lax.rsqrt(jnp.mean(moment * moment, axis=-1, keepdims=True) + 1e-05)
    moved = weights + step_size * unit
    old_sq = jnp.mean(weights * weights, axis=-1, keepdims=True) + 1e-06
    new_sq = jnp.mean(moved * moved, axis=-1, keepdims=True) + 1e-06
    weights = moved * jnp.sqrt(old_sq / new_sq)
    wb_out[...] = weights.astype(bf16)
    if first:
        w_out[...] = weights
        m_out[...] = moment


def update_first(me, p, q, init):
    shape = p.shape
    return pl.pallas_call(
        functools.partial(update_kernel, True),
        out_shape=[
            jax.ShapeDtypeStruct(shape, f32),
            jax.ShapeDtypeStruct(shape, f32),
            jax.ShapeDtypeStruct(shape, bf16),
        ],
        in_specs=[SMEM] + [VMEM] * 3,
        out_specs=[VMEM] * 3,
        scratch_shapes=[pltpu.VMEM(shape, bf16)],
        compiler_params=params(),
        name="update_first",
    )(me, p, q, init)


def update_next(me, p, q, weights, moment):
    return pl.pallas_call(
        functools.partial(update_kernel, False),
        out_shape=jax.ShapeDtypeStruct(p.shape, bf16),
        in_specs=[SMEM] + [VMEM] * 4,
        out_specs=VMEM,
        compiler_params=params(),
        name="update_next",
    )(me, p, q, weights, moment)


def apply_kernel(shards, me_ref, q_ref, *refs):
    w_refs, out, w = refs[:shards], refs[shards], refs[shards + 1]
    assemble(me_ref[0], w_refs, w)
    tok = q_ref.shape[0]
    chunk = min(tok, 256)
    for t in range(0, tok, chunk):
        span = slice(t, t + chunk)
        q = q_ref[span, :]
        a = dot(q, w[0])
        b = dot(q, w[1])
        hid = (a * sigmoid(a) * b).astype(bf16)
        out[span, :] = dot(hid, w[2]).astype(bf16)


def fast_apply(me, q, w):
    width = q.shape[1]
    return pl.pallas_call(
        functools.partial(apply_kernel, len(w)),
        out_shape=jax.ShapeDtypeStruct(q.shape, bf16),
        in_specs=[SMEM] + [VMEM] * (1 + len(w)),
        out_specs=VMEM,
        scratch_shapes=[pltpu.VMEM((3, width, width), bf16)],
        compiler_params=params(),
        name="apply",
    )(me, q, *w)


def project_kernel(o_ref, other_ref, proj_ref, proj_other_ref, *refs):
    out = refs[-1]
    out[0] = (dot(o_ref[...], proj_ref[...]) + dot(other_ref[...], proj_other_ref[...])).astype(bf16)


def project(block, blocks, o, o_other, proj, proj_other, into):
    tok, width = o.shape
    cols = proj.shape[1]
    part = min(cols, 256)
    whole = pl.BlockSpec((tok, width), lambda i: (0, 0))
    columns = pl.BlockSpec((width, part), lambda i: (0, i))
    args = [o, o_other, proj, proj_other]
    specs = [whole, whole, columns, columns]
    aliases = {}
    if into is not None:
        args.append(into)
        specs.append(pl.BlockSpec(memory_space=pl.ANY))
        aliases = {4: 0}
    return pl.pallas_call(
        project_kernel,
        grid=(cols // part,),
        out_shape=jax.ShapeDtypeStruct((blocks, tok, cols), bf16),
        in_specs=specs,
        out_specs=pl.BlockSpec((1, tok, part), lambda i: (block, 0, i)),
        input_output_aliases=aliases,
        compiler_params=params(),
        name="project",
    )(*args)


SHARDS = 8


def solution(mesh):
    ctx, heads = mesh.shape["ctx"], mesh.shape["head"]
    assert ctx & (ctx - 1) == 0 and ctx >= SHARDS and heads == 2

    def swap(x, bit):
        return lax.ppermute(x, "ctx", [(i, i ^ bit) for i in range(ctx)])

    def swap_head(x):
        return lax.ppermute(x, "head", [(0, 1), (1, 0)])

    order = (1, 2, 4, 3, 5, 6, 7)

    def reduce_parts(parts):
        got = {j: swap(parts[j], j) for j in order}
        p = sum_parts([parts[0]] + [got[j] for j in order])
        bit = SHARDS
        while bit < ctx // 2:
            p = sum_parts([p, swap(p, bit)])
            bit *= 2
        return p, (swap(p, bit) if bit < ctx else jnp.zeros_like(p))

    def gather(part):
        got = {j: swap(part, j) for j in order}
        return [part] + [got[j] for j in range(1, SHARDS)]

    def on_device(queries, key_vectors, value_vectors, token_rates, fast_init, out_proj):
        blocks, tok, _, width = queries.shape
        flat = lambda x: x.reshape(blocks, tok, width)
        q, k, v = flat(queries), flat(key_vectors), flat(value_vectors)
        r = token_rates.reshape(blocks, 1, tok)
        init, proj_all = fast_init[0], out_proj[0]
        me = (lax.axis_index("ctx") % SHARDS).astype(jnp.int32).reshape(1)
        half = proj_all.shape[1] // heads
        head = lax.axis_index("head")
        proj = lax.dynamic_slice_in_dim(proj_all, head * half, half, 1)
        proj_other = swap_head(lax.dynamic_slice_in_dim(proj_all, (1 - head) * half, half, 1))

        result = None
        w = [init]
        weights = moment = None
        for c in range(blocks):
            p, p_other = reduce_parts(local_grads(me, k[c], v[c], r[c], w))
            if c == 0:
                weights, moment, wb = update_first(me, p, p_other, init)
            else:
                wb = update_next(me, p, p_other, weights, moment)
            w = gather(wb)
            o = fast_apply(me, q[c], w)
            result = project(c, blocks, o, swap_head(o), proj, proj_other, result)
        return result

    placed = (
        P(None, "ctx", "head", None),
        P(None, "ctx", "head", None),
        P(None, "ctx", "head", None),
        P(None, "ctx", "head"),
        P("head", None, None, None),
        P("head", None, None),
    )
    return jax.shard_map(on_device, mesh=mesh, in_specs=placed, out_specs=P(None, "ctx", "head"), check_vma=False)
```

time: 360 us -> 127 us (0.35)
  waiting for transfers between devices: 294 us -> 60.1 us
  starting transfers between devices: 0.31 us -> 46 us
  matrix products: 25.6 us -> 0 us
  other arithmetic: 21.1 us -> 0 us
  Pallas kernels: 0 us -> 16 us
  between operations: 13.4 us -> 0.15 us
    psum x2 -> x0, waiting for transfers between devices: 285 us -> none  [on_device(): grad_total = lax.psum(local_terms, 'ctx')]
    ppermute x0 -> x33, waiting for transfers between devices: none -> 60.1 us  [the longest x30 60.1 us: swap(): return lax.ppermute(x, 'ctx', [(i, i ^ bit) for i in range(ctx)])]
    ppermute x0 -> x33, starting transfers between devices: none -> 46 us  [the longest x30 45.8 us: swap(): return lax.ppermute(x, 'ctx', [(i, i ^ bit) for i in range(ctx)])]
    dot_general x18 -> x0, matrix products: 25.6 us -> none  [the longest x2 7.27 us: on_device(): jnp.dot(head_outs, out_proj[0], preferred_element_type=jnp.float32)]
    pallas_call x0 -> x10, Pallas kernels: none -> 16 us  [the longest x2 5.96 us: project(): pl.pallas_call(project_kernel, grid=(cols // part,), out_shape=jax.ShapeD...]
    reduce_sum x4 -> x0, other arithmetic: 12.1 us -> none  [the longest x2 6.21 us: renorm(): jnp.mean(moment * moment, axis=-1, keepdims=True) + 1e-05]
    reduce_scatter x2 -> x0, waiting for transfers between devices: 8.89 us -> none  [on_device(): lax.psum_scatter(mixed_out.astype(jnp.bfloat16), 'head', scatter_dimensio...]
    another operation x3 -> x0, other arithmetic: 7.06 us -> none  [the longest x2 4.01 us: on_device(): jnp.stack([fast_grads(weights_bf[0], key_vectors[block_idx, :, 0], value_...]
  transfers between devices with their start and end apart: 4 -> 33, of which waited for: 3 -> 18; matrix products, arithmetic and copies ran while one was open for 7% -> 1% of each run, Pallas kernels for 0% -> 5%
where the time goes in v1:
time: 127 us
  waiting for transfers between devices  60.1 us (47%)
  starting transfers between devices  46 us (36%)
  Pallas kernels  16 us (13%)
  local copies, waits for them, and re-layouts  4.52 us (4%)
    ppermute x30, waiting for transfers between devices, swap(): return lax.ppermute(x, 'ctx', [(i, i ^ bit) for i in range(ctx)])  60.1 us
    ppermute x30, starting transfers between devices, swap(): return lax.ppermute(x, 'ctx', [(i, i ^ bit) for i in range(ctx)])  45.8 us
    pallas_call x2, Pallas kernels, project(): pl.pallas_call(project_kernel, grid=(cols // part,), out_shape=jax.ShapeD...  5.96 us
    pallas_call x2, Pallas kernels, local_grads(): pl.pallas_call(functools.partial(grads_kernel, shards, first), out_shape=...  5.59 us
  transfers between devices with their start and end apart: 33, of which 18 were waited for; matrix products, arithmetic and copies ran while one was open for 1% of the time, Pallas kernels for 5%

profile of v1, /device:TPU:0, one launch (start us, length us, event | category | flops | bytes accessed | tf_op | source)
XLA Modules:
  0.0 126.8 jit_solution(6030096400515761762)
XLA Ops:
  0.7 1.8 %slice_bitcast_fusion.1 = (bf16[512,512]{1,0:T(8,128)(2,1)S(1)}, bf16[512,512]{1,0:T(8,128)(2,1)S(1)}, bf16[512,512]{1,0:T(8,128)(2,1)S(1)}, bf16[512,512]{1,0:T(8,128)(2,1)S(1)}) fusion(bf16[2,512,1,512]{3,1,2,0:T(8,128)(2,1)} %param.8, bf16[2,512,1,512]{3,1,2,0:T(8,128)(2,1)} %param.7), kind=kLoop, calls=%fused_computation.3 | loop fusion | bytes 4194304 | tf_op jit(solution)/shard_map/squeeze | solution.py:268
  2.7 2.4 %grads.2 = (bf16[192,512]{1,0:T(8,128)(2,1)S(1)}, bf16[192,512]{1,0:T(8,128)(2,1)S(1)}, bf16[192,512]{1,0:T(8,128)(2,1)S(1)}, bf16[192,512]{1,0:T(8,128)(2,1)S(1...) custom-call(s32[1]{0:T(128)} %bitcast.me_ref, ...), custom_call_target="tpu_custom_call" | custom-call | tf_op jit(solution)/shard_map/grads/pallas_call | solution.py:85
  5.1 3.0 %collective-permute-start = (bf16[192,512]{1,0:T(8,128)(2,1)S(1)}, bf16[192,512]{1,0:T(8,128)(2,1)S(1)}, u32[]{:S(2)}, u32[]{:S(2)}) collective-permute-start(bf16[192,512]{1,0:T(8,128)(2,1)S(1)} %get-tuple-element.25), channel_id=1, source_target_pairs={{0,2},{2,0},{4,6},{6,4},{8,10},{10,8},{12,14},{14,12},{16,18},{18,... | collective-permute-start | bytes 589832 | tf_op jit(solution)/shard_map/ppermute | solution.py:232
  13.4 5.0 %collective-permute-start.5 = (bf16[192,512]{1,0:T(8,128)(2,1)S(1)}, bf16[192,512]{1,0:T(8,128)(2,1)S(1)}, u32[]{:S(2)}, u32[]{:S(2)}) collective-permute-start(bf16[192,512]{1,0:T(8,128)(2,1)S(1)} %get-tuple-element.30), channel_id=1, source_target_pairs={{0,12},{2,14},{4,8},{6,10},{8,4},{10,6},{12,0},{14,2},{16,28},{18,... | collective-permute-start | bytes 589832 | tf_op jit(solution)/shard_map/ppermute | solution.py:232
  19.4 10.2 %collective-permute-done.3.refs_4_ = bf16[192,512]{1,0:T(8,128)(2,1)S(1)} collective-permute-done((bf16[192,512]{1,0:T(8,128)(2,1)S(1)}, bf16[192,512]{1,0:T(8,128)(2,1)S(1)}, u32[]{:S(2)}, u32[]{:S(2)}) %collective-permute-start.3) | collective-permute-done | bytes 196640 | tf_op jit(solution)/shard_map/ppermute | solution.py:232
  29.8 2.6 %collective-permute-start.7 = (bf16[192,512]{1,0:T(8,128)(2,1)S(1)}, bf16[192,512]{1,0:T(8,128)(2,1)S(1)}, u32[]{:S(2)}, u32[]{:S(2)}) collective-permute-start(bf16[192,512]{1,0:T(8,128)(2,1)S(1)} %sum_parts.2.p_ref), channel_id=1, source_target_pairs={{0,16},{2,18},{4,20},{6,22},{8,24},{10,26},{12,28},{14,30},{16,0},... | collective-permute-start | bytes 589832 | tf_op jit(solution)/shard_map/ppermute | solution.py:232
  32.4 7.5 %collective-permute-done.7.q_ref = bf16[192,512]{1,0:T(8,128)(2,1)S(1)} collective-permute-done((bf16[192,512]{1,0:T(8,128)(2,1)S(1)}, bf16[192,512]{1,0:T(8,128)(2,1)S(1)}, u32[]{:S(2)}, u32[]{:S(2)}) %collective-permute-start.7) | collective-permute-done | bytes 196640 | tf_op jit(solution)/shard_map/ppermute | solution.py:232
  44.1 2.1 %collective-permute-start.12 = (bf16[192,512]{1,0:T(8,128)(2,1)S(1)}, bf16[192,512]{1,0:T(8,128)(2,1)S(1)}, u32[]{:S(2)}, u32[]{:S(2)}) collective-permute-start(bf16[192,512]{1,0:T(8,128)(2,1)S(1)} %get-tuple-element.32.refs_0_), channel_id=1, source_target_pairs={{0,10},{2,8},{4,14},{6,12},{8,2},{10,0},{12,6},{14,4},{16,26},{18,... | collective-permute-start | bytes 589832 | tf_op jit(solution)/shard_map/ppermute | solution.py:232
  46.2 3.1 %collective-permute-done.8.refs_1_ = bf16[192,512]{1,0:T(8,128)(2,1)S(1)} collective-permute-done((bf16[192,512]{1,0:T(8,128)(2,1)S(1)}, bf16[192,512]{1,0:T(8,128)(2,1)S(1)}, u32[]{:S(2)}, u32[]{:S(2)}) %collective-permute-start.8) | collective-permute-done | bytes 196640 | tf_op jit(solution)/shard_map/ppermute | solution.py:232
  49.3 3.2 %collective-permute-start.14 = (bf16[192,512]{1,0:T(8,128)(2,1)S(1)}, bf16[192,512]{1,0:T(8,128)(2,1)S(1)}, u32[]{:S(2)}, u32[]{:S(2)}) collective-permute-start(bf16[192,512]{1,0:T(8,128)(2,1)S(1)} %get-tuple-element.32.refs_0_), channel_id=1, source_target_pairs={{0,14},{2,12},{4,10},{6,8},{8,6},{10,4},{12,2},{14,0},{16,30},{18,... | collective-permute-start | bytes 589832 | tf_op jit(solution)/shard_map/ppermute | solution.py:232
  52.9 3.3 %collective-permute-done.12.refs_5_ = bf16[192,512]{1,0:T(8,128)(2,1)S(1)} collective-permute-done((bf16[192,512]{1,0:T(8,128)(2,1)S(1)}, bf16[192,512]{1,0:T(8,128)(2,1)S(1)}, u32[]{:S(2)}, u32[]{:S(2)}) %collective-permute-start.12) | collective-permute-done | bytes 196640 | tf_op jit(solution)/shard_map/ppermute | solution.py:232
  56.2 3.3 %collective-permute-done.13.refs_6_ = bf16[192,512]{1,0:T(8,128)(2,1)S(1)} collective-permute-done((bf16[192,512]{1,0:T(8,128)(2,1)S(1)}, bf16[192,512]{1,0:T(8,128)(2,1)S(1)}, u32[]{:S(2)}, u32[]{:S(2)}) %collective-permute-start.13) | collective-permute-done | bytes 196640 | tf_op jit(solution)/shard_map/ppermute | solution.py:232
  59.5 2.6 %collective-permute-done.14.refs_7_ = bf16[192,512]{1,0:T(8,128)(2,1)S(1)} collective-permute-done((bf16[192,512]{1,0:T(8,128)(2,1)S(1)}, bf16[192,512]{1,0:T(8,128)(2,1)S(1)}, u32[]{:S(2)}, u32[]{:S(2)}) %collective-permute-start.14) | collective-permute-done | bytes 196640 | tf_op jit(solution)/shard_map/ppermute | solution.py:232
  62.1 3.2 %grads.3 = (bf16[192,512]{1,0:T(8,128)(2,1)S(1)}, bf16[192,512]{1,0:T(8,128)(2,1)S(1)}, bf16[192,512]{1,0:T(8,128)(2,1)S(1)}, bf16[192,512]{1,0:T(8,128)(2,1)}, ...) custom-call(s32[1]{0:T(128)} %bitcast.me_ref, ...), custom_call_target="tpu_custom_call" | custom-call | tf_op jit(solution)/shard_map/grads/pallas_call | solution.py:85
  66.1 1.7 %collective-permute-start.16 = (bf16[192,512]{1,0:T(8,128)(2,1)S(1)}, bf16[192,512]{1,0:T(8,128)(2,1)S(1)}, u32[]{:S(2)}, u32[]{:S(2)}) collective-permute-start(bf16[192,512]{1,0:T(8,128)(2,1)S(1)} %get-tuple-element.35), channel_id=1, source_target_pairs={{0,4},{2,6},{4,0},{6,2},{8,12},{10,14},{12,8},{14,10},{16,20},{18,... | collective-permute-start | bytes 589832 | tf_op jit(solution)/shard_map/ppermute | solution.py:232
  68.1 1.9 %collective-permute-start.18 = (bf16[192,512]{1,0:T(8,128)(2,1)}, bf16[192,512]{1,0:T(8,128)(2,1)S(1)}, u32[]{:S(2)}, u32[]{:S(2)}) collective-permute-start(bf16[192,512]{1,0:T(8,128)(2,1)} %get-tuple-element.37), channel_id=1, source_target_pairs={{0,6},{2,4},{4,2},{6,0},{8,14},{10,12},{12,10},{14,8},{16,22},{18,... | collective-permute-start | bytes 589832 | tf_op jit(solution)/shard_map/ppermute | solution.py:232
  71.1 3.0 %collective-permute-done.15.refs_1_ = bf16[192,512]{1,0:T(8,128)(2,1)S(1)} collective-permute-done((bf16[192,512]{1,0:T(8,128)(2,1)S(1)}, bf16[192,512]{1,0:T(8,128)(2,1)S(1)}, u32[]{:S(2)}, u32[]{:S(2)}) %collective-permute-start.15) | collective-permute-done | bytes 196640 | tf_op jit(solution)/shard_map/ppermute | solution.py:232
  74.1 2.1 %collective-permute-start.20 = (bf16[192,512]{1,0:T(8,128)(2,1)}, bf16[192,512]{1,0:T(8,128)(2,1)}, u32[]{:S(2)}, u32[]{:S(2)}) collective-permute-start(bf16[192,512]{1,0:T(8,128)(2,1)} %get-tuple-element.39), channel_id=1, source_target_pairs={{0,12},{2,14},{4,8},{6,10},{8,4},{10,6},{12,0},{14,2},{16,28},{18,... | collective-permute-start | bytes 589832 | tf_op jit(solution)/shard_map/ppermute | solution.py:232
  76.2 1.9 %collective-permute-start.21 = (bf16[192,512]{1,0:T(8,128)(2,1)}, bf16[192,512]{1,0:T(8,128)(2,1)}, u32[]{:S(2)}, u32[]{:S(2)}) collective-permute-start(bf16[192,512]{1,0:T(8,128)(2,1)} %get-tuple-element.40), channel_id=1, source_target_pairs={{0,14},{2,12},{4,10},{6,8},{8,6},{10,4},{12,2},{14,0},{16,30},{18,... | collective-permute-start | bytes 589832 | tf_op jit(solution)/shard_map/ppermute | solution.py:232
  78.1 3.7 %collective-permute-done.18.refs_4_ = bf16[192,512]{1,0:T(8,128)(2,1)S(1)} collective-permute-done((bf16[192,512]{1,0:T(8,128)(2,1)}, bf16[192,512]{1,0:T(8,128)(2,1)S(1)}, u32[]{:S(2)}, u32[]{:S(2)}) %collective-permute-start.18) | collective-permute-done | bytes 196640 | tf_op jit(solution)/shard_map/ppermute | solution.py:232
  83.1 2.6 %collective-permute-done.21.refs_7_ = bf16[192,512]{1,0:T(8,128)(2,1)} collective-permute-done((bf16[192,512]{1,0:T(8,128)(2,1)}, bf16[192,512]{1,0:T(8,128)(2,1)}, u32[]{:S(2)}, u32[]{:S(2)}) %collective-permute-start.21) | collective-permute-done | bytes 196640 | tf_op jit(solution)/shard_map/ppermute | solution.py:232
  87.0 3.2 %collective-permute-start.22 = (bf16[192,512]{1,0:T(8,128)(2,1)S(1)}, bf16[192,512]{1,0:T(8,128)(2,1)S(1)}, u32[]{:S(2)}, u32[]{:S(2)}) collective-permute-start(bf16[192,512]{1,0:T(8,128)(2,1)S(1)} %sum_parts.3.p_ref), channel_id=1, source_target_pairs={{0,16},{2,18},{4,20},{6,22},{8,24},{10,26},{12,28},{14,30},{16,0},... | collective-permute-start | bytes 589832 | tf_op jit(solution)/shard_map/ppermute | solution.py:232
  90.2 1.7 %dynamic-slice_bitcast_fusion = (bf16[512,1024]{1,0:T(8,128)(2,1)S(1)}, bf16[512,1024]{1,0:T(8,128)(2,1)S(1)}) fusion(bf16[1,512,2048]{2,1,0:T(8,128)(2,1)} %param.11, s32[]{:T(128)S(6)} %select_n.15, s32[]{:T(128)S(6)} %select_n.14), kind=kLoop, calls=%fused_computation | loop fusion | bytes 4194312 | tf_op jit(solution)/shard_map/dynamic_slice | solution.py:262
  92.0 4.0 %collective-permute-done.22.q_ref = bf16[192,512]{1,0:T(8,128)(2,1)S(1)} collective-permute-done((bf16[192,512]{1,0:T(8,128)(2,1)S(1)}, bf16[192,512]{1,0:T(8,128)(2,1)S(1)}, u32[]{:S(2)}, u32[]{:S(2)}) %collective-permute-start.22) | collective-permute-done | bytes 196640 | tf_op jit(solution)/shard_map/ppermute | solution.py:232
  100.5 4.8 %collective-permute-done.23.refs_1_ = bf16[192,512]{1,0:T(8,128)(2,1)S(1)} collective-permute-done((bf16[192,512]{1,0:T(8,128)(2,1)S(1)}, bf16[192,512]{1,0:T(8,128)(2,1)S(1)}, u32[]{:S(2)}, u32[]{:S(2)}) %collective-permute-start.23) | collective-permute-done | bytes 196640 | tf_op jit(solution)/shard_map/ppermute | solution.py:232
  105.3 2.8 %collective-permute-start.28 = (bf16[192,512]{1,0:T(8,128)(2,1)S(1)}, bf16[192,512]{1,0:T(8,128)(2,1)S(1)}, u32[]{:S(2)}, u32[]{:S(2)}) collective-permute-start(bf16[192,512]{1,0:T(8,128)(2,1)S(1)} %update_next.1.refs_0_), channel_id=1, source_target_pairs={{0,12},{2,14},{4,8},{6,10},{8,4},{10,6},{12,0},{14,2},{16,28},{18,... | collective-permute-start | bytes 589832 | tf_op jit(solution)/shard_map/ppermute | solution.py:232
  108.1 1.8 %collective-permute-done.25.refs_3_ = bf16[192,512]{1,0:T(8,128)(2,1)S(1)} collective-permute-done((bf16[192,512]{1,0:T(8,128)(2,1)S(1)}, bf16[192,512]{1,0:T(8,128)(2,1)S(1)}, u32[]{:S(2)}, u32[]{:S(2)}) %collective-permute-start.25) | collective-permute-done | bytes 196640 | tf_op jit(solution)/shard_map/ppermute | solution.py:232
  111.4 2.6 %collective-permute-done.27.refs_5_ = bf16[192,512]{1,0:T(8,128)(2,1)S(1)} collective-permute-done((bf16[192,512]{1,0:T(8,128)(2,1)S(1)}, bf16[192,512]{1,0:T(8,128)(2,1)S(1)}, u32[]{:S(2)}, u32[]{:S(2)}) %collective-permute-start.27) | collective-permute-done | bytes 196640 | tf_op jit(solution)/shard_map/ppermute | solution.py:232
  114.0 2.7 %collective-permute-done.28.refs_6_ = bf16[192,512]{1,0:T(8,128)(2,1)S(1)} collective-permute-done((bf16[192,512]{1,0:T(8,128)(2,1)S(1)}, bf16[192,512]{1,0:T(8,128)(2,1)S(1)}, u32[]{:S(2)}, u32[]{:S(2)}) %collective-permute-start.28) | collective-permute-done | bytes 196640 | tf_op jit(solution)/shard_map/ppermute | solution.py:232
  116.7 2.8 %collective-permute-done.29.refs_7_ = bf16[192,512]{1,0:T(8,128)(2,1)S(1)} collective-permute-done((bf16[192,512]{1,0:T(8,128)(2,1)S(1)}, bf16[192,512]{1,0:T(8,128)(2,1)S(1)}, u32[]{:S(2)}, u32[]{:S(2)}) %collective-permute-start.29) | collective-permute-done | bytes 196640 | tf_op jit(solution)/shard_map/ppermute | solution.py:232
  120.9 3.0 %project.2.refs_0_ = bf16[2,512,1024]{2,1,0:T(8,128)(2,1)} custom-call(bf16[512,512]{1,0:T(8,128)(2,1)S(1)} %apply.3.o_ref, bf16[512,512]{1,0:T(8,128)(2,1)S(1)} %collective-permute-done.32.other_ref, bf16[512,1024]{1,0:T(8,128)(2,1)S(1)} %get-tuple-element.44.proj_ref, bf16[512,1024]{1,0:T(8,128)(2,1)S(1)} %collective-permute-done.31.proj_other_ref), custom_call_target="tpu_custom_call" | custom-call | tf_op jit(solution)/shard_map/project/pallas_call | solution.py:212
  123.9 3.0 %project.3 = bf16[2,512,1024]{2,1,0:T(8,128)(2,1)} custom-call(bf16[512,512]{1,0:T(8,128)(2,1)S(1)} %apply.2.o_ref, bf16[512,512]{1,0:T(8,128)(2,1)S(1)} %collective-permute-done.30.other_ref, bf16[512,1024]{1,0:T(8,128)(2,1)S(1)} %get-tuple-element.44.proj_ref, ...), custom_call_target="tpu_custom_call", output_to_operand_aliasing={{}: (4, {})} | custom-call | tf_op jit(solution)/shard_map/project/pallas_call | solution.py:212
  (52 shorter events, 24.0 us)
Async XLA Ops:
  5.1 8.3 %collective-permute-start = (bf16[192,512]{1,0:T(8,128)(2,1)S(1)}, bf16[192,512]{1,0:T(8,128)(2,1)S(1)}, u32[]{:S(2)}, u32[]{:S(2)}) collective-permute-start(bf16[192,512]{1,0:T(8,128)(2,1)S(1)} %get-tuple-element.25), channel_id=1, source_target_pairs={{0,2},{2,0},{4,6},{6,4},{8,10},{10,8},{12,14},{14,12},{16,18},{18,... | collective-permute-start | bytes 589832 | tf_op jit(solution)/shard_map/ppermute | solution.py:232
  8.1 10.3 %collective-permute-start.1 = (bf16[192,512]{1,0:T(8,128)(2,1)S(1)}, bf16[192,512]{1,0:T(8,128)(2,1)S(1)}, u32[]{:S(2)}, u32[]{:S(2)}) collective-permute-start(bf16[192,512]{1,0:T(8,128)(2,1)S(1)} %get-tuple-element.26), channel_id=1, source_target_pairs={{0,4},{2,6},{4,0},{6,2},{8,12},{10,14},{12,8},{14,10},{16,20},{18,... | collective-permute-start | bytes 589832 | tf_op jit(solution)/shard_map/ppermute | solution.py:232
  9.6 9.8 %collective-permute-start.2 = (bf16[192,512]{1,0:T(8,128)(2,1)S(1)}, bf16[192,512]{1,0:T(8,128)(2,1)S(1)}, u32[]{:S(2)}, u32[]{:S(2)}) collective-permute-start(bf16[192,512]{1,0:T(8,128)(2,1)S(1)} %get-tuple-element.27), channel_id=1, source_target_pairs={{0,8},{2,10},{4,12},{6,14},{8,0},{10,2},{12,4},{14,6},{16,24},{18,... | collective-permute-start | bytes 589832 | tf_op jit(solution)/shard_map/ppermute | solution.py:232
  11.2 18.3 %collective-permute-start.3 = (bf16[192,512]{1,0:T(8,128)(2,1)S(1)}, bf16[192,512]{1,0:T(8,128)(2,1)S(1)}, u32[]{:S(2)}, u32[]{:S(2)}) collective-permute-start(bf16[192,512]{1,0:T(8,128)(2,1)S(1)} %get-tuple-element.28), channel_id=1, source_target_pairs={{0,6},{2,4},{4,2},{6,0},{8,14},{10,12},{12,10},{14,8},{16,22},{18,... | collective-permute-start | bytes 589832 | tf_op jit(solution)/shard_map/ppermute | solution.py:232
  11.7 17.9 %collective-permute-start.4 = (bf16[192,512]{1,0:T(8,128)(2,1)S(1)}, bf16[192,512]{1,0:T(8,128)(2,1)S(1)}, u32[]{:S(2)}, u32[]{:S(2)}) collective-permute-start(bf16[192,512]{1,0:T(8,128)(2,1)S(1)} %get-tuple-element.29), channel_id=1, source_target_pairs={{0,10},{2,8},{4,14},{6,12},{8,2},{10,0},{12,6},{14,4},{16,26},{18,... | collective-permute-start | bytes 589832 | tf_op jit(solution)/shard_map/ppermute | solution.py:232
  13.4 16.2 %collective-permute-start.5 = (bf16[192,512]{1,0:T(8,128)(2,1)S(1)}, bf16[192,512]{1,0:T(8,128)(2,1)S(1)}, u32[]{:S(2)}, u32[]{:S(2)}) collective-permute-start(bf16[192,512]{1,0:T(8,128)(2,1)S(1)} %get-tuple-element.30), channel_id=1, source_target_pairs={{0,12},{2,14},{4,8},{6,10},{8,4},{10,6},{12,0},{14,2},{16,28},{18,... | collective-permute-start | bytes 589832 | tf_op jit(solution)/shard_map/ppermute | solution.py:232
  18.4 11.1 %collective-permute-start.6 = (bf16[192,512]{1,0:T(8,128)(2,1)S(1)}, bf16[192,512]{1,0:T(8,128)(2,1)S(1)}, u32[]{:S(2)}, u32[]{:S(2)}) collective-permute-start(bf16[192,512]{1,0:T(8,128)(2,1)S(1)} %get-tuple-element.31), channel_id=1, source_target_pairs={{0,14},{2,12},{4,10},{6,8},{8,6},{10,4},{12,2},{14,0},{16,30},{18,... | collective-permute-start | bytes 589832 | tf_op jit(solution)/shard_map/ppermute | solution.py:232
  29.8 10.1 %collective-permute-start.7 = (bf16[192,512]{1,0:T(8,128)(2,1)S(1)}, bf16[192,512]{1,0:T(8,128)(2,1)S(1)}, u32[]{:S(2)}, u32[]{:S(2)}) collective-permute-start(bf16[192,512]{1,0:T(8,128)(2,1)S(1)} %sum_parts.2.p_ref), channel_id=1, source_target_pairs={{0,16},{2,18},{4,20},{6,22},{8,24},{10,26},{12,28},{14,30},{16,0},... | collective-permute-start | bytes 589832 | tf_op jit(solution)/shard_map/ppermute | solution.py:232
  40.2 9.1 %collective-permute-start.8 = (bf16[192,512]{1,0:T(8,128)(2,1)S(1)}, bf16[192,512]{1,0:T(8,128)(2,1)S(1)}, u32[]{:S(2)}, u32[]{:S(2)}) collective-permute-start(bf16[192,512]{1,0:T(8,128)(2,1)S(1)} %get-tuple-element.32.refs_0_), channel_id=1, source_target_pairs={{0,2},{2,0},{4,6},{6,4},{8,10},{10,8},{12,14},{14,12},{16,18},{18,... | collective-permute-start | bytes 589832 | tf_op jit(solution)/shard_map/ppermute | solution.py:232
  41.2 8.1 %collective-permute-start.9 = (bf16[192,512]{1,0:T(8,128)(2,1)S(1)}, bf16[192,512]{1,0:T(8,128)(2,1)S(1)}, u32[]{:S(2)}, u32[]{:S(2)}) collective-permute-start(bf16[192,512]{1,0:T(8,128)(2,1)S(1)} %get-tuple-element.32.refs_0_), channel_id=1, source_target_pairs={{0,4},{2,6},{4,0},{6,2},{8,12},{10,14},{12,8},{14,10},{16,20},{18,... | collective-permute-start | bytes 589832 | tf_op jit(solution)/shard_map/ppermute | solution.py:232
  42.2 10.8 %collective-permute-start.10 = (bf16[192,512]{1,0:T(8,128)(2,1)S(1)}, bf16[192,512]{1,0:T(8,128)(2,1)S(1)}, u32[]{:S(2)}, u32[]{:S(2)}) collective-permute-start(bf16[192,512]{1,0:T(8,128)(2,1)S(1)} %get-tuple-element.32.refs_0_), channel_id=1, source_target_pairs={{0,6},{2,4},{4,2},{6,0},{8,14},{10,12},{12,10},{14,8},{16,22},{18,... | collective-permute-start | bytes 589832 | tf_op jit(solution)/shard_map/ppermute | solution.py:232
  43.7 9.2 %collective-permute-start.11 = (bf16[192,512]{1,0:T(8,128)(2,1)S(1)}, bf16[192,512]{1,0:T(8,128)(2,1)S(1)}, u32[]{:S(2)}, u32[]{:S(2)}) collective-permute-start(bf16[192,512]{1,0:T(8,128)(2,1)S(1)} %get-tuple-element.32.refs_0_), channel_id=1, source_target_pairs={{0,8},{2,10},{4,12},{6,14},{8,0},{10,2},{12,4},{14,6},{16,24},{18,... | collective-permute-start | bytes 589832 | tf_op jit(solution)/shard_map/ppermute | solution.py:232
  44.1 12.1 %collective-permute-start.12 = (bf16[192,512]{1,0:T(8,128)(2,1)S(1)}, bf16[192,512]{1,0:T(8,128)(2,1)S(1)}, u32[]{:S(2)}, u32[]{:S(2)}) collective-permute-start(bf16[192,512]{1,0:T(8,128)(2,1)S(1)} %get-tuple-element.32.refs_0_), channel_id=1, source_target_pairs={{0,10},{2,8},{4,14},{6,12},{8,2},{10,0},{12,6},{14,4},{16,26},{18,... | collective-permute-start | bytes 589832 | tf_op jit(solution)/shard_map/ppermute | solution.py:232
  49.3 10.2 %collective-permute-start.13 = (bf16[192,512]{1,0:T(8,128)(2,1)S(1)}, bf16[192,512]{1,0:T(8,128)(2,1)S(1)}, u32[]{:S(2)}, u32[]{:S(2)}) collective-permute-start(bf16[192,512]{1,0:T(8,128)(2,1)S(1)} %get-tuple-element.32.refs_0_), channel_id=1, source_target_pairs={{0,12},{2,14},{4,8},{6,10},{8,4},{10,6},{12,0},{14,2},{16,28},{18,... | collective-permute-start | bytes 589832 | tf_op jit(solution)/shard_map/ppermute | solution.py:232
  49.3 12.8 %collective-permute-start.14 = (bf16[192,512]{1,0:T(8,128)(2,1)S(1)}, bf16[192,512]{1,0:T(8,128)(2,1)S(1)}, u32[]{:S(2)}, u32[]{:S(2)}) collective-permute-start(bf16[192,512]{1,0:T(8,128)(2,1)S(1)} %get-tuple-element.32.refs_0_), channel_id=1, source_target_pairs={{0,14},{2,12},{4,10},{6,8},{8,6},{10,4},{12,2},{14,0},{16,30},{18,... | collective-permute-start | bytes 589832 | tf_op jit(solution)/shard_map/ppermute | solution.py:232
  65.3 8.8 %collective-permute-start.15 = (bf16[192,512]{1,0:T(8,128)(2,1)S(1)}, bf16[192,512]{1,0:T(8,128)(2,1)S(1)}, u32[]{:S(2)}, u32[]{:S(2)}) collective-permute-start(bf16[192,512]{1,0:T(8,128)(2,1)S(1)} %get-tuple-element.34), channel_id=1, source_target_pairs={{0,2},{2,0},{4,6},{6,4},{8,10},{10,8},{12,14},{14,12},{16,18},{18,... | collective-permute-start | bytes 589832 | tf_op jit(solution)/shard_map/ppermute | solution.py:232
  66.1 10.1 %collective-permute-start.16 = (bf16[192,512]{1,0:T(8,128)(2,1)S(1)}, bf16[192,512]{1,0:T(8,128)(2,1)S(1)}, u32[]{:S(2)}, u32[]{:S(2)}) collective-permute-start(bf16[192,512]{1,0:T(8,128)(2,1)S(1)} %get-tuple-element.35), channel_id=1, source_target_pairs={{0,4},{2,6},{4,0},{6,2},{8,12},{10,14},{12,8},{14,10},{16,20},{18,... | collective-permute-start | bytes 589832 | tf_op jit(solution)/shard_map/ppermute | solution.py:232
  67.8 10.3 %collective-permute-start.17 = (bf16[192,512]{1,0:T(8,128)(2,1)}, bf16[192,512]{1,0:T(8,128)(2,1)S(1)}, u32[]{:S(2)}, u32[]{:S(2)}) collective-permute-start(bf16[192,512]{1,0:T(8,128)(2,1)} %get-tuple-element.36), channel_id=1, source_target_pairs={{0,8},{2,10},{4,12},{6,14},{8,0},{10,2},{12,4},{14,6},{16,24},{18,... | collective-permute-start | bytes 589832 | tf_op jit(solution)/shard_map/ppermute | solution.py:232
  68.1 13.7 %collective-permute-start.18 = (bf16[192,512]{1,0:T(8,128)(2,1)}, bf16[192,512]{1,0:T(8,128)(2,1)S(1)}, u32[]{:S(2)}, u32[]{:S(2)}) collective-permute-start(bf16[192,512]{1,0:T(8,128)(2,1)} %get-tuple-element.37), channel_id=1, source_target_pairs={{0,6},{2,4},{4,2},{6,0},{8,14},{10,12},{12,10},{14,8},{16,22},{18,... | collective-permute-start | bytes 589832 | tf_op jit(solution)/shard_map/ppermute | solution.py:232
  70.0 11.9 %collective-permute-start.19 = (bf16[192,512]{1,0:T(8,128)(2,1)}, bf16[192,512]{1,0:T(8,128)(2,1)S(1)}, u32[]{:S(2)}, u32[]{:S(2)}) collective-permute-start(bf16[192,512]{1,0:T(8,128)(2,1)} %get-tuple-element.38), channel_id=1, source_target_pairs={{0,10},{2,8},{4,14},{6,12},{8,2},{10,0},{12,6},{14,4},{16,26},{18,... | collective-permute-start | bytes 589832 | tf_op jit(solution)/shard_map/ppermute | solution.py:232
  74.1 9.0 %collective-permute-start.20 = (bf16[192,512]{1,0:T(8,128)(2,1)}, bf16[192,512]{1,0:T(8,128)(2,1)}, u32[]{:S(2)}, u32[]{:S(2)}) collective-permute-start(bf16[192,512]{1,0:T(8,128)(2,1)} %get-tuple-element.39), channel_id=1, source_target_pairs={{0,12},{2,14},{4,8},{6,10},{8,4},{10,6},{12,0},{14,2},{16,28},{18,... | collective-permute-start | bytes 589832 | tf_op jit(solution)/shard_map/ppermute | solution.py:232
  76.2 9.5 %collective-permute-start.21 = (bf16[192,512]{1,0:T(8,128)(2,1)}, bf16[192,512]{1,0:T(8,128)(2,1)}, u32[]{:S(2)}, u32[]{:S(2)}) collective-permute-start(bf16[192,512]{1,0:T(8,128)(2,1)} %get-tuple-element.40), channel_id=1, source_target_pairs={{0,14},{2,12},{4,10},{6,8},{8,6},{10,4},{12,2},{14,0},{16,30},{18,... | collective-permute-start | bytes 589832 | tf_op jit(solution)/shard_map/ppermute | solution.py:232
  87.0 9.0 %collective-permute-start.22 = (bf16[192,512]{1,0:T(8,128)(2,1)S(1)}, bf16[192,512]{1,0:T(8,128)(2,1)S(1)}, u32[]{:S(2)}, u32[]{:S(2)}) collective-permute-start(bf16[192,512]{1,0:T(8,128)(2,1)S(1)} %sum_parts.3.p_ref), channel_id=1, source_target_pairs={{0,16},{2,18},{4,20},{6,22},{8,24},{10,26},{12,28},{14,30},{16,0},... | collective-permute-start | bytes 589832 | tf_op jit(solution)/shard_map/ppermute | solution.py:232
  91.9 29.0 %collective-permute-start.31 = (bf16[512,1024]{1,0:T(8,128)(2,1)S(1)}, bf16[512,1024]{1,0:T(8,128)(2,1)S(1)}, u32[]{:S(2)}, u32[]{:S(2)}) collective-permute-start(bf16[512,1024]{1,0:T(8,128)(2,1)S(1)} %get-tuple-element.43), channel_id=1, source_target_pairs={{0,1},{1,0},{2,3},{3,2},{4,5},{5,4},{6,7},{7,6},{8,9},{9,8},{10,11... | collective-permute-start | bytes 3145736 | tf_op jit(solution)/shard_map/ppermute | solution.py:235
  96.2 9.1 %collective-permute-start.23 = (bf16[192,512]{1,0:T(8,128)(2,1)S(1)}, bf16[192,512]{1,0:T(8,128)(2,1)S(1)}, u32[]{:S(2)}, u32[]{:S(2)}) collective-permute-start(bf16[192,512]{1,0:T(8,128)(2,1)S(1)} %update_next.1.refs_0_), channel_id=1, source_target_pairs={{0,2},{2,0},{4,6},{6,4},{8,10},{10,8},{12,14},{14,12},{16,18},{18,... | collective-permute-start | bytes 589832 | tf_op jit(solution)/shard_map/ppermute | solution.py:232
  97.0 8.3 %collective-permute-start.24 = (bf16[192,512]{1,0:T(8,128)(2,1)S(1)}, bf16[192,512]{1,0:T(8,128)(2,1)S(1)}, u32[]{:S(2)}, u32[]{:S(2)}) collective-permute-start(bf16[192,512]{1,0:T(8,128)(2,1)S(1)} %update_next.1.refs_0_), channel_id=1, source_target_pairs={{0,4},{2,6},{4,0},{6,2},{8,12},{10,14},{12,8},{14,10},{16,20},{18,... | collective-permute-start | bytes 589832 | tf_op jit(solution)/shard_map/ppermute | solution.py:232
  98.3 11.6 %collective-permute-start.25 = (bf16[192,512]{1,0:T(8,128)(2,1)S(1)}, bf16[192,512]{1,0:T(8,128)(2,1)S(1)}, u32[]{:S(2)}, u32[]{:S(2)}) collective-permute-start(bf16[192,512]{1,0:T(8,128)(2,1)S(1)} %update_next.1.refs_0_), channel_id=1, source_target_pairs={{0,6},{2,4},{4,2},{6,0},{8,14},{10,12},{12,10},{14,8},{16,22},{18,... | collective-permute-start | bytes 589832 | tf_op jit(solution)/shard_map/ppermute | solution.py:232
  99.8 11.5 %collective-permute-start.26 = (bf16[192,512]{1,0:T(8,128)(2,1)S(1)}, bf16[192,512]{1,0:T(8,128)(2,1)S(1)}, u32[]{:S(2)}, u32[]{:S(2)}) collective-permute-start(bf16[192,512]{1,0:T(8,128)(2,1)S(1)} %update_next.1.refs_0_), channel_id=1, source_target_pairs={{0,8},{2,10},{4,12},{6,14},{8,0},{10,2},{12,4},{14,6},{16,24},{18,... | collective-permute-start | bytes 589832 | tf_op jit(solution)/shard_map/ppermute | solution.py:232
  105.3 8.7 %collective-permute-start.27 = (bf16[192,512]{1,0:T(8,128)(2,1)S(1)}, bf16[192,512]{1,0:T(8,128)(2,1)S(1)}, u32[]{:S(2)}, u32[]{:S(2)}) collective-permute-start(bf16[192,512]{1,0:T(8,128)(2,1)S(1)} %update_next.1.refs_0_), channel_id=1, source_target_pairs={{0,10},{2,8},{4,14},{6,12},{8,2},{10,0},{12,6},{14,4},{16,26},{18,... | collective-permute-start | bytes 589832 | tf_op jit(solution)/shard_map/ppermute | solution.py:232
  105.3 11.4 %collective-permute-start.28 = (bf16[192,512]{1,0:T(8,128)(2,1)S(1)}, bf16[192,512]{1,0:T(8,128)(2,1)S(1)}, u32[]{:S(2)}, u32[]{:S(2)}) collective-permute-start(bf16[192,512]{1,0:T(8,128)(2,1)S(1)} %update_next.1.refs_0_), channel_id=1, source_target_pairs={{0,12},{2,14},{4,8},{6,10},{8,4},{10,6},{12,0},{14,2},{16,28},{18,... | collective-permute-start | bytes 589832 | tf_op jit(solution)/shard_map/ppermute | solution.py:232
  110.0 9.6 %collective-permute-start.29 = (bf16[192,512]{1,0:T(8,128)(2,1)S(1)}, bf16[192,512]{1,0:T(8,128)(2,1)S(1)}, u32[]{:S(2)}, u32[]{:S(2)}) collective-permute-start(bf16[192,512]{1,0:T(8,128)(2,1)S(1)} %update_next.1.refs_0_), channel_id=1, source_target_pairs={{0,14},{2,12},{4,10},{6,8},{8,6},{10,4},{12,2},{14,0},{16,30},{18,... | collective-permute-start | bytes 589832 | tf_op jit(solution)/shard_map/ppermute | solution.py:232
  111.3 9.6 %collective-permute-start.32 = (bf16[512,512]{1,0:T(8,128)(2,1)S(1)}, bf16[512,512]{1,0:T(8,128)(2,1)S(1)}, u32[]{:S(2)}, u32[]{:S(2)}) collective-permute-start(bf16[512,512]{1,0:T(8,128)(2,1)S(1)} %apply.3.o_ref), channel_id=1, source_target_pairs={{0,1},{1,0},{2,3},{3,2},{4,5},{5,4},{6,7},{7,6},{8,9},{9,8},{10,11... | collective-permute-start | bytes 1572872 | tf_op jit(solution)/shard_map/ppermute | solution.py:235
  (3 other events, 28.1 us)

commit v2 on v1

v2 whole, which is shorter than its diff:
```python
import functools

import jax
import jax.numpy as jnp
from jax import lax
from jax.experimental import pallas as pl
from jax.experimental.pallas import tpu as pltpu
from jax.sharding import PartitionSpec as P

momentum_beta = 0.9
step_size = 0.03
f32 = jnp.float32
bf16 = jnp.bfloat16
VMEM = pl.BlockSpec(memory_space=pltpu.VMEM)
SMEM = pl.BlockSpec(memory_space=pltpu.SMEM)


def params(mib=40):
    return pltpu.CompilerParams(vmem_limit_bytes=mib * 2**20)


def dot(x, y, contract=((1,), (0,))):
    return lax.dot_general(x, y, (contract, ((), ())), preferred_element_type=f32)


def sigmoid(x):
    return 0.5 * jnp.tanh(0.5 * x) + 0.5


def base_row(owner, width):
    return ((owner % 2) * (SHARDS // 2) + owner // 2) * (width // SHARDS)


def pieces_of(chunk, mine):
    found = [(i, 0, r) for i, r in enumerate((0, 2, 4, 6))]
    return found + [(4, i * mine, r) for i, r in enumerate((1, 3, 5, 7))]


def assemble(me, refs, full):
    width = full.shape[1]
    chunks = len(refs) // 5
    rows = width // SHARDS // chunks
    for h in range(chunks):
        for i, first, r in pieces_of(h, 3 * rows):
            ref = refs[5 * h + i]
            place = pl.ds(pl.multiple_of(base_row(me ^ r, width) + h * rows, rows), rows)
            for m in range(3):
                full[m, place, :] = ref[first + m * rows : first + (m + 1) * rows, :]


def grads_kernel(first, me_ref, k_ref, v_ref, r_ref, *refs):
    n_w = 1 if first else 5 * CHUNKS
    w_refs, out_refs = refs[:n_w], refs[n_w : n_w + 2 * CHUNKS]
    scratch = refs[n_w + 2 * CHUNKS :]
    da_s, db_s, hid_s, dy_s, g_s = scratch[:5]
    me = me_ref[0]
    if first:
        w = w_refs[0]
    else:
        w = scratch[5]
        assemble(me, w_refs, w)
    tok, width = k_ref.shape
    rate_col = jnp.broadcast_to(r_ref[...], (8, tok)).T[:, :1]
    chunk = min(tok, 256)
    for t in range(0, tok, chunk):
        span = slice(t, t + chunk)
        k = k_ref[span, :]
        a = dot(k, w[0])
        b = dot(k, w[1])
        sig = sigmoid(a)
        silu = a * sig
        hid_s[span, :] = (silu * b).astype(bf16)
        dy = (rate_col[span] * v_ref[span, :].astype(f32)).astype(bf16)
        dy_s[span, :] = dy
        dh = dot(dy, w[2], ((1,), (1,)))
        da_s[span, :] = (dh * b * sig * (1.0 + a * (1.0 - sig))).astype(bf16)
        db_s[span, :] = (dh * silu).astype(bf16)
    over_tokens = ((0,), (0,))
    g_s[0] = dot(k_ref[...], da_s[...], over_tokens).astype(bf16)
    g_s[1] = dot(k_ref[...], db_s[...], over_tokens).astype(bf16)
    g_s[2] = dot(hid_s[...], dy_s[...], over_tokens).astype(bf16)
    rows = width // SHARDS // CHUNKS
    for h in range(CHUNKS):
        for out, relative in ((out_refs[2 * h], (1, 3, 5, 7)), (out_refs[2 * h + 1], (0, 2, 4, 6))):
            for i, r in enumerate(relative):
                place = pl.ds(pl.multiple_of(base_row(me ^ r, width) + h * rows, rows), rows)
                for m in range(3):
                    row = (3 * i + m) * rows
                    out[row : row + rows, :] = g_s[m, place, :]


def local_grads(me, k, v, r, block, w):
    first = len(w) == 1
    _, tok, width = k.shape
    rows = 3 * width // 2 // CHUNKS
    scratch = [pltpu.VMEM((tok, width), bf16)] * 4 + [pltpu.VMEM((3, width, width), bf16)]
    if not first:
        scratch.append(pltpu.VMEM((3, width, width), bf16))
    of_block = lambda *shape: pl.BlockSpec((None, *shape), lambda i: (block, 0, 0))
    return pl.pallas_call(
        functools.partial(grads_kernel, first),
        grid=(1,),
        out_shape=[jax.ShapeDtypeStruct((rows, width), bf16)] * (2 * CHUNKS),
        in_specs=[SMEM, of_block(tok, width), of_block(tok, width), of_block(1, tok)] + [VMEM] * len(w),
        out_specs=[VMEM] * (2 * CHUNKS),
        scratch_shapes=scratch,
        compiler_params=params(),
        name="grads",
    )(me, k, v, r, *w)


def update_kernel(first, chunk, keep, me_ref, p_ref, q_ref, *refs):
    grad = p_ref[...].astype(f32) + q_ref[...].astype(f32)
    if first:
        init_ref, *refs, w_s = refs
        width = init_ref.shape[1]
        rows = p_ref.shape[0] // 3
        place = pl.ds(pl.multiple_of(base_row(me_ref[0], width) + chunk * rows, rows), rows)
        for m in range(3):
            w_s[m * rows : (m + 1) * rows, :] = init_ref[m, place, :]
        weights = w_s[...].astype(f32)
        moment = grad
    else:
        w_ref, m_ref, *refs = refs
        weights = w_ref[...]
        moment = momentum_beta * m_ref[...] + grad
    unit = moment * lax.rsqrt(jnp.mean(moment * moment, axis=-1, keepdims=True) + 1e-05)
    moved = weights + step_size * unit
    old_sq = jnp.mean(weights * weights, axis=-1, keepdims=True) + 1e-06
    new_sq = jnp.mean(moved * moved, axis=-1, keepdims=True) + 1e-06
    weights = moved * jnp.sqrt(old_sq / new_sq)
    refs[0][...] = weights.astype(bf16)
    if keep:
        refs[1][...] = weights
        refs[2][...] = moment


def update(me, p, q, chunk, state, init, keep):
    shape = p.shape
    first = state is None
    out = [jax.ShapeDtypeStruct(shape, bf16)] + [jax.ShapeDtypeStruct(shape, f32)] * (2 if keep else 0)
    state = [init] if first else state
    got = pl.pallas_call(
        functools.partial(update_kernel, first, chunk, keep),
        out_shape=out,
        in_specs=[SMEM] + [VMEM] * (2 + len(state)),
        out_specs=[VMEM] * len(out),
        scratch_shapes=[pltpu.VMEM(shape, bf16)] if first else [],
        compiler_params=params(),
        name="update",
    )(me, p, q, *state)
    return got[0], got[1:]


def apply_kernel(n_w, me_ref, q_ref, *refs):
    w_refs, out, w = refs[:n_w], refs[n_w], refs[n_w + 1]
    assemble(me_ref[0], w_refs, w)
    tok = q_ref.shape[0]
    chunk = min(tok, 256)
    for t in range(0, tok, chunk):
        span = slice(t, t + chunk)
        q = q_ref[span, :]
        a = dot(q, w[0])
        b = dot(q, w[1])
        hid = (a * sigmoid(a) * b).astype(bf16)
        out[span, :] = dot(hid, w[2]).astype(bf16)


def fast_apply(me, q, block, w):
    _, tok, width = q.shape
    return pl.pallas_call(
        functools.partial(apply_kernel, len(w)),
        grid=(1,),
        out_shape=jax.ShapeDtypeStruct((tok, width), bf16),
        in_specs=[SMEM, pl.BlockSpec((None, tok, width), lambda i: (block, 0, 0))] + [VMEM] * len(w),
        out_specs=VMEM,
        scratch_shapes=[pltpu.VMEM((3, width, width), bf16)],
        compiler_params=params(),
        name="apply",
    )(me, q, *w)


def project_kernel(o_ref, other_ref, proj_ref, proj_other_ref, *refs):
    out = refs[-1]
    out[0] = (dot(o_ref[...], proj_ref[...]) + dot(other_ref[...], proj_other_ref[...])).astype(bf16)


def project(block, blocks, o, o_other, proj, proj_other, into):
    tok, width = o.shape
    cols = proj.shape[1]
    part = min(cols, 256)
    whole = pl.BlockSpec((tok, width), lambda i: (0, 0))
    columns = pl.BlockSpec((width, part), lambda i: (0, i))
    args = [o, o_other, proj, proj_other]
    specs = [whole, whole, columns, columns]
    aliases = {}
    if into is not None:
        args.append(into)
        specs.append(pl.BlockSpec(memory_space=pl.ANY))
        aliases = {4: 0}
    return pl.pallas_call(
        project_kernel,
        grid=(cols // part,),
        out_shape=jax.ShapeDtypeStruct((blocks, tok, cols), bf16),
        in_specs=specs,
        out_specs=pl.BlockSpec((1, tok, part), lambda i: (block, 0, i)),
        input_output_aliases=aliases,
        compiler_params=params(),
        name="project",
    )(*args)


SHARDS = 8
CHUNKS = 2


def swap_low_bits(i):
    return (i & ~3) | ((i & 1) << 1) | ((i >> 1) & 1)


def tie(x, other):
    return lax.optimization_barrier((x, other))[0]


def solution(mesh):
    ctx, heads = mesh.shape["ctx"], mesh.shape["head"]
    assert ctx & (ctx - 1) == 0 and ctx >= SHARDS and heads == 2

    def swap(x, bits):
        pairs = [(2 * i, 2 * (i ^ bits)) for i in range(ctx)]
        pairs += [(2 * i + 1, 2 * (i ^ swap_low_bits(bits)) + 1) for i in range(ctx)]
        return lax.ppermute(x, ("ctx", "head"), pairs)

    def swap_head(x):
        return lax.ppermute(x, "head", [(0, 1), (1, 0)])

    def add(x, y):
        return x.astype(f32) + y.astype(f32)

    def reduce_chunk(send, keep):
        total = add(keep, swap(send, 1))
        n = total.shape[0] // 4
        mine = total[:n]
        for i, bits in ((2, 4), (3, 6), (1, 2)):
            mine = add(mine, swap(total[i * n : (i + 1) * n].astype(bf16), bits))
        p = mine.astype(bf16)
        bit = SHARDS
        while bit < ctx // 2:
            p = add(p, swap(p, bit)).astype(bf16)
            bit *= 2
        return p, (swap(p, bit) if bit < ctx else jnp.zeros_like(p))

    def gather(part):
        near = [part] + [swap(part, bits) for bits in (2, 4, 6)]
        return near + [swap(jnp.concatenate(near), 1)]

    def on_device(queries, key_vectors, value_vectors, token_rates, fast_init, out_proj):
        blocks, tok, _, width = queries.shape
        flat = lambda x: x.reshape(blocks, tok, width)
        q, k, v = flat(queries), flat(key_vectors), flat(value_vectors)
        r = token_rates.reshape(blocks, 1, tok)
        init, proj_all = fast_init[0], out_proj[0]
        head = lax.axis_index("head")
        label = (lax.axis_index("ctx") % SHARDS).astype(jnp.int32)
        me = jnp.where(head == 0, label, swap_low_bits(label)).reshape(1)
        half = proj_all.shape[1] // heads
        proj = lax.dynamic_slice_in_dim(proj_all, head * half, half, 1)
        proj_other = swap_head(lax.dynamic_slice_in_dim(proj_all, (1 - head) * half, half, 1))

        result = None
        w = [init]
        state = [None] * CHUNKS
        for c in range(blocks):
            grads = local_grads(me, k, v, r, c, w)
            w = []
            for h in range(CHUNKS):
                p, p_other = reduce_chunk(grads[2 * h], grads[2 * h + 1])
                wb, state[h] = update(me, p, p_other, h, state[h], init, c + 1 < blocks)
                w += gather(wb)
            o = fast_apply(me, q, c, w)
            result = project(c, blocks, o, swap_head(o), proj, proj_other, result)
        return result

    placed = (
        P(None, "ctx", "head", None),
        P(None, "ctx", "head", None),
        P(None, "ctx", "head", None),
        P(None, "ctx", "head"),
        P("head", None, None, None),
        P("head", None, None),
    )
    return jax.shard_map(on_device, mesh=mesh, in_specs=placed, out_specs=P(None, "ctx", "head"), check_vma=False)
```

time: 127 us -> 115 us (0.906)
  waiting for transfers between devices: 60.1 us -> 46.3 us
  other arithmetic: 0 us -> 1.8 us
    ppermute x30 -> x36, waiting for transfers between devices: 60.1 us -> 46.3 us  [swap(): return lax.ppermute(x, ('ctx', 'head'), pairs)]
    unnamed x4 -> x16, local copies, waits for them, and re-layouts: 0.27 us -> 4.56 us
    squeeze x3 -> x0, local copies, waits for them, and re-layouts: 2.54 us -> none  [the longest x2 2.47 us: on_device(): p, p_other = reduce_parts(local_grads(me, k[c], v[c], r[c], w))]
    dynamic_slice x1, local copies, waits for them, and re-layouts: 1.71 us -> 0.2 us  [on_device(): lax.dynamic_slice_in_dim(proj_all, (1 - head) * half, half, 1)]
    another operation x0 -> x4, other arithmetic: none -> 1.5 us
    ppermute x30 -> x36, starting transfers between devices: 45.8 us -> 46 us  [swap(): return lax.ppermute(x, ('ctx', 'head'), pairs)]
  transfers between devices with their start and end apart: 33 -> 39, of which waited for: 18 -> 22; matrix products, arithmetic and copies ran while one was open for 1% -> 2% of each run, Pallas kernels for 5% -> 6%
where the time goes in v2:
time: 115 us; the launch traced here: 114 us
  waiting for transfers between devices  46.3 us (40%)
  starting transfers between devices  46.2 us (40%)
  Pallas kernels  15 us (13%)
  local copies, waits for them, and re-layouts  4.85 us (4%)
  other arithmetic  1.8 us (2%)
    ppermute x36, waiting for transfers between devices, swap(): return lax.ppermute(x, ('ctx', 'head'), pairs)  46.3 us
    ppermute x36, starting transfers between devices, swap(): return lax.ppermute(x, ('ctx', 'head'), pairs)  46 us
    pallas_call x2, Pallas kernels, project(): pl.pallas_call(project_kernel, grid=(cols // part,), out_shape=jax.ShapeD...  5.96 us
    pallas_call x2, Pallas kernels, local_grads(): pl.pallas_call(functools.partial(grads_kernel, first), grid=(1,), out_sha...  5.57 us
    unnamed x16, local copies, waits for them, and re-layouts  4.56 us
    pallas_call x2, Pallas kernels, fast_apply(): pl.pallas_call(functools.partial(apply_kernel, len(w)), grid=(1,), out_sh...  2.54 us
  transfers between devices with their start and end apart: 39, of which 22 were waited for; matrix products, arithmetic and copies ran while one was open for 2% of the time, Pallas kernels for 6%

profile of v2, /device:TPU:0, one launch (start us, length us, event | category | flops | bytes accessed | tf_op | source)
XLA Modules:
  0.0 114.5 jit_solution(3223608990759315312)
XLA Ops:
  4.5 2.4 %grads.2 = (bf16[384,512]{1,0:T(8,128)(2,1)S(1)}, bf16[384,512]{1,0:T(8,128)(2,1)S(1)}, bf16[384,512]{1,0:T(8,128)(2,1)S(1)}, bf16[384,512]{1,0:T(8,128)(2,1)S(1)}) custom-call(s32[1]{0:T(128)} %bitcast.me_ref, bf16[2,512,512]{2,1,0:T(8,128)(2,1)S(1)} %bitcast.13, bf16[2,512,512]{2,1,0:T(8,128)(2,1)S(1)} %bitcast.15, f32[2,1,512]{2,1,0:T(1,128)S(1)} %bitcast.19, ...), custom_call_target="tpu_custom_call" | custom-call | tf_op jit(solution)/shard_map/grads/pallas_call | solution.py:100
  6.9 3.0 %collective-permute-start = (bf16[384,512]{1,0:T(8,128)(2,1)S(1)}, bf16[384,512]{1,0:T(8,128)(2,1)S(1)}, u32[]{:S(2)}, u32[]{:S(2)}) collective-permute-start(bf16[384,512]{1,0:T(8,128)(2,1)S(1)} %get-tuple-element.20), channel_id=1, source_target_pairs={{0,2},{2,0},{4,6},{6,4},{8,10},{10,8},{12,14},{14,12},{16,18},{18,... | collective-permute-start | bytes 1179656 | tf_op jit(solution)/shard_map/ppermute | solution.py:232
  10.0 5.7 %collective-permute-done = bf16[384,512]{1,0:T(8,128)(2,1)S(1)} collective-permute-done((bf16[384,512]{1,0:T(8,128)(2,1)S(1)}, bf16[384,512]{1,0:T(8,128)(2,1)S(1)}, u32[]{:S(2)}, u32[]{:S(2)}) %collective-permute-start) | collective-permute-done | bytes 393248 | tf_op jit(solution)/shard_map/ppermute | solution.py:232
  15.8 2.2 %collective-permute-start.1 = (bf16[96,512]{1,0:T(8,128)(2,1)S(1)}, bf16[96,512]{1,0:T(8,128)(2,1)S(1)}, u32[]{:S(2)}, u32[]{:S(2)}) collective-permute-start(bf16[96,512]{1,0:T(8,128)(2,1)S(1)} %get-tuple-element.52), channel_id=1, source_target_pairs={{0,8},{2,10},{4,12},{6,14},{8,0},{10,2},{12,4},{14,6},{16,24},{18,... | collective-permute-start | bytes 294920 | tf_op jit(solution)/shard_map/ppermute | solution.py:232
  18.0 1.5 %collective-permute-start.3 = (bf16[96,512]{1,0:T(8,128)(2,1)S(1)}, bf16[96,512]{1,0:T(8,128)(2,1)S(1)}, u32[]{:S(2)}, u32[]{:S(2)}) collective-permute-start(bf16[96,512]{1,0:T(8,128)(2,1)S(1)} %get-tuple-element.53), channel_id=1, source_target_pairs={{0,4},{2,6},{4,0},{6,2},{8,12},{10,14},{12,8},{14,10},{16,20},{18,... | collective-permute-start | bytes 294920 | tf_op jit(solution)/shard_map/ppermute | solution.py:232
  19.6 1.8 %collective-permute-done.9 = bf16[384,512]{1,0:T(8,128)(2,1)S(1)} collective-permute-done((bf16[384,512]{1,0:T(8,128)(2,1)S(1)}, bf16[384,512]{1,0:T(8,128)(2,1)S(1)}, u32[]{:S(2)}, u32[]{:S(2)}) %collective-permute-start.9) | collective-permute-done | bytes 393248 | tf_op jit(solution)/shard_map/ppermute | solution.py:232
  21.5 3.0 %collective-permute-start.10 = (bf16[96,512]{1,0:T(8,128)(2,1)S(1)}, bf16[96,512]{1,0:T(8,128)(2,1)S(1)}, u32[]{:S(2)}, u32[]{:S(2)}) collective-permute-start(bf16[96,512]{1,0:T(8,128)(2,1)S(1)} %get-tuple-element.49), channel_id=1, source_target_pairs={{0,8},{2,10},{4,12},{6,14},{8,0},{10,2},{12,4},{14,6},{16,24},{18,... | collective-permute-start | bytes 294920 | tf_op jit(solution)/shard_map/ppermute | solution.py:232
  24.5 1.4 %collective-permute-start.12 = (bf16[96,512]{1,0:T(8,128)(2,1)S(1)}, bf16[96,512]{1,0:T(8,128)(2,1)S(1)}, u32[]{:S(2)}, u32[]{:S(2)}) collective-permute-start(bf16[96,512]{1,0:T(8,128)(2,1)S(1)} %get-tuple-element.50), channel_id=1, source_target_pairs={{0,4},{2,6},{4,0},{6,2},{8,12},{10,14},{12,8},{14,10},{16,20},{18,... | collective-permute-start | bytes 294920 | tf_op jit(solution)/shard_map/ppermute | solution.py:232
  26.1 2.6 %collective-permute-start.4 = (bf16[96,512]{1,0:T(8,128)(2,1)S(1)}, bf16[96,512]{1,0:T(8,128)(2,1)S(1)}, u32[]{:S(2)}, u32[]{:S(2)}) collective-permute-start(bf16[96,512]{1,0:T(8,128)(2,1)S(1)} %fusion.11.p_ref), channel_id=1, source_target_pairs={{0,16},{2,18},{4,20},{6,22},{8,24},{10,26},{12,28},{14,30},{16,0},... | collective-permute-start | bytes 294920 | tf_op jit(solution)/shard_map/ppermute | solution.py:232
  29.1 2.8 %collective-permute-done.11 = bf16[96,512]{1,0:T(8,128)(2,1)S(1)} collective-permute-done((bf16[96,512]{1,0:T(8,128)(2,1)S(1)}, bf16[96,512]{1,0:T(8,128)(2,1)S(1)}, u32[]{:S(2)}, u32[]{:S(2)}) %collective-permute-start.11) | collective-permute-done | bytes 98336 | tf_op jit(solution)/shard_map/ppermute | solution.py:232
  31.9 2.3 %collective-permute-start.13 = (bf16[96,512]{1,0:T(8,128)(2,1)S(1)}, bf16[96,512]{1,0:T(8,128)(2,1)S(1)}, u32[]{:S(2)}, u32[]{:S(2)}) collective-permute-start(bf16[96,512]{1,0:T(8,128)(2,1)S(1)} %fusion.8.p_ref), channel_id=1, source_target_pairs={{0,16},{2,18},{4,20},{6,22},{8,24},{10,26},{12,28},{14,30},{16,0},... | collective-permute-start | bytes 294920 | tf_op jit(solution)/shard_map/ppermute | solution.py:232
  35.8 2.0 %collective-permute-start.6 = (bf16[96,512]{1,0:T(8,128)(2,1)S(1)}, bf16[96,512]{1,0:T(8,128)(2,1)S(1)}, u32[]{:S(2)}, u32[]{:S(2)}) collective-permute-start(bf16[96,512]{1,0:T(8,128)(2,1)S(1)} %get-tuple-element.21.refs_0_), channel_id=1, source_target_pairs={{0,8},{2,10},{4,12},{6,14},{8,0},{10,2},{12,4},{14,6},{16,24},{18,... | collective-permute-start | bytes 294920 | tf_op jit(solution)/shard_map/ppermute | solution.py:232
  39.5 2.0 %collective-permute-start.15 = (bf16[96,512]{1,0:T(8,128)(2,1)S(1)}, bf16[96,512]{1,0:T(8,128)(2,1)S(1)}, u32[]{:S(2)}, u32[]{:S(2)}) collective-permute-start(bf16[96,512]{1,0:T(8,128)(2,1)S(1)} %get-tuple-element.24.refs_5_), channel_id=1, source_target_pairs={{0,8},{2,10},{4,12},{6,14},{8,0},{10,2},{12,4},{14,6},{16,24},{18,... | collective-permute-start | bytes 294920 | tf_op jit(solution)/shard_map/ppermute | solution.py:232
  42.1 2.4 %collective-permute-done.5.refs_1_ = bf16[96,512]{1,0:T(8,128)(2,1)S(1)} collective-permute-done((bf16[96,512]{1,0:T(8,128)(2,1)S(1)}, bf16[96,512]{1,0:T(8,128)(2,1)S(1)}, u32[]{:S(2)}, u32[]{:S(2)}) %collective-permute-start.5) | collective-permute-done | bytes 98336 | tf_op jit(solution)/shard_map/ppermute | solution.py:232
  45.2 2.0 %collective-permute-done.14.refs_6_ = bf16[96,512]{1,0:T(8,128)(2,1)S(1)} collective-permute-done((bf16[96,512]{1,0:T(8,128)(2,1)S(1)}, bf16[96,512]{1,0:T(8,128)(2,1)S(1)}, u32[]{:S(2)}, u32[]{:S(2)}) %collective-permute-start.14) | collective-permute-done | bytes 98336 | tf_op jit(solution)/shard_map/ppermute | solution.py:232
  48.3 4.0 %collective-permute-done.8.refs_4_ = bf16[384,512]{1,0:T(8,128)(2,1)S(1)} collective-permute-done((bf16[384,512]{1,0:T(8,128)(2,1)S(1)}, bf16[384,512]{1,0:T(8,128)(2,1)S(1)}, u32[]{:S(2)}, u32[]{:S(2)}) %collective-permute-start.8) | collective-permute-done | bytes 393248 | tf_op jit(solution)/shard_map/ppermute | solution.py:232
  52.4 4.2 %collective-permute-done.17.refs_9_ = bf16[384,512]{1,0:T(8,128)(2,1)S(1)} collective-permute-done((bf16[384,512]{1,0:T(8,128)(2,1)S(1)}, bf16[384,512]{1,0:T(8,128)(2,1)S(1)}, u32[]{:S(2)}, u32[]{:S(2)}) %collective-permute-start.17) | collective-permute-done | bytes 393248 | tf_op jit(solution)/shard_map/ppermute | solution.py:232
  56.6 3.2 %grads.3 = (bf16[384,512]{1,0:T(8,128)(2,1)}, bf16[384,512]{1,0:T(8,128)(2,1)S(1)}, bf16[384,512]{1,0:T(8,128)(2,1)S(1)}, bf16[384,512]{1,0:T(8,128)(2,1)S(1)}) custom-call(s32[1]{0:T(128)} %bitcast.me_ref, bf16[2,512,512]{2,1,0:T(8,128)(2,1)S(1)} %bitcast.14, bf16[2,512,512]{2,1,0:T(8,128)(2,1)S(1)} %bitcast.16, f32[2,1,512]{2,1,0:T(1,128)S(1)} %bitcast.20, ...), custom_call_target="tpu_custom_call" | custom-call | tf_op jit(solution)/shard_map/grads/pallas_call | solution.py:100
  59.8 2.0 %collective-permute-start.27 = (bf16[384,512]{1,0:T(8,128)(2,1)S(1)}, bf16[384,512]{1,0:T(8,128)(2,1)S(1)}, u32[]{:S(2)}, u32[]{:S(2)}) collective-permute-start(bf16[384,512]{1,0:T(8,128)(2,1)S(1)} %get-tuple-element.30), channel_id=1, source_target_pairs={{0,2},{2,0},{4,6},{6,4},{8,10},{10,8},{12,14},{14,12},{16,18},{18,... | collective-permute-start | bytes 1179656 | tf_op jit(solution)/shard_map/ppermute | solution.py:232
  61.8 8.2 %collective-permute-done.18 = bf16[384,512]{1,0:T(8,128)(2,1)} collective-permute-done((bf16[384,512]{1,0:T(8,128)(2,1)}, bf16[384,512]{1,0:T(8,128)(2,1)}, u32[]{:S(2)}, u32[]{:S(2)}) %collective-permute-start.18) | collective-permute-done | bytes 393248 | tf_op jit(solution)/shard_map/ppermute | solution.py:232
  71.3 3.4 %collective-permute-start.20 = (bf16[96,512]{1,0:T(8,128)(2,1)S(1)}, bf16[96,512]{1,0:T(8,128)(2,1)S(1)}, u32[]{:S(2)}, u32[]{:S(2)}) collective-permute-start(bf16[96,512]{1,0:T(8,128)(2,1)S(1)} %get-tuple-element.48), channel_id=1, source_target_pairs={{0,12},{2,14},{4,8},{6,10},{8,4},{10,6},{12,0},{14,2},{16,28},{18,... | collective-permute-start | bytes 294920 | tf_op jit(solution)/shard_map/ppermute | solution.py:232
  74.7 1.5 %collective-permute-done.27 = bf16[384,512]{1,0:T(8,128)(2,1)S(1)} collective-permute-done((bf16[384,512]{1,0:T(8,128)(2,1)S(1)}, bf16[384,512]{1,0:T(8,128)(2,1)S(1)}, u32[]{:S(2)}, u32[]{:S(2)}) %collective-permute-start.27) | collective-permute-done | bytes 393248 | tf_op jit(solution)/shard_map/ppermute | solution.py:232
  77.8 2.2 %collective-permute-start.29 = (bf16[96,512]{1,0:T(8,128)(2,1)S(1)}, bf16[96,512]{1,0:T(8,128)(2,1)S(1)}, u32[]{:S(2)}, u32[]{:S(2)}) collective-permute-start(bf16[96,512]{1,0:T(8,128)(2,1)S(1)} %get-tuple-element.45), channel_id=1, source_target_pairs={{0,12},{2,14},{4,8},{6,10},{8,4},{10,6},{12,0},{14,2},{16,28},{18,... | collective-permute-start | bytes 294920 | tf_op jit(solution)/shard_map/ppermute | solution.py:232
  80.0 1.6 %collective-permute-start.22 = (bf16[96,512]{1,0:T(8,128)(2,1)S(1)}, bf16[96,512]{1,0:T(8,128)(2,1)S(1)}, u32[]{:S(2)}, u32[]{:S(2)}) collective-permute-start(bf16[96,512]{1,0:T(8,128)(2,1)S(1)} %fusion.5.p_ref), channel_id=1, source_target_pairs={{0,16},{2,18},{4,20},{6,22},{8,24},{10,26},{12,28},{14,30},{16,0},... | collective-permute-start | bytes 294920 | tf_op jit(solution)/shard_map/ppermute | solution.py:232
  82.0 1.5 %collective-permute-done.29 = bf16[96,512]{1,0:T(8,128)(2,1)S(1)} collective-permute-done((bf16[96,512]{1,0:T(8,128)(2,1)S(1)}, bf16[96,512]{1,0:T(8,128)(2,1)S(1)}, u32[]{:S(2)}, u32[]{:S(2)}) %collective-permute-start.29) | collective-permute-done | bytes 98336 | tf_op jit(solution)/shard_map/ppermute | solution.py:232
  83.5 2.3 %collective-permute-start.31 = (bf16[96,512]{1,0:T(8,128)(2,1)S(1)}, bf16[96,512]{1,0:T(8,128)(2,1)S(1)}, u32[]{:S(2)}, u32[]{:S(2)}) collective-permute-start(bf16[96,512]{1,0:T(8,128)(2,1)S(1)} %fusion.2.p_ref), channel_id=1, source_target_pairs={{0,16},{2,18},{4,20},{6,22},{8,24},{10,26},{12,28},{14,30},{16,0},... | collective-permute-start | bytes 294920 | tf_op jit(solution)/shard_map/ppermute | solution.py:232
  87.6 1.8 %collective-permute-start.24 = (bf16[96,512]{1,0:T(8,128)(2,1)S(1)}, bf16[96,512]{1,0:T(8,128)(2,1)S(1)}, u32[]{:S(2)}, u32[]{:S(2)}) collective-permute-start(bf16[96,512]{1,0:T(8,128)(2,1)S(1)} %update.6.refs_0_), channel_id=1, source_target_pairs={{0,8},{2,10},{4,12},{6,14},{8,0},{10,2},{12,4},{14,6},{16,24},{18,... | collective-permute-start | bytes 294920 | tf_op jit(solution)/shard_map/ppermute | solution.py:232
  95.7 1.5 %collective-permute-done.34.refs_8_ = bf16[96,512]{1,0:T(8,128)(2,1)S(1)} collective-permute-done((bf16[96,512]{1,0:T(8,128)(2,1)S(1)}, bf16[96,512]{1,0:T(8,128)(2,1)S(1)}, u32[]{:S(2)}, u32[]{:S(2)}) %collective-permute-start.34) | collective-permute-done | bytes 98336 | tf_op jit(solution)/shard_map/ppermute | solution.py:232
  97.8 1.5 %collective-permute-done.32.refs_6_ = bf16[96,512]{1,0:T(8,128)(2,1)S(1)} collective-permute-done((bf16[96,512]{1,0:T(8,128)(2,1)S(1)}, bf16[96,512]{1,0:T(8,128)(2,1)S(1)}, u32[]{:S(2)}, u32[]{:S(2)}) %collective-permute-start.32) | collective-permute-done | bytes 98336 | tf_op jit(solution)/shard_map/ppermute | solution.py:232
  102.4 4.7 %collective-permute-done.35.refs_9_ = bf16[384,512]{1,0:T(8,128)(2,1)S(1)} collective-permute-done((bf16[384,512]{1,0:T(8,128)(2,1)S(1)}, bf16[384,512]{1,0:T(8,128)(2,1)S(1)}, u32[]{:S(2)}, u32[]{:S(2)}) %collective-permute-start.35) | collective-permute-done | bytes 393248 | tf_op jit(solution)/shard_map/ppermute | solution.py:232
  108.5 3.0 %project.2.refs_0_ = bf16[2,512,1024]{2,1,0:T(8,128)(2,1)} custom-call(bf16[512,512]{1,0:T(8,128)(2,1)S(1)} %apply.3.o_ref, bf16[512,512]{1,0:T(8,128)(2,1)S(1)} %collective-permute-done.38.other_ref, bf16[512,1024]{1,0:T(8,128)(2,1)S(1)} %get-tuple-element.34.proj_ref, bf16[512,1024]{1,0:T(8,128)(2,1)S(1)} %collective-permute-done.37.proj_other_ref), custom_call_target="tpu_custom_call" | custom-call | tf_op jit(solution)/shard_map/project/pallas_call | solution.py:201
  111.5 3.0 %project.3 = bf16[2,512,1024]{2,1,0:T(8,128)(2,1)} custom-call(bf16[512,512]{1,0:T(8,128)(2,1)S(1)} %apply.2.o_ref, bf16[512,512]{1,0:T(8,128)(2,1)S(1)} %collective-permute-done.36.other_ref, bf16[512,1024]{1,0:T(8,128)(2,1)S(1)} %get-tuple-element.34.proj_ref, ...), custom_call_target="tpu_custom_call", output_to_operand_aliasing={{}: (4, {})} | custom-call | tf_op jit(solution)/shard_map/project/pallas_call | solution.py:201
  (89 shorter events, 27.9 us)
Async XLA Ops:
  6.9 8.8 %collective-permute-start = (bf16[384,512]{1,0:T(8,128)(2,1)S(1)}, bf16[384,512]{1,0:T(8,128)(2,1)S(1)}, u32[]{:S(2)}, u32[]{:S(2)}) collective-permute-start(bf16[384,512]{1,0:T(8,128)(2,1)S(1)} %get-tuple-element.20), channel_id=1, source_target_pairs={{0,2},{2,0},{4,6},{6,4},{8,10},{10,8},{12,14},{14,12},{16,18},{18,... | collective-permute-start | bytes 1179656 | tf_op jit(solution)/shard_map/ppermute | solution.py:232
  9.9 11.4 %collective-permute-start.9 = (bf16[384,512]{1,0:T(8,128)(2,1)S(1)}, bf16[384,512]{1,0:T(8,128)(2,1)S(1)}, u32[]{:S(2)}, u32[]{:S(2)}) collective-permute-start(bf16[384,512]{1,0:T(8,128)(2,1)S(1)} %get-tuple-element.23), channel_id=1, source_target_pairs={{0,2},{2,0},{4,6},{6,4},{8,10},{10,8},{12,14},{14,12},{16,18},{18,... | collective-permute-start | bytes 1179656 | tf_op jit(solution)/shard_map/ppermute | solution.py:232
  15.8 10.1 %collective-permute-start.1 = (bf16[96,512]{1,0:T(8,128)(2,1)S(1)}, bf16[96,512]{1,0:T(8,128)(2,1)S(1)}, u32[]{:S(2)}, u32[]{:S(2)}) collective-permute-start(bf16[96,512]{1,0:T(8,128)(2,1)S(1)} %get-tuple-element.52), channel_id=1, source_target_pairs={{0,8},{2,10},{4,12},{6,14},{8,0},{10,2},{12,4},{14,6},{16,24},{18,... | collective-permute-start | bytes 294920 | tf_op jit(solution)/shard_map/ppermute | solution.py:232
  18.0 8.0 %collective-permute-start.3 = (bf16[96,512]{1,0:T(8,128)(2,1)S(1)}, bf16[96,512]{1,0:T(8,128)(2,1)S(1)}, u32[]{:S(2)}, u32[]{:S(2)}) collective-permute-start(bf16[96,512]{1,0:T(8,128)(2,1)S(1)} %get-tuple-element.53), channel_id=1, source_target_pairs={{0,4},{2,6},{4,0},{6,2},{8,12},{10,14},{12,8},{14,10},{16,20},{18,... | collective-permute-start | bytes 294920 | tf_op jit(solution)/shard_map/ppermute | solution.py:232
  19.5 6.5 %collective-permute-start.2 = (bf16[96,512]{1,0:T(8,128)(2,1)S(1)}, bf16[96,512]{1,0:T(8,128)(2,1)S(1)}, u32[]{:S(2)}, u32[]{:S(2)}) collective-permute-start(bf16[96,512]{1,0:T(8,128)(2,1)S(1)} %get-tuple-element.54), channel_id=1, source_target_pairs={{0,12},{2,14},{4,8},{6,10},{8,4},{10,6},{12,0},{14,2},{16,28},{18,... | collective-permute-start | bytes 294920 | tf_op jit(solution)/shard_map/ppermute | solution.py:232
  21.5 7.1 %collective-permute-start.10 = (bf16[96,512]{1,0:T(8,128)(2,1)S(1)}, bf16[96,512]{1,0:T(8,128)(2,1)S(1)}, u32[]{:S(2)}, u32[]{:S(2)}) collective-permute-start(bf16[96,512]{1,0:T(8,128)(2,1)S(1)} %get-tuple-element.49), channel_id=1, source_target_pairs={{0,8},{2,10},{4,12},{6,14},{8,0},{10,2},{12,4},{14,6},{16,24},{18,... | collective-permute-start | bytes 294920 | tf_op jit(solution)/shard_map/ppermute | solution.py:232
  25.9 6.0 %collective-permute-start.11 = (bf16[96,512]{1,0:T(8,128)(2,1)S(1)}, bf16[96,512]{1,0:T(8,128)(2,1)S(1)}, u32[]{:S(2)}, u32[]{:S(2)}) collective-permute-start(bf16[96,512]{1,0:T(8,128)(2,1)S(1)} %get-tuple-element.51), channel_id=1, source_target_pairs={{0,12},{2,14},{4,8},{6,10},{8,4},{10,6},{12,0},{14,2},{16,28},{18,... | collective-permute-start | bytes 294920 | tf_op jit(solution)/shard_map/ppermute | solution.py:232
  26.1 8.3 %collective-permute-start.4 = (bf16[96,512]{1,0:T(8,128)(2,1)S(1)}, bf16[96,512]{1,0:T(8,128)(2,1)S(1)}, u32[]{:S(2)}, u32[]{:S(2)}) collective-permute-start(bf16[96,512]{1,0:T(8,128)(2,1)S(1)} %fusion.11.p_ref), channel_id=1, source_target_pairs={{0,16},{2,18},{4,20},{6,22},{8,24},{10,26},{12,28},{14,30},{16,0},... | collective-permute-start | bytes 294920 | tf_op jit(solution)/shard_map/ppermute | solution.py:232
  31.9 6.4 %collective-permute-start.13 = (bf16[96,512]{1,0:T(8,128)(2,1)S(1)}, bf16[96,512]{1,0:T(8,128)(2,1)S(1)}, u32[]{:S(2)}, u32[]{:S(2)}) collective-permute-start(bf16[96,512]{1,0:T(8,128)(2,1)S(1)} %fusion.8.p_ref), channel_id=1, source_target_pairs={{0,16},{2,18},{4,20},{6,22},{8,24},{10,26},{12,28},{14,30},{16,0},... | collective-permute-start | bytes 294920 | tf_op jit(solution)/shard_map/ppermute | solution.py:232
  34.7 6.8 %collective-permute-start.7 = (bf16[96,512]{1,0:T(8,128)(2,1)S(1)}, bf16[96,512]{1,0:T(8,128)(2,1)S(1)}, u32[]{:S(2)}, u32[]{:S(2)}) collective-permute-start(bf16[96,512]{1,0:T(8,128)(2,1)S(1)} %get-tuple-element.21.refs_0_), channel_id=1, source_target_pairs={{0,12},{2,14},{4,8},{6,10},{8,4},{10,6},{12,0},{14,2},{16,28},{18,... | collective-permute-start | bytes 294920 | tf_op jit(solution)/shard_map/ppermute | solution.py:232
  35.8 6.4 %collective-permute-start.6 = (bf16[96,512]{1,0:T(8,128)(2,1)S(1)}, bf16[96,512]{1,0:T(8,128)(2,1)S(1)}, u32[]{:S(2)}, u32[]{:S(2)}) collective-permute-start(bf16[96,512]{1,0:T(8,128)(2,1)S(1)} %get-tuple-element.21.refs_0_), channel_id=1, source_target_pairs={{0,8},{2,10},{4,12},{6,14},{8,0},{10,2},{12,4},{14,6},{16,24},{18,... | collective-permute-start | bytes 294920 | tf_op jit(solution)/shard_map/ppermute | solution.py:232
  37.7 6.8 %collective-permute-start.5 = (bf16[96,512]{1,0:T(8,128)(2,1)S(1)}, bf16[96,512]{1,0:T(8,128)(2,1)S(1)}, u32[]{:S(2)}, u32[]{:S(2)}) collective-permute-start(bf16[96,512]{1,0:T(8,128)(2,1)S(1)} %get-tuple-element.21.refs_0_), channel_id=1, source_target_pairs={{0,4},{2,6},{4,0},{6,2},{8,12},{10,14},{12,8},{14,10},{16,20},{18,... | collective-permute-start | bytes 294920 | tf_op jit(solution)/shard_map/ppermute | solution.py:232
  38.6 6.0 %collective-permute-start.16 = (bf16[96,512]{1,0:T(8,128)(2,1)S(1)}, bf16[96,512]{1,0:T(8,128)(2,1)S(1)}, u32[]{:S(2)}, u32[]{:S(2)}) collective-permute-start(bf16[96,512]{1,0:T(8,128)(2,1)S(1)} %get-tuple-element.24.refs_5_), channel_id=1, source_target_pairs={{0,12},{2,14},{4,8},{6,10},{8,4},{10,6},{12,0},{14,2},{16,28},{18,... | collective-permute-start | bytes 294920 | tf_op jit(solution)/shard_map/ppermute | solution.py:232
  39.5 5.7 %collective-permute-start.15 = (bf16[96,512]{1,0:T(8,128)(2,1)S(1)}, bf16[96,512]{1,0:T(8,128)(2,1)S(1)}, u32[]{:S(2)}, u32[]{:S(2)}) collective-permute-start(bf16[96,512]{1,0:T(8,128)(2,1)S(1)} %get-tuple-element.24.refs_5_), channel_id=1, source_target_pairs={{0,8},{2,10},{4,12},{6,14},{8,0},{10,2},{12,4},{14,6},{16,24},{18,... | collective-permute-start | bytes 294920 | tf_op jit(solution)/shard_map/ppermute | solution.py:232
  41.5 5.7 %collective-permute-start.14 = (bf16[96,512]{1,0:T(8,128)(2,1)S(1)}, bf16[96,512]{1,0:T(8,128)(2,1)S(1)}, u32[]{:S(2)}, u32[]{:S(2)}) collective-permute-start(bf16[96,512]{1,0:T(8,128)(2,1)S(1)} %get-tuple-element.24.refs_5_), channel_id=1, source_target_pairs={{0,4},{2,6},{4,0},{6,2},{8,12},{10,14},{12,8},{14,10},{16,20},{18,... | collective-permute-start | bytes 294920 | tf_op jit(solution)/shard_map/ppermute | solution.py:232
  44.5 7.8 %collective-permute-start.8 = (bf16[384,512]{1,0:T(8,128)(2,1)S(1)}, bf16[384,512]{1,0:T(8,128)(2,1)S(1)}, u32[]{:S(2)}, u32[]{:S(2)}) collective-permute-start(bf16[384,512]{1,0:T(8,128)(2,1)S(1)} %pad_maximum_fusion), channel_id=1, source_target_pairs={{0,2},{2,0},{4,6},{6,4},{8,10},{10,8},{12,14},{14,12},{16,18},{18,... | collective-permute-start | bytes 1179656 | tf_op jit(solution)/shard_map/ppermute | solution.py:232
  47.3 9.3 %collective-permute-start.17 = (bf16[384,512]{1,0:T(8,128)(2,1)S(1)}, bf16[384,512]{1,0:T(8,128)(2,1)S(1)}, u32[]{:S(2)}, u32[]{:S(2)}) collective-permute-start(bf16[384,512]{1,0:T(8,128)(2,1)S(1)} %pad_maximum_fusion.1), channel_id=1, source_target_pairs={{0,2},{2,0},{4,6},{6,4},{8,10},{10,8},{12,14},{14,12},{16,18},{18,... | collective-permute-start | bytes 1179656 | tf_op jit(solution)/shard_map/ppermute | solution.py:232
  59.8 10.2 %collective-permute-start.18 = (bf16[384,512]{1,0:T(8,128)(2,1)}, bf16[384,512]{1,0:T(8,128)(2,1)}, u32[]{:S(2)}, u32[]{:S(2)}) collective-permute-start(bf16[384,512]{1,0:T(8,128)(2,1)} %get-tuple-element.26), channel_id=1, source_target_pairs={{0,2},{2,0},{4,6},{6,4},{8,10},{10,8},{12,14},{14,12},{16,18},{18,... | collective-permute-start | bytes 1179656 | tf_op jit(solution)/shard_map/ppermute | solution.py:232
  59.8 16.4 %collective-permute-start.27 = (bf16[384,512]{1,0:T(8,128)(2,1)S(1)}, bf16[384,512]{1,0:T(8,128)(2,1)S(1)}, u32[]{:S(2)}, u32[]{:S(2)}) collective-permute-start(bf16[384,512]{1,0:T(8,128)(2,1)S(1)} %get-tuple-element.30), channel_id=1, source_target_pairs={{0,2},{2,0},{4,6},{6,4},{8,10},{10,8},{12,14},{14,12},{16,18},{18,... | collective-permute-start | bytes 1179656 | tf_op jit(solution)/shard_map/ppermute | solution.py:232
  71.2 6.6 %collective-permute-start.19 = (bf16[96,512]{1,0:T(8,128)(2,1)S(1)}, bf16[96,512]{1,0:T(8,128)(2,1)S(1)}, u32[]{:S(2)}, u32[]{:S(2)}) collective-permute-start(bf16[96,512]{1,0:T(8,128)(2,1)S(1)} %get-tuple-element.46), channel_id=1, source_target_pairs={{0,8},{2,10},{4,12},{6,14},{8,0},{10,2},{12,4},{14,6},{16,24},{18,... | collective-permute-start | bytes 294920 | tf_op jit(solution)/shard_map/ppermute | solution.py:232
  71.3 8.7 %collective-permute-start.21 = (bf16[96,512]{1,0:T(8,128)(2,1)S(1)}, bf16[96,512]{1,0:T(8,128)(2,1)S(1)}, u32[]{:S(2)}, u32[]{:S(2)}) collective-permute-start(bf16[96,512]{1,0:T(8,128)(2,1)S(1)} %get-tuple-element.47), channel_id=1, source_target_pairs={{0,4},{2,6},{4,0},{6,2},{8,12},{10,14},{12,8},{14,10},{16,20},{18,... | collective-permute-start | bytes 294920 | tf_op jit(solution)/shard_map/ppermute | solution.py:232
  71.3 8.6 %collective-permute-start.20 = (bf16[96,512]{1,0:T(8,128)(2,1)S(1)}, bf16[96,512]{1,0:T(8,128)(2,1)S(1)}, u32[]{:S(2)}, u32[]{:S(2)}) collective-permute-start(bf16[96,512]{1,0:T(8,128)(2,1)S(1)} %get-tuple-element.48), channel_id=1, source_target_pairs={{0,12},{2,14},{4,8},{6,10},{8,4},{10,6},{12,0},{14,2},{16,28},{18,... | collective-permute-start | bytes 294920 | tf_op jit(solution)/shard_map/ppermute | solution.py:232
  77.8 5.7 %collective-permute-start.29 = (bf16[96,512]{1,0:T(8,128)(2,1)S(1)}, bf16[96,512]{1,0:T(8,128)(2,1)S(1)}, u32[]{:S(2)}, u32[]{:S(2)}) collective-permute-start(bf16[96,512]{1,0:T(8,128)(2,1)S(1)} %get-tuple-element.45), channel_id=1, source_target_pairs={{0,12},{2,14},{4,8},{6,10},{8,4},{10,6},{12,0},{14,2},{16,28},{18,... | collective-permute-start | bytes 294920 | tf_op jit(solution)/shard_map/ppermute | solution.py:232
  80.0 6.6 %collective-permute-start.22 = (bf16[96,512]{1,0:T(8,128)(2,1)S(1)}, bf16[96,512]{1,0:T(8,128)(2,1)S(1)}, u32[]{:S(2)}, u32[]{:S(2)}) collective-permute-start(bf16[96,512]{1,0:T(8,128)(2,1)S(1)} %fusion.5.p_ref), channel_id=1, source_target_pairs={{0,16},{2,18},{4,20},{6,22},{8,24},{10,26},{12,28},{14,30},{16,0},... | collective-permute-start | bytes 294920 | tf_op jit(solution)/shard_map/ppermute | solution.py:232
  83.5 7.3 %collective-permute-start.31 = (bf16[96,512]{1,0:T(8,128)(2,1)S(1)}, bf16[96,512]{1,0:T(8,128)(2,1)S(1)}, u32[]{:S(2)}, u32[]{:S(2)}) collective-permute-start(bf16[96,512]{1,0:T(8,128)(2,1)S(1)} %fusion.2.p_ref), channel_id=1, source_target_pairs={{0,16},{2,18},{4,20},{6,22},{8,24},{10,26},{12,28},{14,30},{16,0},... | collective-permute-start | bytes 294920 | tf_op jit(solution)/shard_map/ppermute | solution.py:232
  87.6 5.9 %collective-permute-start.24 = (bf16[96,512]{1,0:T(8,128)(2,1)S(1)}, bf16[96,512]{1,0:T(8,128)(2,1)S(1)}, u32[]{:S(2)}, u32[]{:S(2)}) collective-permute-start(bf16[96,512]{1,0:T(8,128)(2,1)S(1)} %update.6.refs_0_), channel_id=1, source_target_pairs={{0,8},{2,10},{4,12},{6,14},{8,0},{10,2},{12,4},{14,6},{16,24},{18,... | collective-permute-start | bytes 294920 | tf_op jit(solution)/shard_map/ppermute | solution.py:232
  90.7 17.8 %collective-permute-start.37 = (bf16[512,1024]{1,0:T(8,128)(2,1)S(1)}, bf16[512,1024]{1,0:T(8,128)(2,1)S(1)}, u32[]{:S(2)}, u32[]{:S(2)}) collective-permute-start(bf16[512,1024]{1,0:T(8,128)(2,1)S(1)} %get-tuple-element.33), channel_id=1, source_target_pairs={{0,1},{1,0},{2,3},{3,2},{4,5},{5,4},{6,7},{7,6},{8,9},{9,8},{10,11... | collective-permute-start | bytes 3145736 | tf_op jit(solution)/shard_map/ppermute | solution.py:235
  91.0 6.2 %collective-permute-start.34 = (bf16[96,512]{1,0:T(8,128)(2,1)S(1)}, bf16[96,512]{1,0:T(8,128)(2,1)S(1)}, u32[]{:S(2)}, u32[]{:S(2)}) collective-permute-start(bf16[96,512]{1,0:T(8,128)(2,1)S(1)} %update.7.refs_5_), channel_id=1, source_target_pairs={{0,12},{2,14},{4,8},{6,10},{8,4},{10,6},{12,0},{14,2},{16,28},{18,... | collective-permute-start | bytes 294920 | tf_op jit(solution)/shard_map/ppermute | solution.py:232
  93.5 5.8 %collective-permute-start.32 = (bf16[96,512]{1,0:T(8,128)(2,1)S(1)}, bf16[96,512]{1,0:T(8,128)(2,1)S(1)}, u32[]{:S(2)}, u32[]{:S(2)}) collective-permute-start(bf16[96,512]{1,0:T(8,128)(2,1)S(1)} %update.7.refs_5_), channel_id=1, source_target_pairs={{0,4},{2,6},{4,0},{6,2},{8,12},{10,14},{12,8},{14,10},{16,20},{18,... | collective-permute-start | bytes 294920 | tf_op jit(solution)/shard_map/ppermute | solution.py:232
  94.6 7.8 %collective-permute-start.26 = (bf16[384,512]{1,0:T(8,128)(2,1)S(1)}, bf16[384,512]{1,0:T(8,128)(2,1)S(1)}, u32[]{:S(2)}, u32[]{:S(2)}) collective-permute-start(bf16[384,512]{1,0:T(8,128)(2,1)S(1)} %pad_maximum_fusion.2), channel_id=1, source_target_pairs={{0,2},{2,0},{4,6},{6,4},{8,10},{10,8},{12,14},{14,12},{16,18},{18,... | collective-permute-start | bytes 1179656 | tf_op jit(solution)/shard_map/ppermute | solution.py:232
  99.3 7.8 %collective-permute-start.35 = (bf16[384,512]{1,0:T(8,128)(2,1)S(1)}, bf16[384,512]{1,0:T(8,128)(2,1)S(1)}, u32[]{:S(2)}, u32[]{:S(2)}) collective-permute-start(bf16[384,512]{1,0:T(8,128)(2,1)S(1)} %pad_maximum_fusion.3), channel_id=1, source_target_pairs={{0,2},{2,0},{4,6},{6,4},{8,10},{10,8},{12,14},{14,12},{16,18},{18,... | collective-permute-start | bytes 1179656 | tf_op jit(solution)/shard_map/ppermute | solution.py:232
  101.7 6.8 %collective-permute-start.38 = (bf16[512,512]{1,0:T(8,128)(2,1)S(1)}, bf16[512,512]{1,0:T(8,128)(2,1)S(1)}, u32[]{:S(2)}, u32[]{:S(2)}) collective-permute-start(bf16[512,512]{1,0:T(8,128)(2,1)S(1)} %apply.3.o_ref), channel_id=1, source_target_pairs={{0,1},{1,0},{2,3},{3,2},{4,5},{5,4},{6,7},{7,6},{8,9},{9,8},{10,11... | collective-permute-start | bytes 1572872 | tf_op jit(solution)/shard_map/ppermute | solution.py:235
  (15 other events, 103.8 us)

commit v3 on v2

v3 whole, which is shorter than its diff:
```python
import functools

import jax
import jax.numpy as jnp
from jax import lax
from jax.experimental import pallas as pl
from jax.experimental.pallas import tpu as pltpu
from jax.sharding import PartitionSpec as P

momentum_beta = 0.9
step_size = 0.03
f32 = jnp.float32
bf16 = jnp.bfloat16
VMEM = pl.BlockSpec(memory_space=pltpu.VMEM)
HBM = pl.BlockSpec(memory_space=pltpu.HBM)
SMEM = pl.BlockSpec(memory_space=pltpu.SMEM)


def params(mib=24):
    return pltpu.CompilerParams(vmem_limit_bytes=mib * 2**20)


def in_hbm(x):
    return pltpu.with_memory_space_constraint(x, pltpu.HBM)


def dot(x, y, contract=((1,), (0,))):
    return lax.dot_general(x, y, (contract, ((), ())), preferred_element_type=f32)


def sigmoid(x):
    return 0.5 * jnp.tanh(0.5 * x) + 0.5


def base_row(owner, width):
    return ((owner % 2) * (SHARDS // 2) + owner // 2) * (width // SHARDS)


def pieces_of(chunk, mine):
    found = [(i, 0, r) for i, r in enumerate((0, 2, 4, 6))]
    return found + [(4, i * mine, r) for i, r in enumerate((1, 3, 5, 7))]


def assemble(me, refs, full):
    width = full.shape[1]
    chunks = len(refs) // 5
    rows = width // SHARDS // chunks
    for h in range(chunks):
        for i, first, r in pieces_of(h, 3 * rows):
            ref = refs[5 * h + i]
            place = pl.ds(pl.multiple_of(base_row(me ^ r, width) + h * rows, rows), rows)
            for m in range(3):
                full[m, place, :] = ref[first + m * rows : first + (m + 1) * rows, :]


def token_grads(k, dy, w, da_s, db_s, hid_s, at):
    tok = k.shape[0]
    chunk = min(tok, 256)
    for t in range(0, tok, chunk):
        rows, span = slice(t, t + chunk), slice(at + t, at + t + chunk)
        a = dot(k[rows, :], w[0])
        b = dot(k[rows, :], w[1])
        sig = sigmoid(a)
        silu = a * sig
        hid_s[span, :] = (silu * b).astype(bf16)
        dh = dot(dy[rows, :], w[2], ((1,), (1,)))
        da_s[span, :] = (dh * b * sig * (1.0 + a * (1.0 - sig))).astype(bf16)
        db_s[span, :] = (dh * silu).astype(bf16)


def first_grads_kernel(me_ref, k_hbm, v_hbm, r_ref, w_hbm, *refs):
    out_refs, w0_refs = refs[: 2 * CHUNKS], refs[2 * CHUNKS : 3 * CHUNKS]
    k_s, v_s, w, da_s, db_s, hid_s, dy_s, g_s, sems = refs[3 * CHUNKS :]
    copies = [pltpu.make_async_copy(k_hbm.at[0], k_s, sems.at[0]), pltpu.make_async_copy(v_hbm.at[0], v_s, sems.at[1])]
    copies += [pltpu.make_async_copy(w_hbm.at[m], w.at[m], sems.at[2 + m]) for m in range(3)]
    for i in (1, 0, 2, 3, 4):
        copies[i].start()
    me = me_ref[0]
    tok, width = k_s.shape
    rate_col = jnp.broadcast_to(r_ref[...], (8, tok)).T[:, :1]
    copies[1].wait()
    dy_s[...] = (rate_col * v_s[...].astype(f32)).astype(bf16)
    for i in (0, 2, 3, 4):
        copies[i].wait()
    token_grads(k_s, dy_s, w, da_s, db_s, hid_s, 0)
    over_tokens = ((0,), (0,))
    g_s[0] = dot(k_s[...], da_s[...], over_tokens).astype(bf16)
    g_s[1] = dot(k_s[...], db_s[...], over_tokens).astype(bf16)
    g_s[2] = dot(hid_s[...], dy_s[...], over_tokens).astype(bf16)
    rows = width // SHARDS // CHUNKS
    for h in range(CHUNKS):
        for out, relative in ((out_refs[2 * h], (1, 3, 5, 7)), (out_refs[2 * h + 1], (0, 2, 4, 6))):
            for i, r in enumerate(relative):
                place = pl.ds(pl.multiple_of(base_row(me ^ r, width) + h * rows, rows), rows)
                for m in range(3):
                    row = (3 * i + m) * rows
                    out[row : row + rows, :] = g_s[m, place, :]
        place = pl.ds(pl.multiple_of(base_row(me, width) + h * rows, rows), rows)
        for m in range(3):
            w0_refs[h][m * rows : (m + 1) * rows, :] = w[m, place, :]


def first_grads(me, k, v, r, init):
    _, tok, width = k.shape
    rows = 3 * width // 2 // CHUNKS
    square = pltpu.VMEM((tok, width), bf16)
    weights = pltpu.VMEM((3, width, width), bf16)
    return pl.pallas_call(
        first_grads_kernel,
        grid=(1,),
        out_shape=[jax.ShapeDtypeStruct((rows, width), bf16)] * (2 * CHUNKS)
        + [jax.ShapeDtypeStruct((rows // 4, width), bf16)] * CHUNKS,
        in_specs=[SMEM, HBM, HBM, pl.BlockSpec((None, 1, tok), lambda i: (0, 0, 0)), HBM],
        out_specs=[VMEM] * (3 * CHUNKS),
        scratch_shapes=[square, square, weights, square, square, square, square, weights, pltpu.SemaphoreType.DMA((5,))],
        compiler_params=params(),
        name="first_grads",
    )(me, in_hbm(k), in_hbm(v), r, in_hbm(init))


def next_grads_kernel(n_w, me_ref, own_hbm, other_hbm, *refs):
    w_refs, out_refs, w_out = refs[:n_w], refs[n_w : n_w + 4 * CHUNKS], refs[n_w + 4 * CHUNKS]
    tok_s, da_s, db_s, hid_s, g_s, w, sems = refs[n_w + 4 * CHUNKS + 1 :]
    loads = [pltpu.make_async_copy(ref, tok_s.at[i], sems.at[i]) for i, ref in enumerate((own_hbm, other_hbm))]
    for load in loads:
        load.start()
    me = me_ref[0]
    assemble(me, w_refs, w)
    keep_w = pltpu.make_async_copy(w, w_out, sems.at[2])
    keep_w.start()
    tok, width = tok_s.shape[2:]
    half = width // 2
    for i, load in enumerate(loads):
        load.wait()
        token_grads(tok_s.at[i, 0], tok_s.at[i, 1], w, da_s, db_s, hid_s, i * tok)
    mine = pl.ds(pl.multiple_of((me % 2) * half, half), half)
    over_tokens = ((0,), (0,))
    spans = ((0, slice(0, tok)), (1, slice(tok, 2 * tok)))
    for m, d_s in ((0, da_s), (1, db_s)):
        g_s[m] = sum(dot(tok_s[i, 0, :, mine], d_s[span, :], over_tokens) for i, span in spans).astype(bf16)
    g_s[2] = sum(dot(hid_s[span, mine], tok_s[i, 1], over_tokens) for i, span in spans).astype(bf16)
    rows = width // SHARDS // CHUNKS
    for h in range(CHUNKS):
        for i, r in enumerate((0, 2, 4, 6)):
            place = pl.ds(pl.multiple_of((me ^ r) // 2 * (rows * CHUNKS) + h * rows, rows), rows)
            for m in range(3):
                out_refs[4 * h + i][m * rows : (m + 1) * rows, :] = g_s[m, place, :]
    keep_w.wait()


def next_grads(me, own, other, w):
    _, tok, width = own.shape
    rows = 3 * width // SHARDS // CHUNKS
    return pl.pallas_call(
        functools.partial(next_grads_kernel, len(w)),
        out_shape=[jax.ShapeDtypeStruct((rows, width), bf16)] * (4 * CHUNKS) + [pltpu.HBM((3, width, width), bf16)],
        in_specs=[SMEM, HBM, HBM] + [VMEM] * len(w),
        out_specs=[VMEM] * (4 * CHUNKS) + [HBM],
        scratch_shapes=[pltpu.VMEM((2, 2, tok, width), bf16)]
        + [pltpu.VMEM((2 * tok, width), bf16)] * 3
        + [pltpu.VMEM((3, width // 2, width), bf16), pltpu.VMEM((3, width, width), bf16), pltpu.SemaphoreType.DMA((3,))],
        compiler_params=params(),
        name="next_grads",
    )(me, in_hbm(own), in_hbm(other), *w)


def update_kernel(keep, p_ref, q_ref, w_ref, *refs):
    moment = p_ref[...].astype(f32) + q_ref[...].astype(f32)
    weights = w_ref[...].astype(f32)
    n_out = 3 if keep else 1
    if len(refs) > n_out:
        moment = momentum_beta * refs[0][...] + moment
    outs = refs[-n_out:]
    unit = moment * lax.rsqrt(jnp.mean(moment * moment, axis=-1, keepdims=True) + 1e-05)
    moved = weights + step_size * unit
    old_sq = jnp.mean(weights * weights, axis=-1, keepdims=True) + 1e-06
    new_sq = jnp.mean(moved * moved, axis=-1, keepdims=True) + 1e-06
    weights = moved * jnp.sqrt(old_sq / new_sq)
    outs[0][...] = weights.astype(bf16)
    if keep:
        outs[1][...] = weights
        outs[2][...] = moment


def update(p, q, state, keep):
    out = [jax.ShapeDtypeStruct(p.shape, bf16)] + [jax.ShapeDtypeStruct(p.shape, f32)] * (2 if keep else 0)
    got = pl.pallas_call(
        functools.partial(update_kernel, keep),
        out_shape=out,
        in_specs=[VMEM] * (2 + len(state)),
        out_specs=[VMEM] * len(out),
        compiler_params=params(),
        name="update",
    )(p, q, *state)
    return got[0], got[1:]


def apply_kernel(n_w, me_ref, q_ref, *refs):
    w_refs, out = refs[:n_w], refs[n_w]
    if n_w == 1:
        w = w_refs[0]
    else:
        w = refs[n_w + 1]
        assemble(me_ref[0], w_refs, w)
    tok = q_ref.shape[0]
    chunk = min(tok, 256)
    for t in range(0, tok, chunk):
        span = slice(t, t + chunk)
        q = q_ref[span, :]
        a = dot(q, w[0])
        b = dot(q, w[1])
        hid = (a * sigmoid(a) * b).astype(bf16)
        out[span, :] = dot(hid, w[2]).astype(bf16)


def fast_apply(me, q, block, w):
    _, tok, width = q.shape
    whole = pl.BlockSpec((3, width, width), lambda i: (0, 0, 0))
    return pl.pallas_call(
        functools.partial(apply_kernel, len(w)),
        grid=(1,),
        out_shape=jax.ShapeDtypeStruct((tok, width), bf16),
        in_specs=[SMEM, pl.BlockSpec((None, tok, width), lambda i: (block, 0, 0))] + ([whole] if len(w) == 1 else [VMEM] * len(w)),
        out_specs=VMEM,
        scratch_shapes=[pltpu.VMEM((3, width, width), bf16)] if len(w) > 1 else [],
        compiler_params=params(),
        name="apply",
    )(me, q, *w)


def project_own_kernel(o_ref, proj_ref, out):
    out[...] = dot(o_ref[...], proj_ref[...])


def project_own(o, proj):
    return pl.pallas_call(
        project_own_kernel,
        out_shape=jax.ShapeDtypeStruct((o.shape[0], proj.shape[1]), f32),
        in_specs=[VMEM] * 2,
        out_specs=VMEM,
        compiler_params=params(),
        name="project_own",
    )(o, proj)


def project_kernel(sum_ref, o_ref, proj_ref, *refs):
    refs[-1][...] = (sum_ref[...] + dot(o_ref[...], proj_ref[...])).astype(bf16)


def project(block, blocks, own, o_other, proj_other, into):
    tok, width = o_other.shape
    cols = proj_other.shape[1]
    args = [own, o_other, proj_other]
    specs = [pl.BlockSpec(x.shape, lambda i: (0, 0)) for x in args]
    aliases = {}
    if into is not None:
        args.append(into)
        specs.append(pl.BlockSpec(memory_space=pl.ANY))
        aliases = {3: 0}
    return pl.pallas_call(
        project_kernel,
        grid=(1,),
        out_shape=jax.ShapeDtypeStruct((blocks, tok, cols), bf16),
        in_specs=specs,
        out_specs=pl.BlockSpec((None, tok, cols), lambda i: (block, 0, 0)),
        input_output_aliases=aliases,
        compiler_params=params(),
        name="project",
    )(*args)


SHARDS = 8
CHUNKS = 2


def swap_low_bits(i):
    return (i & ~3) | ((i & 1) << 1) | ((i >> 1) & 1)


def together(*values):
    return lax.optimization_barrier(values)


def solution(mesh):
    ctx, heads = mesh.shape["ctx"], mesh.shape["head"]
    assert ctx & (ctx - 1) == 0 and ctx >= SHARDS and heads == 2

    def swap(x, bits):
        pairs = [(2 * i, 2 * (i ^ bits)) for i in range(ctx)]
        pairs += [(2 * i + 1, 2 * (i ^ swap_low_bits(bits)) + 1) for i in range(ctx)]
        return lax.ppermute(x, ("ctx", "head"), pairs)

    def swap_head(x):
        return lax.ppermute(x, "head", [(0, 1), (1, 0)])

    def add(x, y):
        return x.astype(f32) + y.astype(f32)

    def reduce_half(send, keep):
        total = add(keep, swap(send, 1))
        n = total.shape[0] // 4
        return [total[i * n : (i + 1) * n] for i in range(4)]

    def reduce_pieces(pieces):
        mine = pieces[0]
        for i, bits in ((2, 4), (3, 6), (1, 2)):
            mine = add(mine, swap(pieces[i].astype(bf16), bits))
        p = mine.astype(bf16)
        bit = SHARDS
        while bit < ctx // 2:
            p = add(p, swap(p, bit)).astype(bf16)
            bit *= 2
        return p

    def last_exchange(p):
        return swap(p, ctx // 2) if ctx > SHARDS else jnp.zeros_like(p)

    def gather_near(part):
        return [part] + [swap(part, bits) for bits in (2, 4, 6)]

    def on_device(queries, key_vectors, value_vectors, token_rates, fast_init, out_proj):
        blocks, tok, _, width = queries.shape
        flat = lambda x: x.reshape(blocks, tok, width)
        q, k, v = flat(queries), flat(key_vectors), flat(value_vectors)
        r = token_rates.reshape(blocks, 1, tok)
        init, proj_all = fast_init[0], out_proj[0]
        head = lax.axis_index("head")
        label = (lax.axis_index("ctx") % SHARDS).astype(jnp.int32)
        me = jnp.where(head == 0, label, swap_low_bits(label)).reshape(1)
        half = proj_all.shape[1] // heads
        proj = lax.dynamic_slice_in_dim(proj_all, head * half, half, 1)
        proj_other = swap_head(lax.dynamic_slice_in_dim(proj_all, (1 - head) * half, half, 1))

        def finish(c, me, w, into):
            o = fast_apply(me, q, c, w)
            return project(c, blocks, project_own(o, proj), swap_head(o), proj_other, into)

        result = None
        for c in range(blocks):
            if c == 0:
                grads = first_grads(me, k, v, r, init)
                state = [[w0] for w0 in grads[2 * CHUNKS :]]
                pieces = [reduce_half(*grads[2 * h : 2 * h + 2]) for h in range(CHUNKS)]
            else:
                grads = next_grads(me, tokens, tokens_other, w)
                pieces = [grads[4 * h : 4 * h + 4] for h in range(CHUNKS)]
            near = []
            for h in range(CHUNKS):
                p = reduce_pieces(pieces[h])
                if h == 0 and c + 1 < blocks:
                    dy = (r[c + 1, 0][:, None] * v[c + 1].astype(f32)).astype(bf16)
                    tokens = jnp.stack([k[c + 1], dy])
                    p, sent = together(p, tokens)
                    tokens_other = swap(sent, 1)
                wb, state[h] = update(p, last_exchange(p), state[h], c + 1 < blocks)
                near.append(gather_near(wb))
            joined = [jnp.concatenate(pieces) for pieces in near]
            if c > 0:
                joined[-1], me = together(joined[-1], me)
                result = finish(c - 1, me, grads[4 * CHUNKS :], result)
                me, result = together(me, result)
            w = [x for pieces, all_near in zip(near, joined) for x in (*pieces, swap(all_near, 1))]
        return finish(blocks - 1, me, w, result)

    placed = (
        P(None, "ctx", "head", None),
        P(None, "ctx", "head", None),
        P(None, "ctx", "head", None),
        P(None, "ctx", "head"),
        P("head", None, None, None),
        P("head", None, None),
    )
    return jax.shard_map(on_device, mesh=mesh, in_specs=placed, out_specs=P(None, "ctx", "head"), check_vma=False)
```

time: 115 us -> 103 us (0.90)
  waiting for transfers between devices: 46.3 us -> 31.9 us
  starting transfers between devices: 46.2 us -> 50.3 us
  local copies, waits for them, and re-layouts: 4.85 us -> 1 us
  Pallas kernels: 15 us -> 17.3 us
    ppermute x36 -> x35, waiting for transfers between devices: 46.3 us -> 30.7 us  [swap(): return lax.ppermute(x, ('ctx', 'head'), pairs)]
    ppermute x36 -> x35, starting transfers between devices: 46 us -> 50.1 us  [swap(): return lax.ppermute(x, ('ctx', 'head'), pairs)]
    unnamed x16 -> x14, local copies, waits for them, and re-layouts: 4.56 us -> 0.71 us
    pallas_call x8 -> x10, Pallas kernels: 12.5 us -> 14.9 us  [the longest x1 5.08 us: next_grads(): pl.pallas_call(functools.partial(next_grads_kernel, len(w)), out_shape=[j...]
    concatenate x4, other arithmetic: 0.11 us -> 1.62 us  [on_device(): joined = [jnp.concatenate(pieces) for pieces in near]]
    ppermute x3, waiting for transfers between devices: 0.01 us -> 1.19 us  [swap_head(): return lax.ppermute(x, 'head', [(0, 1), (1, 0)])]
  transfers between devices with their start and end apart: 39 -> 38, of which waited for: 22 -> 18; matrix products, arithmetic and copies ran while one was open for 2% -> 3% of each run, Pallas kernels for 6% -> 5%
where the time goes in v3:
time: 103 us
  starting transfers between devices  50.3 us (49%)
  waiting for transfers between devices  31.9 us (31%)
  Pallas kernels  17.3 us (17%)
  other arithmetic  2.33 us (2%)
    ppermute x35, starting transfers between devices, swap(): return lax.ppermute(x, ('ctx', 'head'), pairs)  50.1 us
    ppermute x35, waiting for transfers between devices, swap(): return lax.ppermute(x, ('ctx', 'head'), pairs)  30.7 us
    pallas_call x1, Pallas kernels, next_grads(): pl.pallas_call(functools.partial(next_grads_kernel, len(w)), out_shape=[j...  5.08 us
    pallas_call x1, Pallas kernels, first_grads(): pl.pallas_call(first_grads_kernel, grid=(1,), out_shape=[jax.ShapeDtypeSt...  4.09 us
    pallas_call x2, Pallas kernels, project(): pl.pallas_call(project_kernel, grid=(1,), out_shape=jax.ShapeDtypeStruct(...  3.37 us
    pallas_call x2, Pallas kernels, fast_apply(): pl.pallas_call(functools.partial(apply_kernel, len(w)), grid=(1,), out_sh...  2.4 us
  transfers between devices with their start and end apart: 38, of which 18 were waited for; matrix products, arithmetic and copies ran while one was open for 3% of the time, Pallas kernels for 5%

profile of v3, /device:TPU:0, one launch (start us, length us, event | category | flops | bytes accessed | tf_op | source)
XLA Modules:
  0.0 103.1 jit_solution(7809867413332435787)
XLA Ops:
  0.7 4.1 %first_grads.1 = (bf16[384,512]{1,0:T(8,128)(2,1)S(1)}, bf16[384,512]{1,0:T(8,128)(2,1)S(1)}, bf16[384,512]{1,0:T(8,128)(2,1)S(1)}, bf16[384,512]{1,0:T(8,128)(2...) custom-call(s32[1]{0:T(128)} %bitcast.me_ref, bf16[2,512,512]{2,1,0:T(8,128)(2,1)} %bitcast.19, ...), custom_call_target="tpu_custom_call" | custom-call | tf_op jit(solution)/shard_map/first_grads/pallas_call | solution.py:108
  4.8 3.0 %collective-permute-start = (bf16[384,512]{1,0:T(8,128)(2,1)S(1)}, bf16[384,512]{1,0:T(8,128)(2,1)S(1)}, u32[]{:S(2)}, u32[]{:S(2)}) collective-permute-start(bf16[384,512]{1,0:T(8,128)(2,1)S(1)} %get-tuple-element.33), channel_id=1, source_target_pairs={{0,2},{2,0},{4,6},{6,4},{8,10},{10,8},{12,14},{14,12},{16,18},{18,... | collective-permute-start | bytes 1179656 | tf_op jit(solution)/shard_map/ppermute | solution.py:291
  8.2 5.3 %collective-permute-done = bf16[384,512]{1,0:T(8,128)(2,1)S(1)} collective-permute-done((bf16[384,512]{1,0:T(8,128)(2,1)S(1)}, bf16[384,512]{1,0:T(8,128)(2,1)S(1)}, u32[]{:S(2)}, u32[]{:S(2)}) %collective-permute-start) | collective-permute-done | bytes 393248 | tf_op jit(solution)/shard_map/ppermute | solution.py:291
  13.7 2.2 %collective-permute-start.1 = (bf16[96,512]{1,0:T(8,128)(2,1)S(1)}, bf16[96,512]{1,0:T(8,128)(2,1)S(1)}, u32[]{:S(2)}, u32[]{:S(2)}) collective-permute-start(bf16[96,512]{1,0:T(8,128)(2,1)S(1)} %get-tuple-element.68), channel_id=1, source_target_pairs={{0,8},{2,10},{4,12},{6,14},{8,0},{10,2},{12,4},{14,6},{16,24},{18,... | collective-permute-start | bytes 294920 | tf_op jit(solution)/shard_map/ppermute | solution.py:291
  15.9 1.5 %collective-permute-start.3 = (bf16[96,512]{1,0:T(8,128)(2,1)S(1)}, bf16[96,512]{1,0:T(8,128)(2,1)S(1)}, u32[]{:S(2)}, u32[]{:S(2)}) collective-permute-start(bf16[96,512]{1,0:T(8,128)(2,1)S(1)} %get-tuple-element.69), channel_id=1, source_target_pairs={{0,4},{2,6},{4,0},{6,2},{8,12},{10,14},{12,8},{14,10},{16,20},{18,... | collective-permute-start | bytes 294920 | tf_op jit(solution)/shard_map/ppermute | solution.py:291
  17.4 2.0 %collective-permute-done.10 = bf16[384,512]{1,0:T(8,128)(2,1)S(1)} collective-permute-done((bf16[384,512]{1,0:T(8,128)(2,1)S(1)}, bf16[384,512]{1,0:T(8,128)(2,1)S(1)}, u32[]{:S(2)}, u32[]{:S(2)}) %collective-permute-start.10) | collective-permute-done | bytes 393248 | tf_op jit(solution)/shard_map/ppermute | solution.py:291
  19.5 2.8 %collective-permute-start.11 = (bf16[96,512]{1,0:T(8,128)(2,1)S(1)}, bf16[96,512]{1,0:T(8,128)(2,1)S(1)}, u32[]{:S(2)}, u32[]{:S(2)}) collective-permute-start(bf16[96,512]{1,0:T(8,128)(2,1)S(1)} %get-tuple-element.65), channel_id=1, source_target_pairs={{0,8},{2,10},{4,12},{6,14},{8,0},{10,2},{12,4},{14,6},{16,24},{18,... | collective-permute-start | bytes 294920 | tf_op jit(solution)/shard_map/ppermute | solution.py:291
  22.4 1.4 %collective-permute-start.13 = (bf16[96,512]{1,0:T(8,128)(2,1)S(1)}, bf16[96,512]{1,0:T(8,128)(2,1)S(1)}, u32[]{:S(2)}, u32[]{:S(2)}) collective-permute-start(bf16[96,512]{1,0:T(8,128)(2,1)S(1)} %get-tuple-element.66), channel_id=1, source_target_pairs={{0,4},{2,6},{4,0},{6,2},{8,12},{10,14},{12,8},{14,10},{16,20},{18,... | collective-permute-start | bytes 294920 | tf_op jit(solution)/shard_map/ppermute | solution.py:291
  24.0 1.7 %collective-permute-start.4 = (bf16[2,512,512]{2,1,0:T(8,128)(2,1)S(1)}, bf16[2,512,512]{2,1,0:T(8,128)(2,1)}, u32[]{:S(2)}, u32[]{:S(2)}) collective-permute-start(bf16[2,512,512]{2,1,0:T(8,128)(2,1)S(1)} %pad_maximum_fusion.own_hbm), channel_id=1, source_target_pairs={{0,2},{2,0},{4,6},{6,4},{8,10},{10,8},{12,14},{14,12},{16,18},{18,... | collective-permute-start | bytes 3145736 | tf_op jit(solution)/shard_map/ppermute | solution.py:291
  25.7 2.6 %collective-permute-start.5 = (bf16[96,512]{1,0:T(8,128)(2,1)S(1)}, bf16[96,512]{1,0:T(8,128)(2,1)S(1)}, u32[]{:S(2)}, u32[]{:S(2)}) collective-permute-start(bf16[96,512]{1,0:T(8,128)(2,1)S(1)} %fusion.6.p_ref), channel_id=1, source_target_pairs={{0,16},{2,18},{4,20},{6,22},{8,24},{10,26},{12,28},{14,30},{16,0},... | collective-permute-start | bytes 294920 | tf_op jit(solution)/shard_map/ppermute | solution.py:291
  28.3 1.4 %collective-permute-done.12 = bf16[96,512]{1,0:T(8,128)(2,1)S(1)} collective-permute-done((bf16[96,512]{1,0:T(8,128)(2,1)S(1)}, bf16[96,512]{1,0:T(8,128)(2,1)S(1)}, u32[]{:S(2)}, u32[]{:S(2)}) %collective-permute-start.12) | collective-permute-done | bytes 98336 | tf_op jit(solution)/shard_map/ppermute | solution.py:291
  29.8 2.4 %collective-permute-start.14 = (bf16[96,512]{1,0:T(8,128)(2,1)S(1)}, bf16[96,512]{1,0:T(8,128)(2,1)S(1)}, u32[]{:S(2)}, u32[]{:S(2)}) collective-permute-start(bf16[96,512]{1,0:T(8,128)(2,1)S(1)} %fusion.3.p_ref), channel_id=1, source_target_pairs={{0,16},{2,18},{4,20},{6,22},{8,24},{10,26},{12,28},{14,30},{16,0},... | collective-permute-start | bytes 294920 | tf_op jit(solution)/shard_map/ppermute | solution.py:291
  32.9 1.5 %collective-permute-start.8 = (bf16[96,512]{1,0:T(8,128)(2,1)S(1)}, bf16[96,512]{1,0:T(8,128)(2,1)S(1)}, u32[]{:S(2)}, u32[]{:S(2)}) collective-permute-start(bf16[96,512]{1,0:T(8,128)(2,1)S(1)} %get-tuple-element.37.refs_0_), channel_id=1, source_target_pairs={{0,12},{2,14},{4,8},{6,10},{8,4},{10,6},{12,0},{14,2},{16,28},{18,... | collective-permute-start | bytes 294920 | tf_op jit(solution)/shard_map/ppermute | solution.py:291
  36.7 1.5 %collective-permute-start.17 = (bf16[96,512]{1,0:T(8,128)(2,1)S(1)}, bf16[96,512]{1,0:T(8,128)(2,1)S(1)}, u32[]{:S(2)}, u32[]{:S(2)}) collective-permute-start(bf16[96,512]{1,0:T(8,128)(2,1)S(1)} %get-tuple-element.41.refs_5_), channel_id=1, source_target_pairs={{0,12},{2,14},{4,8},{6,10},{8,4},{10,6},{12,0},{14,2},{16,28},{18,... | collective-permute-start | bytes 294920 | tf_op jit(solution)/shard_map/ppermute | solution.py:291
  38.5 1.5 %collective-permute-start.16 = (bf16[96,512]{1,0:T(8,128)(2,1)S(1)}, bf16[96,512]{1,0:T(8,128)(2,1)S(1)}, u32[]{:S(2)}, u32[]{:S(2)}) collective-permute-start(bf16[96,512]{1,0:T(8,128)(2,1)S(1)} %get-tuple-element.41.refs_5_), channel_id=1, source_target_pairs={{0,8},{2,10},{4,12},{6,14},{8,0},{10,2},{12,4},{14,6},{16,24},{18,... | collective-permute-start | bytes 294920 | tf_op jit(solution)/shard_map/ppermute | solution.py:291
  43.1 2.6 %collective-permute-done.15.refs_6_ = bf16[96,512]{1,0:T(8,128)(2,1)S(1)} collective-permute-done((bf16[96,512]{1,0:T(8,128)(2,1)S(1)}, bf16[96,512]{1,0:T(8,128)(2,1)S(1)}, u32[]{:S(2)}, u32[]{:S(2)}) %collective-permute-start.15) | collective-permute-done | bytes 98336 | tf_op jit(solution)/shard_map/ppermute | solution.py:291
  47.5 2.2 %collective-permute-done.9.refs_4_ = bf16[384,512]{1,0:T(8,128)(2,1)S(1)} collective-permute-done((bf16[384,512]{1,0:T(8,128)(2,1)}, bf16[384,512]{1,0:T(8,128)(2,1)S(1)}, u32[]{:S(2)}, u32[]{:S(2)}) %collective-permute-start.9) | collective-permute-done | bytes 393248 | tf_op jit(solution)/shard_map/ppermute | solution.py:291
  49.7 4.8 %collective-permute-done.18.refs_9_ = bf16[384,512]{1,0:T(8,128)(2,1)S(1)} collective-permute-done((bf16[384,512]{1,0:T(8,128)(2,1)}, bf16[384,512]{1,0:T(8,128)(2,1)S(1)}, u32[]{:S(2)}, u32[]{:S(2)}) %collective-permute-start.18) | collective-permute-done | bytes 393248 | tf_op jit(solution)/shard_map/ppermute | solution.py:291
  54.5 5.1 %next_grads.1 = (bf16[96,512]{1,0:T(8,128)(2,1)S(1)}, bf16[96,512]{1,0:T(8,128)(2,1)S(1)}, bf16[96,512]{1,0:T(8,128)(2,1)S(1)}, bf16[96,512]{1,0:T(8,128)(2,1)S(...) custom-call(s32[1]{0:T(128)} %bitcast.me_ref, ...), custom_call_target="tpu_custom_call" | custom-call | tf_op jit(solution)/shard_map/next_grads/pallas_call | solution.py:154
  60.2 1.9 %collective-permute-start.20 = (bf16[96,512]{1,0:T(8,128)(2,1)S(1)}, bf16[96,512]{1,0:T(8,128)(2,1)S(1)}, u32[]{:S(2)}, u32[]{:S(2)}) collective-permute-start(bf16[96,512]{1,0:T(8,128)(2,1)S(1)} %get-tuple-element.44), channel_id=1, source_target_pairs={{0,12},{2,14},{4,8},{6,10},{8,4},{10,6},{12,0},{14,2},{16,28},{18,... | collective-permute-start | bytes 294920 | tf_op jit(solution)/shard_map/ppermute | solution.py:291
  64.3 1.7 %collective-permute-start.29 = (bf16[96,512]{1,0:T(8,128)(2,1)S(1)}, bf16[96,512]{1,0:T(8,128)(2,1)S(1)}, u32[]{:S(2)}, u32[]{:S(2)}) collective-permute-start(bf16[96,512]{1,0:T(8,128)(2,1)S(1)} %get-tuple-element.53), channel_id=1, source_target_pairs={{0,12},{2,14},{4,8},{6,10},{8,4},{10,6},{12,0},{14,2},{16,28},{18,... | collective-permute-start | bytes 294920 | tf_op jit(solution)/shard_map/ppermute | solution.py:291
  67.3 2.7 %collective-permute-start.22 = (bf16[96,512]{1,0:T(8,128)(2,1)S(1)}, bf16[96,512]{1,0:T(8,128)(2,1)S(1)}, u32[]{:S(2)}, u32[]{:S(2)}) collective-permute-start(bf16[96,512]{1,0:T(8,128)(2,1)S(1)} %add_convert_fusion.1.p_ref), channel_id=1, source_target_pairs={{0,16},{2,18},{4,20},{6,22},{8,24},{10,26},{12,28},{14,30},{16,0},... | collective-permute-start | bytes 294920 | tf_op jit(solution)/shard_map/ppermute | solution.py:291
  70.0 2.2 %collective-permute-done.29 = bf16[96,512]{1,0:T(8,128)(2,1)S(1)} collective-permute-done((bf16[96,512]{1,0:T(8,128)(2,1)S(1)}, bf16[96,512]{1,0:T(8,128)(2,1)S(1)}, u32[]{:S(2)}, u32[]{:S(2)}) %collective-permute-start.29) | collective-permute-done | bytes 98336 | tf_op jit(solution)/shard_map/ppermute | solution.py:291
  72.3 2.4 %collective-permute-start.31 = (bf16[96,512]{1,0:T(8,128)(2,1)S(1)}, bf16[96,512]{1,0:T(8,128)(2,1)S(1)}, u32[]{:S(2)}, u32[]{:S(2)}) collective-permute-start(bf16[96,512]{1,0:T(8,128)(2,1)S(1)} %add_convert_fusion.p_ref), channel_id=1, source_target_pairs={{0,16},{2,18},{4,20},{6,22},{8,24},{10,26},{12,28},{14,30},{16,0},... | collective-permute-start | bytes 294920 | tf_op jit(solution)/shard_map/ppermute | solution.py:291
  77.1 1.7 %collective-permute-start.23 = (bf16[96,512]{1,0:T(8,128)(2,1)S(1)}, bf16[96,512]{1,0:T(8,128)(2,1)S(1)}, u32[]{:S(2)}, u32[]{:S(2)}) collective-permute-start(bf16[96,512]{1,0:T(8,128)(2,1)S(1)} %update.6.refs_5_), channel_id=1, source_target_pairs={{0,4},{2,6},{4,0},{6,2},{8,12},{10,14},{12,8},{14,10},{16,20},{18,... | collective-permute-start | bytes 294920 | tf_op jit(solution)/shard_map/ppermute | solution.py:291
  80.4 1.7 %collective-permute-done.25.refs_8_ = bf16[96,512]{1,0:T(8,128)(2,1)S(1)} collective-permute-done((bf16[96,512]{1,0:T(8,128)(2,1)S(1)}, bf16[96,512]{1,0:T(8,128)(2,1)S(1)}, u32[]{:S(2)}, u32[]{:S(2)}) %collective-permute-start.25) | collective-permute-done | bytes 98336 | tf_op jit(solution)/shard_map/ppermute | solution.py:291
  82.6 1.5 %collective-permute-start.32 = (bf16[96,512]{1,0:T(8,128)(2,1)S(1)}, bf16[96,512]{1,0:T(8,128)(2,1)S(1)}, u32[]{:S(2)}, u32[]{:S(2)}) collective-permute-start(bf16[96,512]{1,0:T(8,128)(2,1)S(1)} %update.7.refs_0_), channel_id=1, source_target_pairs={{0,4},{2,6},{4,0},{6,2},{8,12},{10,14},{12,8},{14,10},{16,20},{18,... | collective-permute-start | bytes 294920 | tf_op jit(solution)/shard_map/ppermute | solution.py:291
  86.2 1.7 %collective-permute-start.36 = (bf16[384,512]{1,0:T(8,128)(2,1)S(1)}, bf16[384,512]{1,0:T(8,128)(2,1)S(1)}, u32[]{:S(2)}, u32[]{:S(2)}) collective-permute-start(bf16[384,512]{1,0:T(8,128)(2,1)S(1)} %pad_maximum_fusion.3), channel_id=1, source_target_pairs={{0,2},{2,0},{4,6},{6,4},{8,10},{10,8},{12,14},{14,12},{16,18},{18,... | collective-permute-start | bytes 1179656 | tf_op jit(solution)/shard_map/ppermute | solution.py:291
  88.0 2.3 %collective-permute-start.35 = (bf16[384,512]{1,0:T(8,128)(2,1)S(1)}, bf16[384,512]{1,0:T(8,128)(2,1)S(1)}, u32[]{:S(2)}, u32[]{:S(2)}) collective-permute-start(bf16[384,512]{1,0:T(8,128)(2,1)S(1)} %pad_maximum_fusion.4), channel_id=1, source_target_pairs={{0,2},{2,0},{4,6},{6,4},{8,10},{10,8},{12,14},{14,12},{16,18},{18,... | collective-permute-start | bytes 1179656 | tf_op jit(solution)/shard_map/ppermute | solution.py:291
  91.0 1.7 %project.2.refs_0_ = bf16[2,512,1024]{2,1,0:T(8,128)(2,1)} custom-call(f32[512,1024]{1,0:T(8,128)S(1)} %project_own.2.sum_ref, bf16[512,512]{1,0:T(8,128)(2,1)S(1)} %collective-permute-done.26.o_ref, bf16[512,1024]{1,0:T(8,128)(2,1)S(1)} %collective-permute-done.27.proj_ref), custom_call_target="tpu_custom_call" | custom-call | tf_op jit(solution)/shard_map/project/pallas_call | solution.py:260
  94.0 4.2 %collective-permute-done.35.refs_4_ = bf16[384,512]{1,0:T(8,128)(2,1)S(1)} collective-permute-done((bf16[384,512]{1,0:T(8,128)(2,1)S(1)}, bf16[384,512]{1,0:T(8,128)(2,1)S(1)}, u32[]{:S(2)}, u32[]{:S(2)}) %collective-permute-start.35) | collective-permute-done | bytes 393248 | tf_op jit(solution)/shard_map/ppermute | solution.py:291
  101.4 1.7 %project.3 = bf16[2,512,1024]{2,1,0:T(8,128)(2,1)} custom-call(f32[512,1024]{1,0:T(8,128)S(1)} %project_own.3.sum_ref, bf16[512,512]{1,0:T(8,128)(2,1)S(1)} %collective-permute-done.37.o_ref, bf16[512,1024]{1,0:T(8,128)(2,1)S(1)} %collective-permute-done.27.proj_ref, bf16[2,512,1024]{2,1,0:T(8,128)(2,1)} %project.2.refs_0_), custom_call_target="tpu_custom_call", output_to_operand_aliasing={{}: (3, {})} | custom-call | tf_op jit(solution)/shard_map/project/pallas_call | solution.py:260
  (87 shorter events, 25.7 us)
Async XLA Ops:
  4.8 8.8 %collective-permute-start = (bf16[384,512]{1,0:T(8,128)(2,1)S(1)}, bf16[384,512]{1,0:T(8,128)(2,1)S(1)}, u32[]{:S(2)}, u32[]{:S(2)}) collective-permute-start(bf16[384,512]{1,0:T(8,128)(2,1)S(1)} %get-tuple-element.33), channel_id=1, source_target_pairs={{0,2},{2,0},{4,6},{6,4},{8,10},{10,8},{12,14},{14,12},{16,18},{18,... | collective-permute-start | bytes 1179656 | tf_op jit(solution)/shard_map/ppermute | solution.py:291
  7.8 11.6 %collective-permute-start.10 = (bf16[384,512]{1,0:T(8,128)(2,1)S(1)}, bf16[384,512]{1,0:T(8,128)(2,1)S(1)}, u32[]{:S(2)}, u32[]{:S(2)}) collective-permute-start(bf16[384,512]{1,0:T(8,128)(2,1)S(1)} %get-tuple-element.39), channel_id=1, source_target_pairs={{0,2},{2,0},{4,6},{6,4},{8,10},{10,8},{12,14},{14,12},{16,18},{18,... | collective-permute-start | bytes 1179656 | tf_op jit(solution)/shard_map/ppermute | solution.py:291
  13.7 10.1 %collective-permute-start.1 = (bf16[96,512]{1,0:T(8,128)(2,1)S(1)}, bf16[96,512]{1,0:T(8,128)(2,1)S(1)}, u32[]{:S(2)}, u32[]{:S(2)}) collective-permute-start(bf16[96,512]{1,0:T(8,128)(2,1)S(1)} %get-tuple-element.68), channel_id=1, source_target_pairs={{0,8},{2,10},{4,12},{6,14},{8,0},{10,2},{12,4},{14,6},{16,24},{18,... | collective-permute-start | bytes 294920 | tf_op jit(solution)/shard_map/ppermute | solution.py:291
  15.9 8.0 %collective-permute-start.3 = (bf16[96,512]{1,0:T(8,128)(2,1)S(1)}, bf16[96,512]{1,0:T(8,128)(2,1)S(1)}, u32[]{:S(2)}, u32[]{:S(2)}) collective-permute-start(bf16[96,512]{1,0:T(8,128)(2,1)S(1)} %get-tuple-element.69), channel_id=1, source_target_pairs={{0,4},{2,6},{4,0},{6,2},{8,12},{10,14},{12,8},{14,10},{16,20},{18,... | collective-permute-start | bytes 294920 | tf_op jit(solution)/shard_map/ppermute | solution.py:291
  17.4 6.5 %collective-permute-start.2 = (bf16[96,512]{1,0:T(8,128)(2,1)S(1)}, bf16[96,512]{1,0:T(8,128)(2,1)S(1)}, u32[]{:S(2)}, u32[]{:S(2)}) collective-permute-start(bf16[96,512]{1,0:T(8,128)(2,1)S(1)} %get-tuple-element.70), channel_id=1, source_target_pairs={{0,12},{2,14},{4,8},{6,10},{8,4},{10,6},{12,0},{14,2},{16,28},{18,... | collective-permute-start | bytes 294920 | tf_op jit(solution)/shard_map/ppermute | solution.py:291
  19.5 8.8 %collective-permute-start.11 = (bf16[96,512]{1,0:T(8,128)(2,1)S(1)}, bf16[96,512]{1,0:T(8,128)(2,1)S(1)}, u32[]{:S(2)}, u32[]{:S(2)}) collective-permute-start(bf16[96,512]{1,0:T(8,128)(2,1)S(1)} %get-tuple-element.65), channel_id=1, source_target_pairs={{0,8},{2,10},{4,12},{6,14},{8,0},{10,2},{12,4},{14,6},{16,24},{18,... | collective-permute-start | bytes 294920 | tf_op jit(solution)/shard_map/ppermute | solution.py:291
  22.4 6.0 %collective-permute-start.13 = (bf16[96,512]{1,0:T(8,128)(2,1)S(1)}, bf16[96,512]{1,0:T(8,128)(2,1)S(1)}, u32[]{:S(2)}, u32[]{:S(2)}) collective-permute-start(bf16[96,512]{1,0:T(8,128)(2,1)S(1)} %get-tuple-element.66), channel_id=1, source_target_pairs={{0,4},{2,6},{4,0},{6,2},{8,12},{10,14},{12,8},{14,10},{16,20},{18,... | collective-permute-start | bytes 294920 | tf_op jit(solution)/shard_map/ppermute | solution.py:291
  23.8 6.0 %collective-permute-start.12 = (bf16[96,512]{1,0:T(8,128)(2,1)S(1)}, bf16[96,512]{1,0:T(8,128)(2,1)S(1)}, u32[]{:S(2)}, u32[]{:S(2)}) collective-permute-start(bf16[96,512]{1,0:T(8,128)(2,1)S(1)} %get-tuple-element.67), channel_id=1, source_target_pairs={{0,12},{2,14},{4,8},{6,10},{8,4},{10,6},{12,0},{14,2},{16,28},{18,... | collective-permute-start | bytes 294920 | tf_op jit(solution)/shard_map/ppermute | solution.py:291
  24.0 30.5 %collective-permute-start.4 = (bf16[2,512,512]{2,1,0:T(8,128)(2,1)S(1)}, bf16[2,512,512]{2,1,0:T(8,128)(2,1)}, u32[]{:S(2)}, u32[]{:S(2)}) collective-permute-start(bf16[2,512,512]{2,1,0:T(8,128)(2,1)S(1)} %pad_maximum_fusion.own_hbm), channel_id=1, source_target_pairs={{0,2},{2,0},{4,6},{6,4},{8,10},{10,8},{12,14},{14,12},{16,18},{18,... | collective-permute-start | bytes 3145736 | tf_op jit(solution)/shard_map/ppermute | solution.py:291
  25.7 6.9 %collective-permute-start.5 = (bf16[96,512]{1,0:T(8,128)(2,1)S(1)}, bf16[96,512]{1,0:T(8,128)(2,1)S(1)}, u32[]{:S(2)}, u32[]{:S(2)}) collective-permute-start(bf16[96,512]{1,0:T(8,128)(2,1)S(1)} %fusion.6.p_ref), channel_id=1, source_target_pairs={{0,16},{2,18},{4,20},{6,22},{8,24},{10,26},{12,28},{14,30},{16,0},... | collective-permute-start | bytes 294920 | tf_op jit(solution)/shard_map/ppermute | solution.py:291
  29.8 6.6 %collective-permute-start.14 = (bf16[96,512]{1,0:T(8,128)(2,1)S(1)}, bf16[96,512]{1,0:T(8,128)(2,1)S(1)}, u32[]{:S(2)}, u32[]{:S(2)}) collective-permute-start(bf16[96,512]{1,0:T(8,128)(2,1)S(1)} %fusion.3.p_ref), channel_id=1, source_target_pairs={{0,16},{2,18},{4,20},{6,22},{8,24},{10,26},{12,28},{14,30},{16,0},... | collective-permute-start | bytes 294920 | tf_op jit(solution)/shard_map/ppermute | solution.py:291
  32.9 5.6 %collective-permute-start.8 = (bf16[96,512]{1,0:T(8,128)(2,1)S(1)}, bf16[96,512]{1,0:T(8,128)(2,1)S(1)}, u32[]{:S(2)}, u32[]{:S(2)}) collective-permute-start(bf16[96,512]{1,0:T(8,128)(2,1)S(1)} %get-tuple-element.37.refs_0_), channel_id=1, source_target_pairs={{0,12},{2,14},{4,8},{6,10},{8,4},{10,6},{12,0},{14,2},{16,28},{18,... | collective-permute-start | bytes 294920 | tf_op jit(solution)/shard_map/ppermute | solution.py:291
  35.1 5.9 %collective-permute-start.6 = (bf16[96,512]{1,0:T(8,128)(2,1)S(1)}, bf16[96,512]{1,0:T(8,128)(2,1)S(1)}, u32[]{:S(2)}, u32[]{:S(2)}) collective-permute-start(bf16[96,512]{1,0:T(8,128)(2,1)S(1)} %get-tuple-element.37.refs_0_), channel_id=1, source_target_pairs={{0,4},{2,6},{4,0},{6,2},{8,12},{10,14},{12,8},{14,10},{16,20},{18,... | collective-permute-start | bytes 294920 | tf_op jit(solution)/shard_map/ppermute | solution.py:291
  36.7 6.1 %collective-permute-start.17 = (bf16[96,512]{1,0:T(8,128)(2,1)S(1)}, bf16[96,512]{1,0:T(8,128)(2,1)S(1)}, u32[]{:S(2)}, u32[]{:S(2)}) collective-permute-start(bf16[96,512]{1,0:T(8,128)(2,1)S(1)} %get-tuple-element.41.refs_5_), channel_id=1, source_target_pairs={{0,12},{2,14},{4,8},{6,10},{8,4},{10,6},{12,0},{14,2},{16,28},{18,... | collective-permute-start | bytes 294920 | tf_op jit(solution)/shard_map/ppermute | solution.py:291
  40.0 5.7 %collective-permute-start.15 = (bf16[96,512]{1,0:T(8,128)(2,1)S(1)}, bf16[96,512]{1,0:T(8,128)(2,1)S(1)}, u32[]{:S(2)}, u32[]{:S(2)}) collective-permute-start(bf16[96,512]{1,0:T(8,128)(2,1)S(1)} %get-tuple-element.41.refs_5_), channel_id=1, source_target_pairs={{0,4},{2,6},{4,0},{6,2},{8,12},{10,14},{12,8},{14,10},{16,20},{18,... | collective-permute-start | bytes 294920 | tf_op jit(solution)/shard_map/ppermute | solution.py:291
  41.7 8.0 %collective-permute-start.9 = (bf16[384,512]{1,0:T(8,128)(2,1)}, bf16[384,512]{1,0:T(8,128)(2,1)S(1)}, u32[]{:S(2)}, u32[]{:S(2)}) collective-permute-start(bf16[384,512]{1,0:T(8,128)(2,1)} %pad_maximum_fusion.1), channel_id=1, source_target_pairs={{0,2},{2,0},{4,6},{6,4},{8,10},{10,8},{12,14},{14,12},{16,18},{18,... | collective-permute-start | bytes 1179656 | tf_op jit(solution)/shard_map/ppermute | solution.py:291
  46.5 8.0 %collective-permute-start.18 = (bf16[384,512]{1,0:T(8,128)(2,1)}, bf16[384,512]{1,0:T(8,128)(2,1)S(1)}, u32[]{:S(2)}, u32[]{:S(2)}) collective-permute-start(bf16[384,512]{1,0:T(8,128)(2,1)} %pad_maximum_fusion.2), channel_id=1, source_target_pairs={{0,2},{2,0},{4,6},{6,4},{8,10},{10,8},{12,14},{14,12},{16,18},{18,... | collective-permute-start | bytes 1179656 | tf_op jit(solution)/shard_map/ppermute | solution.py:291
  60.2 5.7 %collective-permute-start.20 = (bf16[96,512]{1,0:T(8,128)(2,1)S(1)}, bf16[96,512]{1,0:T(8,128)(2,1)S(1)}, u32[]{:S(2)}, u32[]{:S(2)}) collective-permute-start(bf16[96,512]{1,0:T(8,128)(2,1)S(1)} %get-tuple-element.44), channel_id=1, source_target_pairs={{0,12},{2,14},{4,8},{6,10},{8,4},{10,6},{12,0},{14,2},{16,28},{18,... | collective-permute-start | bytes 294920 | tf_op jit(solution)/shard_map/ppermute | solution.py:291
  63.4 27.6 %collective-permute-start.27 = (bf16[512,1024]{1,0:T(8,128)(2,1)S(1)}, bf16[512,1024]{1,0:T(8,128)(2,1)S(1)}, u32[]{:S(2)}, u32[]{:S(2)}) collective-permute-start(bf16[512,1024]{1,0:T(8,128)(2,1)S(1)} %get-tuple-element.59), channel_id=1, source_target_pairs={{0,1},{1,0},{2,3},{3,2},{4,5},{5,4},{6,7},{7,6},{8,9},{9,8},{10,11... | collective-permute-start | bytes 3145736 | tf_op jit(solution)/shard_map/ppermute | solution.py:294
  63.5 6.5 %collective-permute-start.28 = (bf16[96,512]{1,0:T(8,128)(2,1)S(1)}, bf16[96,512]{1,0:T(8,128)(2,1)S(1)}, u32[]{:S(2)}, u32[]{:S(2)}) collective-permute-start(bf16[96,512]{1,0:T(8,128)(2,1)S(1)} %get-tuple-element.52), channel_id=1, source_target_pairs={{0,8},{2,10},{4,12},{6,14},{8,0},{10,2},{12,4},{14,6},{16,24},{18,... | collective-permute-start | bytes 294920 | tf_op jit(solution)/shard_map/ppermute | solution.py:291
  64.3 7.9 %collective-permute-start.29 = (bf16[96,512]{1,0:T(8,128)(2,1)S(1)}, bf16[96,512]{1,0:T(8,128)(2,1)S(1)}, u32[]{:S(2)}, u32[]{:S(2)}) collective-permute-start(bf16[96,512]{1,0:T(8,128)(2,1)S(1)} %get-tuple-element.53), channel_id=1, source_target_pairs={{0,12},{2,14},{4,8},{6,10},{8,4},{10,6},{12,0},{14,2},{16,28},{18,... | collective-permute-start | bytes 294920 | tf_op jit(solution)/shard_map/ppermute | solution.py:291
  65.9 6.3 %collective-permute-start.30 = (bf16[96,512]{1,0:T(8,128)(2,1)S(1)}, bf16[96,512]{1,0:T(8,128)(2,1)S(1)}, u32[]{:S(2)}, u32[]{:S(2)}) collective-permute-start(bf16[96,512]{1,0:T(8,128)(2,1)S(1)} %get-tuple-element.54), channel_id=1, source_target_pairs={{0,4},{2,6},{4,0},{6,2},{8,12},{10,14},{12,8},{14,10},{16,20},{18,... | collective-permute-start | bytes 294920 | tf_op jit(solution)/shard_map/ppermute | solution.py:291
  67.3 7.7 %collective-permute-start.22 = (bf16[96,512]{1,0:T(8,128)(2,1)S(1)}, bf16[96,512]{1,0:T(8,128)(2,1)S(1)}, u32[]{:S(2)}, u32[]{:S(2)}) collective-permute-start(bf16[96,512]{1,0:T(8,128)(2,1)S(1)} %add_convert_fusion.1.p_ref), channel_id=1, source_target_pairs={{0,16},{2,18},{4,20},{6,22},{8,24},{10,26},{12,28},{14,30},{16,0},... | collective-permute-start | bytes 294920 | tf_op jit(solution)/shard_map/ppermute | solution.py:291
  72.3 7.0 %collective-permute-start.31 = (bf16[96,512]{1,0:T(8,128)(2,1)S(1)}, bf16[96,512]{1,0:T(8,128)(2,1)S(1)}, u32[]{:S(2)}, u32[]{:S(2)}) collective-permute-start(bf16[96,512]{1,0:T(8,128)(2,1)S(1)} %add_convert_fusion.p_ref), channel_id=1, source_target_pairs={{0,16},{2,18},{4,20},{6,22},{8,24},{10,26},{12,28},{14,30},{16,0},... | collective-permute-start | bytes 294920 | tf_op jit(solution)/shard_map/ppermute | solution.py:291
  75.2 6.9 %collective-permute-start.25 = (bf16[96,512]{1,0:T(8,128)(2,1)S(1)}, bf16[96,512]{1,0:T(8,128)(2,1)S(1)}, u32[]{:S(2)}, u32[]{:S(2)}) collective-permute-start(bf16[96,512]{1,0:T(8,128)(2,1)S(1)} %update.6.refs_5_), channel_id=1, source_target_pairs={{0,12},{2,14},{4,8},{6,10},{8,4},{10,6},{12,0},{14,2},{16,28},{18,... | collective-permute-start | bytes 294920 | tf_op jit(solution)/shard_map/ppermute | solution.py:291
  76.6 6.0 %collective-permute-start.24 = (bf16[96,512]{1,0:T(8,128)(2,1)S(1)}, bf16[96,512]{1,0:T(8,128)(2,1)S(1)}, u32[]{:S(2)}, u32[]{:S(2)}) collective-permute-start(bf16[96,512]{1,0:T(8,128)(2,1)S(1)} %update.6.refs_5_), channel_id=1, source_target_pairs={{0,8},{2,10},{4,12},{6,14},{8,0},{10,2},{12,4},{14,6},{16,24},{18,... | collective-permute-start | bytes 294920 | tf_op jit(solution)/shard_map/ppermute | solution.py:291
  77.1 7.1 %collective-permute-start.23 = (bf16[96,512]{1,0:T(8,128)(2,1)S(1)}, bf16[96,512]{1,0:T(8,128)(2,1)S(1)}, u32[]{:S(2)}, u32[]{:S(2)}) collective-permute-start(bf16[96,512]{1,0:T(8,128)(2,1)S(1)} %update.6.refs_5_), channel_id=1, source_target_pairs={{0,4},{2,6},{4,0},{6,2},{8,12},{10,14},{12,8},{14,10},{16,20},{18,... | collective-permute-start | bytes 294920 | tf_op jit(solution)/shard_map/ppermute | solution.py:291
  79.5 6.7 %collective-permute-start.34 = (bf16[96,512]{1,0:T(8,128)(2,1)S(1)}, bf16[96,512]{1,0:T(8,128)(2,1)S(1)}, u32[]{:S(2)}, u32[]{:S(2)}) collective-permute-start(bf16[96,512]{1,0:T(8,128)(2,1)S(1)} %update.7.refs_0_), channel_id=1, source_target_pairs={{0,12},{2,14},{4,8},{6,10},{8,4},{10,6},{12,0},{14,2},{16,28},{18,... | collective-permute-start | bytes 294920 | tf_op jit(solution)/shard_map/ppermute | solution.py:291
  82.1 5.8 %collective-permute-start.33 = (bf16[96,512]{1,0:T(8,128)(2,1)S(1)}, bf16[96,512]{1,0:T(8,128)(2,1)S(1)}, u32[]{:S(2)}, u32[]{:S(2)}) collective-permute-start(bf16[96,512]{1,0:T(8,128)(2,1)S(1)} %update.7.refs_0_), channel_id=1, source_target_pairs={{0,8},{2,10},{4,12},{6,14},{8,0},{10,2},{12,4},{14,6},{16,24},{18,... | collective-permute-start | bytes 294920 | tf_op jit(solution)/shard_map/ppermute | solution.py:291
  85.3 5.7 %collective-permute-start.26 = (bf16[512,512]{1,0:T(8,128)(2,1)S(1)}, bf16[512,512]{1,0:T(8,128)(2,1)S(1)}, u32[]{:S(2)}, u32[]{:S(2)}) collective-permute-start(bf16[512,512]{1,0:T(8,128)(2,1)S(1)} %apply.2.o_ref), channel_id=1, source_target_pairs={{0,1},{1,0},{2,3},{3,2},{4,5},{5,4},{6,7},{7,6},{8,9},{9,8},{10,11... | collective-permute-start | bytes 1572872 | tf_op jit(solution)/shard_map/ppermute | solution.py:294
  86.2 7.8 %collective-permute-start.36 = (bf16[384,512]{1,0:T(8,128)(2,1)S(1)}, bf16[384,512]{1,0:T(8,128)(2,1)S(1)}, u32[]{:S(2)}, u32[]{:S(2)}) collective-permute-start(bf16[384,512]{1,0:T(8,128)(2,1)S(1)} %pad_maximum_fusion.3), channel_id=1, source_target_pairs={{0,2},{2,0},{4,6},{6,4},{8,10},{10,8},{12,14},{14,12},{16,18},{18,... | collective-permute-start | bytes 1179656 | tf_op jit(solution)/shard_map/ppermute | solution.py:291
  88.0 10.2 %collective-permute-start.35 = (bf16[384,512]{1,0:T(8,128)(2,1)S(1)}, bf16[384,512]{1,0:T(8,128)(2,1)S(1)}, u32[]{:S(2)}, u32[]{:S(2)}) collective-permute-start(bf16[384,512]{1,0:T(8,128)(2,1)S(1)} %pad_maximum_fusion.4), channel_id=1, source_target_pairs={{0,2},{2,0},{4,6},{6,4},{8,10},{10,8},{12,14},{14,12},{16,18},{18,... | collective-permute-start | bytes 1179656 | tf_op jit(solution)/shard_map/ppermute | solution.py:291
  (13 other events, 115.5 us)

commit v4 on v3

--- a/solution.py
+++ b/solution.py
@@ -53,18 +53,24 @@
                 full[m, place, :] = ref[first + m * rows : first + (m + 1) * rows, :]
 
 
-def token_grads(k, dy, w, da_s, db_s, hid_s, at):
+def token_grads(k, dy, w, da_s, db_s, hid_s, at, ready=lambda name: None):
     tok = k.shape[0]
-    chunk = min(tok, 256)
+    chunk = min(tok, 512)
     for t in range(0, tok, chunk):
         rows, span = slice(t, t + chunk), slice(at + t, at + t + chunk)
+        if t == 0:
+            ready("gate")
         a = dot(k[rows, :], w[0])
+        if t == 0:
+            ready("linear")
         b = dot(k[rows, :], w[1])
         sig = sigmoid(a)
         silu = a * sig
         hid_s[span, :] = (silu * b).astype(bf16)
+        if t == 0:
+            ready("output")
         dh = dot(dy[rows, :], w[2], ((1,), (1,)))
-        da_s[span, :] = (dh * b * sig * (1.0 + a * (1.0 - sig))).astype(bf16)
+        da_s[span, :] = (dh * (b * (sig + silu * (1.0 - sig)))).astype(bf16)
         db_s[span, :] = (dh * silu).astype(bf16)
 
 
@@ -73,16 +79,19 @@
     k_s, v_s, w, da_s, db_s, hid_s, dy_s, g_s, sems = refs[3 * CHUNKS :]
     copies = [pltpu.make_async_copy(k_hbm.at[0], k_s, sems.at[0]), pltpu.make_async_copy(v_hbm.at[0], v_s, sems.at[1])]
     copies += [pltpu.make_async_copy(w_hbm.at[m], w.at[m], sems.at[2 + m]) for m in range(3)]
-    for i in (1, 0, 2, 3, 4):
+    for i in (0, 2, 3, 1, 4):
         copies[i].start()
     me = me_ref[0]
     tok, width = k_s.shape
     rate_col = jnp.broadcast_to(r_ref[...], (8, tok)).T[:, :1]
-    copies[1].wait()
-    dy_s[...] = (rate_col * v_s[...].astype(f32)).astype(bf16)
-    for i in (0, 2, 3, 4):
-        copies[i].wait()
-    token_grads(k_s, dy_s, w, da_s, db_s, hid_s, 0)
+
+    def ready(name):
+        for i in {"gate": (0, 2), "linear": (3,), "output": (1, 4)}[name]:
+            copies[i].wait()
+        if name == "output":
+            dy_s[...] = (rate_col * v_s[...].astype(f32)).astype(bf16)
+
+    token_grads(k_s, dy_s, w, da_s, db_s, hid_s, 0, ready)
     over_tokens = ((0,), (0,))
     g_s[0] = dot(k_s[...], da_s[...], over_tokens).astype(bf16)
     g_s[1] = dot(k_s[...], db_s[...], over_tokens).astype(bf16)
@@ -115,24 +124,32 @@
         scratch_shapes=[square, square, weights, square, square, square, square, weights, pltpu.SemaphoreType.DMA((5,))],
         compiler_params=params(),
         name="first_grads",
-    )(me, in_hbm(k), in_hbm(v), r, in_hbm(init))
+    )(me, in_hbm(k), in_hbm(v), in_hbm(r), in_hbm(init))
 
 
 def next_grads_kernel(n_w, me_ref, own_hbm, other_hbm, *refs):
     w_refs, out_refs, w_out = refs[:n_w], refs[n_w : n_w + 4 * CHUNKS], refs[n_w + 4 * CHUNKS]
     tok_s, da_s, db_s, hid_s, g_s, w, sems = refs[n_w + 4 * CHUNKS + 1 :]
-    loads = [pltpu.make_async_copy(ref, tok_s.at[i], sems.at[i]) for i, ref in enumerate((own_hbm, other_hbm))]
-    for load in loads:
-        load.start()
+    loads = [
+        [pltpu.make_async_copy(ref.at[j], tok_s.at[i, j], sems.at[2 * i + j]) for j in range(2)]
+        for i, ref in enumerate((own_hbm, other_hbm))
+    ]
+    for pair in loads:
+        for load in pair:
+            load.start()
     me = me_ref[0]
     assemble(me, w_refs, w)
-    keep_w = pltpu.make_async_copy(w, w_out, sems.at[2])
-    keep_w.start()
+    keep_w = pltpu.make_async_copy(w, w_out, sems.at[4])
     tok, width = tok_s.shape[2:]
     half = width // 2
-    for i, load in enumerate(loads):
-        load.wait()
-        token_grads(tok_s.at[i, 0], tok_s.at[i, 1], w, da_s, db_s, hid_s, i * tok)
+    for i, pair in enumerate(loads):
+
+        def ready(name, pair=pair):
+            if name != "linear":
+                pair[name == "output"].wait()
+
+        token_grads(tok_s.at[i, 0], tok_s.at[i, 1], w, da_s, db_s, hid_s, i * tok, ready)
+    keep_w.start()
     mine = pl.ds(pl.multiple_of((me % 2) * half, half), half)
     over_tokens = ((0,), (0,))
     spans = ((0, slice(0, tok)), (1, slice(tok, 2 * tok)))
@@ -158,10 +175,28 @@
         out_specs=[VMEM] * (4 * CHUNKS) + [HBM],
         scratch_shapes=[pltpu.VMEM((2, 2, tok, width), bf16)]
         + [pltpu.VMEM((2 * tok, width), bf16)] * 3
-        + [pltpu.VMEM((3, width // 2, width), bf16), pltpu.VMEM((3, width, width), bf16), pltpu.SemaphoreType.DMA((3,))],
+        + [pltpu.VMEM((3, width // 2, width), bf16), pltpu.VMEM((3, width, width), bf16), pltpu.SemaphoreType.DMA((5,))],
         compiler_params=params(),
         name="next_grads",
     )(me, in_hbm(own), in_hbm(other), *w)
+
+
+def join_kernel(*refs):
+    rows = refs[0].shape[0]
+    for i, ref in enumerate(refs[:-1]):
+        refs[-1][i * rows : (i + 1) * rows, :] = ref[...]
+
+
+def join(pieces):
+    rows, width = pieces[0].shape
+    return pl.pallas_call(
+        join_kernel,
+        out_shape=jax.ShapeDtypeStruct((len(pieces) * rows, width), bf16),
+        in_specs=[VMEM] * len(pieces),
+        out_specs=VMEM,
+        compiler_params=params(),
+        name="join",
+    )(*pieces)
 
 
 def update_kernel(keep, p_ref, q_ref, w_ref, *refs):
@@ -203,7 +238,7 @@
         w = refs[n_w + 1]
         assemble(me_ref[0], w_refs, w)
     tok = q_ref.shape[0]
-    chunk = min(tok, 256)
+    chunk = min(tok, 512)
     for t in range(0, tok, chunk):
         span = slice(t, t + chunk)
         q = q_ref[span, :]
@@ -271,6 +306,8 @@
 
 SHARDS = 8
 CHUNKS = 2
+O = {'join': (0, 0), 't01': 0, 'flows': (0, 1, 2), 'aflows': (0, 1, 2), 'p0_after_t1': 0, 'p01': (0, 0), 'u01': (0, 0), 'tokdone': '', 'tok': 'p0', 'j01': (0, 0), 'app': 'wb', 'res': 'me', 's2': ((0, 0), (0, 0)), 'A': ((0, 0), (0, 0)), 'jf': (0, 0)}
+FLOWS = ((1, 2), (2, 4), (3, 6))
 
 
 def swap_low_bits(i):
@@ -279,6 +316,10 @@
 
 def together(*values):
     return lax.optimization_barrier(values)
+
+
+def after(x, *others):
+    return together(x, *others)[0]
 
 
 def solution(mesh):
@@ -296,16 +337,13 @@
     def add(x, y):
         return x.astype(f32) + y.astype(f32)
 
-    def reduce_half(send, keep):
-        total = add(keep, swap(send, 1))
+    def reduce_half(received, keep):
+        total = add(keep, received)
         n = total.shape[0] // 4
         return [total[i * n : (i + 1) * n] for i in range(4)]
 
-    def reduce_pieces(pieces):
-        mine = pieces[0]
-        for i, bits in ((2, 4), (3, 6), (1, 2)):
-            mine = add(mine, swap(pieces[i].astype(bf16), bits))
-        p = mine.astype(bf16)
+    def reduce_pieces(pieces, received):
+        p = sum((x.astype(f32) for x in received), pieces[0].astype(f32)).astype(bf16)
         bit = SHARDS
         while bit < ctx // 2:
             p = add(p, swap(p, bit)).astype(bf16)
@@ -314,9 +352,6 @@
 
     def last_exchange(p):
         return swap(p, ctx // 2) if ctx > SHARDS else jnp.zeros_like(p)
-
-    def gather_near(part):
-        return [part] + [swap(part, bits) for bits in (2, 4, 6)]
 
     def on_device(queries, key_vectors, value_vectors, token_rates, fast_init, out_proj):
         blocks, tok, _, width = queries.shape
@@ -329,6 +364,10 @@
         me = jnp.where(head == 0, label, swap_low_bits(label)).reshape(1)
         half = proj_all.shape[1] // heads
         proj = lax.dynamic_slice_in_dim(proj_all, head * half, half, 1)
+        tokens = None
+        if blocks > 1:
+            dy = (r[1, 0][:, None] * v[1].astype(f32)).astype(bf16)
+            tokens = jnp.stack([k[1], dy])
         proj_other = swap_head(lax.dynamic_slice_in_dim(proj_all, (1 - head) * half, half, 1))
 
         def finish(c, me, w, into):
@@ -337,29 +376,72 @@
 
         result = None
         for c in range(blocks):
+            last = c + 1 == blocks
+            jn = join if O["join"][c] else jnp.concatenate
             if c == 0:
                 grads = first_grads(me, k, v, r, init)
                 state = [[w0] for w0 in grads[2 * CHUNKS :]]
-                pieces = [reduce_half(*grads[2 * h : 2 * h + 2]) for h in range(CHUNKS)]
+                received = [swap(grads[2 * h], 1) for h in range(CHUNKS)]
+                pieces = []
+                for h in range(CHUNKS):
+                    got = after(received[h], pieces[-1][0]) if h and O["t01"] else received[h]
+                    pieces.append(reduce_half(got, grads[2 * h + 1]))
             else:
                 grads = next_grads(me, tokens, tokens_other, w)
                 pieces = [grads[4 * h : 4 * h + 4] for h in range(CHUNKS)]
-            near = []
+            flows = [FLOWS[i] for i in O["flows"]]
+            received = []
             for h in range(CHUNKS):
-                p = reduce_pieces(pieces[h])
-                if h == 0 and c + 1 < blocks:
-                    dy = (r[c + 1, 0][:, None] * v[c + 1].astype(f32)).astype(bf16)
-                    tokens = jnp.stack([k[c + 1], dy])
-                    p, sent = together(p, tokens)
-                    tokens_other = swap(sent, 1)
-                wb, state[h] = update(p, last_exchange(p), state[h], c + 1 < blocks)
-                near.append(gather_near(wb))
-            joined = [jnp.concatenate(pieces) for pieces in near]
+                ps = pieces[h]
+                if O["s2"][c][h]:
+                    got = swap(jnp.concatenate([ps[1].astype(bf16), ps[3].astype(bf16)]), 2)
+                    n = got.shape[0] // 2
+                    mine, send = add(ps[0], got[:n]), add(ps[2], got[n:]).astype(bf16)
+                    pieces[h] = [mine]
+                    received.append([swap(send, 4)])
+                else:
+                    received.append([swap(ps[i].astype(bf16), bits) for i, bits in flows])
+            sums, near = [], []
+            if c == 0 and O["p0_after_t1"]:
+                received[0][0] = after(received[0][0], pieces[1][0])
+            for h in range(CHUNKS):
+                if h and O["p01"][c]:
+                    received[h][0] = after(received[h][0], sums[-1])
+                sums.append(reduce_pieces(pieces[h], received[h]))
+            others = [last_exchange(p) for p in sums]
+            for h in range(CHUNKS):
+                if h:
+                    extra = []
+                    if O["u01"][c]: extra.append(near[-1][0])
+                    if not last and O["tokdone"] == "q1": extra.append(tokens_other)
+                    if extra: others[h] = after(others[h], *extra)
+                wb, state[h] = update(sums[h], others[h], state[h], not last)
+                if O["A"][c][h]:
+                    z = swap(wb, 4)
+                    g = swap(jnp.concatenate([wb, z]), 2)
+                    n = wb.shape[0]
+                    near.append([wb, g[:n], z, g[n:]])
+                else:
+                    got = {FLOWS[i][1]: swap(wb, FLOWS[i][1]) for i in O["aflows"]}
+                    near.append([wb] + [got[bits] for bits in (2, 4, 6)])
+                if not last and h == 0:
+                    dep = {"grads": grads[0], "p0": sums[0], "t1": pieces[1][0], "t0": pieces[0][0], "p1": sums[1], "wb0": wb, "keep": grads[1]}[O["tok"]]
+                    tokens_other = swap(after(tokens, dep), 1)
+            joined, far = [], []
+            for h in range(CHUNKS):
+                ps = list(near[h])
+                if h and O["j01"][c]: ps[0] = after(ps[0], joined[-1])
+                if h and not last and O["tokdone"] == "j1": ps[0] = after(ps[0], tokens_other)
+                if h and O["jf"][c]: ps[0] = after(ps[0], far[0])
+                joined.append(jn(ps))
+                far.append(swap(joined[-1], 1))
             if c > 0:
-                joined[-1], me = together(joined[-1], me)
-                result = finish(c - 1, me, grads[4 * CHUNKS :], result)
-                me, result = together(me, result)
-            w = [x for pieces, all_near in zip(near, joined) for x in (*pieces, swap(all_near, 1))]
+                deps = {"w1": [near[1][0]], "w0": [near[0][0]], "z": near[0][1:] + near[1][1:], "z1": near[1][1:], "z0": near[0][1:], "j": joined, "f0": far[:1], "f1": far[1:], "n": [], "wb": [near[1][0], near[0][0]], "p": sums}[O["app"]]
+                me_late = after(me, *deps) if deps else me
+                result = finish(c - 1, me_late, grads[4 * CHUNKS :], result)
+                if O["res"] == "me":
+                    me, result = together(me, result)
+            w = [x for h in range(CHUNKS) for x in (*near[h], far[h])]
         return finish(blocks - 1, me, w, result)
 
     placed = (

time: 103 us -> 102 us (level)
  starting transfers between devices: 50.3 us -> 49.1 us
    ppermute x35, starting transfers between devices: 50.1 us -> 48.8 us  [swap(): return lax.ppermute(x, ('ctx', 'head'), pairs)]
  transfers between devices with their start and end apart: 38 -> 38, of which waited for: 18 -> 15; matrix products, arithmetic and copies ran while one was open for 3% -> 3% of each run, Pallas kernels for 5% -> 5%
where the time goes in v4:
time: 102 us; the launch traced here: 101 us
  starting transfers between devices  49.1 us (48%)
  waiting for transfers between devices  32.4 us (32%)
  Pallas kernels  17 us (17%)
  other arithmetic  2.33 us (2%)
    ppermute x35, starting transfers between devices, swap(): return lax.ppermute(x, ('ctx', 'head'), pairs)  48.8 us
    ppermute x35, waiting for transfers between devices, swap(): return lax.ppermute(x, ('ctx', 'head'), pairs)  31.3 us
    pallas_call x1, Pallas kernels, next_grads(): pl.pallas_call(functools.partial(next_grads_kernel, len(w)), out_shape=[j...  4.66 us
    pallas_call x1, Pallas kernels, first_grads(): pl.pallas_call(first_grads_kernel, grid=(1,), out_shape=[jax.ShapeDtypeSt...  4.58 us
    pallas_call x2, Pallas kernels, project(): pl.pallas_call(project_kernel, grid=(1,), out_shape=jax.ShapeDtypeStruct(...  3.38 us
    pallas_call x2, Pallas kernels, fast_apply(): pl.pallas_call(functools.partial(apply_kernel, len(w)), grid=(1,), out_sh...  2.09 us
  transfers between devices with their start and end apart: 38, of which 15 were waited for; matrix products, arithmetic and copies ran while one was open for 3% of the time, Pallas kernels for 5%

profile of v4, /device:TPU:0, one launch (start us, length us, event | category | flops | bytes accessed | tf_op | source)
XLA Modules:
  0.0 101.4 jit_solution(7289831297393266467)
XLA Ops:
  0.0 4.6 %first_grads.1 = (bf16[384,512]{1,0:T(8,128)(2,1)S(1)}, bf16[384,512]{1,0:T(8,128)(2,1)S(1)}, bf16[384,512]{1,0:T(8,128)(2,1)S(1)}, bf16[384,512]{1,0:T(8,128)(2...) custom-call(s32[1]{0:T(128)} %bitcast.me_ref, bf16[2,512,512]{2,1,0:T(8,128)(2,1)} %bitcast.18, ...), custom_call_target="tpu_custom_call" | custom-call | tf_op jit(solution)/shard_map/first_grads/pallas_call | solution.py:117
  4.6 3.0 %collective-permute-start = (bf16[384,512]{1,0:T(8,128)(2,1)S(1)}, bf16[384,512]{1,0:T(8,128)(2,1)S(1)}, u32[]{:S(2)}, u32[]{:S(2)}) collective-permute-start(bf16[384,512]{1,0:T(8,128)(2,1)S(1)} %get-tuple-element.31), channel_id=1, source_target_pairs={{0,2},{2,0},{4,6},{6,4},{8,10},{10,8},{12,14},{14,12},{16,18},{18,... | collective-permute-start | bytes 1179656 | tf_op jit(solution)/shard_map/ppermute | solution.py:332
  8.0 5.3 %collective-permute-done = bf16[384,512]{1,0:T(8,128)(2,1)S(1)} collective-permute-done((bf16[384,512]{1,0:T(8,128)(2,1)S(1)}, bf16[384,512]{1,0:T(8,128)(2,1)S(1)}, u32[]{:S(2)}, u32[]{:S(2)}) %collective-permute-start) | collective-permute-done | bytes 393248 | tf_op jit(solution)/shard_map/ppermute | solution.py:332
  13.5 3.1 %collective-permute-start.3 = (bf16[96,512]{1,0:T(8,128)(2,1)S(1)}, bf16[96,512]{1,0:T(8,128)(2,1)S(1)}, u32[]{:S(2)}, u32[]{:S(2)}) collective-permute-start(bf16[96,512]{1,0:T(8,128)(2,1)S(1)} %get-tuple-element.65), channel_id=1, source_target_pairs={{0,12},{2,14},{4,8},{6,10},{8,4},{10,6},{12,0},{14,2},{16,28},{18,... | collective-permute-start | bytes 294920 | tf_op jit(solution)/shard_map/ppermute | solution.py:332
  17.3 1.9 %collective-permute-done.10 = bf16[384,512]{1,0:T(8,128)(2,1)S(1)} collective-permute-done((bf16[384,512]{1,0:T(8,128)(2,1)S(1)}, bf16[384,512]{1,0:T(8,128)(2,1)S(1)}, u32[]{:S(2)}, u32[]{:S(2)}) %collective-permute-start.10) | collective-permute-done | bytes 393248 | tf_op jit(solution)/shard_map/ppermute | solution.py:332
  19.4 3.5 %collective-permute-start.13 = (bf16[96,512]{1,0:T(8,128)(2,1)S(1)}, bf16[96,512]{1,0:T(8,128)(2,1)S(1)}, u32[]{:S(2)}, u32[]{:S(2)}) collective-permute-start(bf16[96,512]{1,0:T(8,128)(2,1)S(1)} %get-tuple-element.62), channel_id=1, source_target_pairs={{0,12},{2,14},{4,8},{6,10},{8,4},{10,6},{12,0},{14,2},{16,28},{18,... | collective-permute-start | bytes 294920 | tf_op jit(solution)/shard_map/ppermute | solution.py:332
  23.6 1.9 %collective-permute-start.4 = (bf16[2,512,512]{2,1,0:T(8,128)(2,1)S(1)}, bf16[2,512,512]{2,1,0:T(8,128)(2,1)}, u32[]{:S(2)}, u32[]{:S(2)}) collective-permute-start(bf16[2,512,512]{2,1,0:T(8,128)(2,1)S(1)} %pad_maximum_fusion.own_hbm), channel_id=1, source_target_pairs={{0,2},{2,0},{4,6},{6,4},{8,10},{10,8},{12,14},{14,12},{16,18},{18,... | collective-permute-start | bytes 3145736 | tf_op jit(solution)/shard_map/ppermute | solution.py:332
  25.6 2.6 %collective-permute-start.5 = (bf16[96,512]{1,0:T(8,128)(2,1)S(1)}, bf16[96,512]{1,0:T(8,128)(2,1)S(1)}, u32[]{:S(2)}, u32[]{:S(2)}) collective-permute-start(bf16[96,512]{1,0:T(8,128)(2,1)S(1)} %fusion.6.p_ref), channel_id=1, source_target_pairs={{0,16},{2,18},{4,20},{6,22},{8,24},{10,26},{12,28},{14,30},{16,0},... | collective-permute-start | bytes 294920 | tf_op jit(solution)/shard_map/ppermute | solution.py:332
  29.2 2.6 %collective-permute-start.14 = (bf16[96,512]{1,0:T(8,128)(2,1)S(1)}, bf16[96,512]{1,0:T(8,128)(2,1)S(1)}, u32[]{:S(2)}, u32[]{:S(2)}) collective-permute-start(bf16[96,512]{1,0:T(8,128)(2,1)S(1)} %fusion.3.p_ref), channel_id=1, source_target_pairs={{0,16},{2,18},{4,20},{6,22},{8,24},{10,26},{12,28},{14,30},{16,0},... | collective-permute-start | bytes 294920 | tf_op jit(solution)/shard_map/ppermute | solution.py:332
  33.1 1.5 %collective-permute-start.7 = (bf16[96,512]{1,0:T(8,128)(2,1)S(1)}, bf16[96,512]{1,0:T(8,128)(2,1)S(1)}, u32[]{:S(2)}, u32[]{:S(2)}) collective-permute-start(bf16[96,512]{1,0:T(8,128)(2,1)S(1)} %get-tuple-element.34.refs_0_), channel_id=1, source_target_pairs={{0,8},{2,10},{4,12},{6,14},{8,0},{10,2},{12,4},{14,6},{16,24},{18,... | collective-permute-start | bytes 294920 | tf_op jit(solution)/shard_map/ppermute | solution.py:332
  34.6 1.7 %collective-permute-start.8 = (bf16[96,512]{1,0:T(8,128)(2,1)S(1)}, bf16[96,512]{1,0:T(8,128)(2,1)S(1)}, u32[]{:S(2)}, u32[]{:S(2)}) collective-permute-start(bf16[96,512]{1,0:T(8,128)(2,1)S(1)} %get-tuple-element.34.refs_0_), channel_id=1, source_target_pairs={{0,12},{2,14},{4,8},{6,10},{8,4},{10,6},{12,0},{14,2},{16,28},{18,... | collective-permute-start | bytes 294920 | tf_op jit(solution)/shard_map/ppermute | solution.py:332
  37.4 1.6 %collective-permute-start.16 = (bf16[96,512]{1,0:T(8,128)(2,1)S(1)}, bf16[96,512]{1,0:T(8,128)(2,1)S(1)}, u32[]{:S(2)}, u32[]{:S(2)}) collective-permute-start(bf16[96,512]{1,0:T(8,128)(2,1)S(1)} %get-tuple-element.38.refs_5_), channel_id=1, source_target_pairs={{0,8},{2,10},{4,12},{6,14},{8,0},{10,2},{12,4},{14,6},{16,24},{18,... | collective-permute-start | bytes 294920 | tf_op jit(solution)/shard_map/ppermute | solution.py:332
  39.0 1.3 %collective-permute-start.17 = (bf16[96,512]{1,0:T(8,128)(2,1)S(1)}, bf16[96,512]{1,0:T(8,128)(2,1)S(1)}, u32[]{:S(2)}, u32[]{:S(2)}) collective-permute-start(bf16[96,512]{1,0:T(8,128)(2,1)S(1)} %get-tuple-element.38.refs_5_), channel_id=1, source_target_pairs={{0,12},{2,14},{4,8},{6,10},{8,4},{10,6},{12,0},{14,2},{16,28},{18,... | collective-permute-start | bytes 294920 | tf_op jit(solution)/shard_map/ppermute | solution.py:332
  41.1 1.6 %collective-permute-start.9 = (bf16[384,512]{1,0:T(8,128)(2,1)}, bf16[384,512]{1,0:T(8,128)(2,1)S(1)}, u32[]{:S(2)}, u32[]{:S(2)}) collective-permute-start(bf16[384,512]{1,0:T(8,128)(2,1)} %pad_maximum_fusion.1), channel_id=1, source_target_pairs={{0,2},{2,0},{4,6},{6,4},{8,10},{10,8},{12,14},{14,12},{16,18},{18,... | collective-permute-start | bytes 1179656 | tf_op jit(solution)/shard_map/ppermute | solution.py:332
  42.7 2.0 %collective-permute-done.17.refs_8_ = bf16[96,512]{1,0:T(8,128)(2,1)S(1)} collective-permute-done((bf16[96,512]{1,0:T(8,128)(2,1)S(1)}, bf16[96,512]{1,0:T(8,128)(2,1)S(1)}, u32[]{:S(2)}, u32[]{:S(2)}) %collective-permute-start.17) | collective-permute-done | bytes 98336 | tf_op jit(solution)/shard_map/ppermute | solution.py:332
  46.7 2.4 %collective-permute-done.9.refs_4_ = bf16[384,512]{1,0:T(8,128)(2,1)S(1)} collective-permute-done((bf16[384,512]{1,0:T(8,128)(2,1)}, bf16[384,512]{1,0:T(8,128)(2,1)S(1)}, u32[]{:S(2)}, u32[]{:S(2)}) %collective-permute-start.9) | collective-permute-done | bytes 393248 | tf_op jit(solution)/shard_map/ppermute | solution.py:332
  49.1 4.3 %collective-permute-done.18.refs_9_ = bf16[384,512]{1,0:T(8,128)(2,1)S(1)} collective-permute-done((bf16[384,512]{1,0:T(8,128)(2,1)}, bf16[384,512]{1,0:T(8,128)(2,1)S(1)}, u32[]{:S(2)}, u32[]{:S(2)}) %collective-permute-start.18) | collective-permute-done | bytes 393248 | tf_op jit(solution)/shard_map/ppermute | solution.py:332
  53.4 4.7 %next_grads.1 = (bf16[96,512]{1,0:T(8,128)(2,1)S(1)}, bf16[96,512]{1,0:T(8,128)(2,1)S(1)}, bf16[96,512]{1,0:T(8,128)(2,1)S(1)}, bf16[96,512]{1,0:T(8,128)(2,1)S(...) custom-call(s32[1]{0:T(128)} %bitcast.me_ref, ...), custom_call_target="tpu_custom_call" | custom-call | tf_op jit(solution)/shard_map/next_grads/pallas_call | solution.py:171
  58.1 1.6 %collective-permute-start.25 = (bf16[96,512]{1,0:T(8,128)(2,1)S(1)}, bf16[96,512]{1,0:T(8,128)(2,1)S(1)}, u32[]{:S(2)}, u32[]{:S(2)}) collective-permute-start(bf16[96,512]{1,0:T(8,128)(2,1)S(1)} %get-tuple-element.48), channel_id=1, source_target_pairs={{0,12},{2,14},{4,8},{6,10},{8,4},{10,6},{12,0},{14,2},{16,28},{18,... | collective-permute-start | bytes 294920 | tf_op jit(solution)/shard_map/ppermute | solution.py:332
  61.9 1.6 %collective-permute-start.21 = (bf16[96,512]{1,0:T(8,128)(2,1)S(1)}, bf16[96,512]{1,0:T(8,128)(2,1)S(1)}, u32[]{:S(2)}, u32[]{:S(2)}) collective-permute-start(bf16[96,512]{1,0:T(8,128)(2,1)S(1)} %get-tuple-element.42), channel_id=1, source_target_pairs={{0,12},{2,14},{4,8},{6,10},{8,4},{10,6},{12,0},{14,2},{16,28},{18,... | collective-permute-start | bytes 294920 | tf_op jit(solution)/shard_map/ppermute | solution.py:332
  63.7 1.3 %collective-permute-start.20 = (bf16[96,512]{1,0:T(8,128)(2,1)S(1)}, bf16[96,512]{1,0:T(8,128)(2,1)S(1)}, u32[]{:S(2)}, u32[]{:S(2)}) collective-permute-start(bf16[96,512]{1,0:T(8,128)(2,1)S(1)} %get-tuple-element.41), channel_id=1, source_target_pairs={{0,8},{2,10},{4,12},{6,14},{8,0},{10,2},{12,4},{14,6},{16,24},{18,... | collective-permute-start | bytes 294920 | tf_op jit(solution)/shard_map/ppermute | solution.py:332
  65.8 3.2 %collective-permute-start.26 = (bf16[96,512]{1,0:T(8,128)(2,1)S(1)}, bf16[96,512]{1,0:T(8,128)(2,1)S(1)}, u32[]{:S(2)}, u32[]{:S(2)}) collective-permute-start(bf16[96,512]{1,0:T(8,128)(2,1)S(1)} %add_convert_fusion.p_ref), channel_id=1, source_target_pairs={{0,16},{2,18},{4,20},{6,22},{8,24},{10,26},{12,28},{14,30},{16,0},... | collective-permute-start | bytes 294920 | tf_op jit(solution)/shard_map/ppermute | solution.py:332
  69.0 3.4 %collective-permute-done.20 = bf16[96,512]{1,0:T(8,128)(2,1)S(1)} collective-permute-done((bf16[96,512]{1,0:T(8,128)(2,1)S(1)}, bf16[96,512]{1,0:T(8,128)(2,1)S(1)}, u32[]{:S(2)}, u32[]{:S(2)}) %collective-permute-start.20) | collective-permute-done | bytes 98336 | tf_op jit(solution)/shard_map/ppermute | solution.py:332
  74.9 1.8 %collective-permute-start.30 = (bf16[96,512]{1,0:T(8,128)(2,1)S(1)}, bf16[96,512]{1,0:T(8,128)(2,1)S(1)}, u32[]{:S(2)}, u32[]{:S(2)}) collective-permute-start(bf16[96,512]{1,0:T(8,128)(2,1)S(1)} %update.7.refs_0_), channel_id=1, source_target_pairs={{0,8},{2,10},{4,12},{6,14},{8,0},{10,2},{12,4},{14,6},{16,24},{18,... | collective-permute-start | bytes 294920 | tf_op jit(solution)/shard_map/ppermute | solution.py:332
  77.3 2.2 %collective-permute-done.22.q_ref = bf16[96,512]{1,0:T(8,128)(2,1)S(1)} collective-permute-done((bf16[96,512]{1,0:T(8,128)(2,1)S(1)}, bf16[96,512]{1,0:T(8,128)(2,1)S(1)}, u32[]{:S(2)}, u32[]{:S(2)}) %collective-permute-start.22) | collective-permute-done | bytes 98336 | tf_op jit(solution)/shard_map/ppermute | solution.py:332
  81.9 2.5 %collective-permute-start.35 = (bf16[96,512]{1,0:T(8,128)(2,1)S(1)}, bf16[96,512]{1,0:T(8,128)(2,1)S(1)}, u32[]{:S(2)}, u32[]{:S(2)}) collective-permute-start(bf16[96,512]{1,0:T(8,128)(2,1)S(1)} %update.6.refs_5_), channel_id=1, source_target_pairs={{0,12},{2,14},{4,8},{6,10},{8,4},{10,6},{12,0},{14,2},{16,28},{18,... | collective-permute-start | bytes 294920 | tf_op jit(solution)/shard_map/ppermute | solution.py:332
  85.2 1.7 %collective-permute-done.34.refs_7_ = bf16[96,512]{1,0:T(8,128)(2,1)S(1)} collective-permute-done((bf16[96,512]{1,0:T(8,128)(2,1)S(1)}, bf16[96,512]{1,0:T(8,128)(2,1)S(1)}, u32[]{:S(2)}, u32[]{:S(2)}) %collective-permute-start.34) | collective-permute-done | bytes 98336 | tf_op jit(solution)/shard_map/ppermute | solution.py:332
  86.8 1.6 %collective-permute-done.35.refs_8_ = bf16[96,512]{1,0:T(8,128)(2,1)S(1)} collective-permute-done((bf16[96,512]{1,0:T(8,128)(2,1)S(1)}, bf16[96,512]{1,0:T(8,128)(2,1)S(1)}, u32[]{:S(2)}, u32[]{:S(2)}) %collective-permute-start.35) | collective-permute-done | bytes 98336 | tf_op jit(solution)/shard_map/ppermute | solution.py:332
  88.5 1.6 %collective-permute-start.36 = (bf16[384,512]{1,0:T(8,128)(2,1)S(1)}, bf16[384,512]{1,0:T(8,128)(2,1)S(1)}, u32[]{:S(2)}, u32[]{:S(2)}) collective-permute-start(bf16[384,512]{1,0:T(8,128)(2,1)S(1)} %pad_maximum_fusion.4), channel_id=1, source_target_pairs={{0,2},{2,0},{4,6},{6,4},{8,10},{10,8},{12,14},{14,12},{16,18},{18,... | collective-permute-start | bytes 1179656 | tf_op jit(solution)/shard_map/ppermute | solution.py:332
  90.8 1.7 %project.2.refs_0_ = bf16[2,512,1024]{2,1,0:T(8,128)(2,1)} custom-call(f32[512,1024]{1,0:T(8,128)S(1)} %project_own.2.sum_ref, bf16[512,512]{1,0:T(8,128)(2,1)S(1)} %collective-permute-done.27.o_ref, bf16[512,1024]{1,0:T(8,128)(2,1)S(1)} %collective-permute-done.28.proj_ref), custom_call_target="tpu_custom_call" | custom-call | tf_op jit(solution)/shard_map/project/pallas_call | solution.py:295
  92.5 4.1 %collective-permute-done.36.refs_9_ = bf16[384,512]{1,0:T(8,128)(2,1)S(1)} collective-permute-done((bf16[384,512]{1,0:T(8,128)(2,1)S(1)}, bf16[384,512]{1,0:T(8,128)(2,1)S(1)}, u32[]{:S(2)}, u32[]{:S(2)}) %collective-permute-start.36) | collective-permute-done | bytes 393248 | tf_op jit(solution)/shard_map/ppermute | solution.py:332
  99.7 1.7 %project.3 = bf16[2,512,1024]{2,1,0:T(8,128)(2,1)} custom-call(f32[512,1024]{1,0:T(8,128)S(1)} %project_own.3.sum_ref, bf16[512,512]{1,0:T(8,128)(2,1)S(1)} %collective-permute-done.37.o_ref, bf16[512,1024]{1,0:T(8,128)(2,1)S(1)} %collective-permute-done.28.proj_ref, bf16[2,512,1024]{2,1,0:T(8,128)(2,1)} %project.2.refs_0_), custom_call_target="tpu_custom_call", output_to_operand_aliasing={{}: (3, {})} | custom-call | tf_op jit(solution)/shard_map/project/pallas_call | solution.py:295
  (87 shorter events, 21.7 us)
Async XLA Ops:
  4.6 8.8 %collective-permute-start = (bf16[384,512]{1,0:T(8,128)(2,1)S(1)}, bf16[384,512]{1,0:T(8,128)(2,1)S(1)}, u32[]{:S(2)}, u32[]{:S(2)}) collective-permute-start(bf16[384,512]{1,0:T(8,128)(2,1)S(1)} %get-tuple-element.31), channel_id=1, source_target_pairs={{0,2},{2,0},{4,6},{6,4},{8,10},{10,8},{12,14},{14,12},{16,18},{18,... | collective-permute-start | bytes 1179656 | tf_op jit(solution)/shard_map/ppermute | solution.py:332
  7.6 11.6 %collective-permute-start.10 = (bf16[384,512]{1,0:T(8,128)(2,1)S(1)}, bf16[384,512]{1,0:T(8,128)(2,1)S(1)}, u32[]{:S(2)}, u32[]{:S(2)}) collective-permute-start(bf16[384,512]{1,0:T(8,128)(2,1)S(1)} %get-tuple-element.36), channel_id=1, source_target_pairs={{0,2},{2,0},{4,6},{6,4},{8,10},{10,8},{12,14},{14,12},{16,18},{18,... | collective-permute-start | bytes 1179656 | tf_op jit(solution)/shard_map/ppermute | solution.py:332
  13.5 9.9 %collective-permute-start.3 = (bf16[96,512]{1,0:T(8,128)(2,1)S(1)}, bf16[96,512]{1,0:T(8,128)(2,1)S(1)}, u32[]{:S(2)}, u32[]{:S(2)}) collective-permute-start(bf16[96,512]{1,0:T(8,128)(2,1)S(1)} %get-tuple-element.65), channel_id=1, source_target_pairs={{0,12},{2,14},{4,8},{6,10},{8,4},{10,6},{12,0},{14,2},{16,28},{18,... | collective-permute-start | bytes 294920 | tf_op jit(solution)/shard_map/ppermute | solution.py:332
  16.6 6.9 %collective-permute-start.2 = (bf16[96,512]{1,0:T(8,128)(2,1)S(1)}, bf16[96,512]{1,0:T(8,128)(2,1)S(1)}, u32[]{:S(2)}, u32[]{:S(2)}) collective-permute-start(bf16[96,512]{1,0:T(8,128)(2,1)S(1)} %get-tuple-element.66), channel_id=1, source_target_pairs={{0,8},{2,10},{4,12},{6,14},{8,0},{10,2},{12,4},{14,6},{16,24},{18,... | collective-permute-start | bytes 294920 | tf_op jit(solution)/shard_map/ppermute | solution.py:332
  17.1 6.5 %collective-permute-start.1 = (bf16[96,512]{1,0:T(8,128)(2,1)S(1)}, bf16[96,512]{1,0:T(8,128)(2,1)S(1)}, u32[]{:S(2)}, u32[]{:S(2)}) collective-permute-start(bf16[96,512]{1,0:T(8,128)(2,1)S(1)} %get-tuple-element.64), channel_id=1, source_target_pairs={{0,4},{2,6},{4,0},{6,2},{8,12},{10,14},{12,8},{14,10},{16,20},{18,... | collective-permute-start | bytes 294920 | tf_op jit(solution)/shard_map/ppermute | solution.py:332
  19.4 8.8 %collective-permute-start.13 = (bf16[96,512]{1,0:T(8,128)(2,1)S(1)}, bf16[96,512]{1,0:T(8,128)(2,1)S(1)}, u32[]{:S(2)}, u32[]{:S(2)}) collective-permute-start(bf16[96,512]{1,0:T(8,128)(2,1)S(1)} %get-tuple-element.62), channel_id=1, source_target_pairs={{0,12},{2,14},{4,8},{6,10},{8,4},{10,6},{12,0},{14,2},{16,28},{18,... | collective-permute-start | bytes 294920 | tf_op jit(solution)/shard_map/ppermute | solution.py:332
  22.9 6.2 %collective-permute-start.12 = (bf16[96,512]{1,0:T(8,128)(2,1)S(1)}, bf16[96,512]{1,0:T(8,128)(2,1)S(1)}, u32[]{:S(2)}, u32[]{:S(2)}) collective-permute-start(bf16[96,512]{1,0:T(8,128)(2,1)S(1)} %get-tuple-element.63), channel_id=1, source_target_pairs={{0,8},{2,10},{4,12},{6,14},{8,0},{10,2},{12,4},{14,6},{16,24},{18,... | collective-permute-start | bytes 294920 | tf_op jit(solution)/shard_map/ppermute | solution.py:332
  23.4 5.8 %collective-permute-start.11 = (bf16[96,512]{1,0:T(8,128)(2,1)S(1)}, bf16[96,512]{1,0:T(8,128)(2,1)S(1)}, u32[]{:S(2)}, u32[]{:S(2)}) collective-permute-start(bf16[96,512]{1,0:T(8,128)(2,1)S(1)} %get-tuple-element.61), channel_id=1, source_target_pairs={{0,4},{2,6},{4,0},{6,2},{8,12},{10,14},{12,8},{14,10},{16,20},{18,... | collective-permute-start | bytes 294920 | tf_op jit(solution)/shard_map/ppermute | solution.py:332
  23.6 29.8 %collective-permute-start.4 = (bf16[2,512,512]{2,1,0:T(8,128)(2,1)S(1)}, bf16[2,512,512]{2,1,0:T(8,128)(2,1)}, u32[]{:S(2)}, u32[]{:S(2)}) collective-permute-start(bf16[2,512,512]{2,1,0:T(8,128)(2,1)S(1)} %pad_maximum_fusion.own_hbm), channel_id=1, source_target_pairs={{0,2},{2,0},{4,6},{6,4},{8,10},{10,8},{12,14},{14,12},{16,18},{18,... | collective-permute-start | bytes 3145736 | tf_op jit(solution)/shard_map/ppermute | solution.py:332
  25.6 7.0 %collective-permute-start.5 = (bf16[96,512]{1,0:T(8,128)(2,1)S(1)}, bf16[96,512]{1,0:T(8,128)(2,1)S(1)}, u32[]{:S(2)}, u32[]{:S(2)}) collective-permute-start(bf16[96,512]{1,0:T(8,128)(2,1)S(1)} %fusion.6.p_ref), channel_id=1, source_target_pairs={{0,16},{2,18},{4,20},{6,22},{8,24},{10,26},{12,28},{14,30},{16,0},... | collective-permute-start | bytes 294920 | tf_op jit(solution)/shard_map/ppermute | solution.py:332
  29.2 7.1 %collective-permute-start.14 = (bf16[96,512]{1,0:T(8,128)(2,1)S(1)}, bf16[96,512]{1,0:T(8,128)(2,1)S(1)}, u32[]{:S(2)}, u32[]{:S(2)}) collective-permute-start(bf16[96,512]{1,0:T(8,128)(2,1)S(1)} %fusion.3.p_ref), channel_id=1, source_target_pairs={{0,16},{2,18},{4,20},{6,22},{8,24},{10,26},{12,28},{14,30},{16,0},... | collective-permute-start | bytes 294920 | tf_op jit(solution)/shard_map/ppermute | solution.py:332
  33.1 5.9 %collective-permute-start.7 = (bf16[96,512]{1,0:T(8,128)(2,1)S(1)}, bf16[96,512]{1,0:T(8,128)(2,1)S(1)}, u32[]{:S(2)}, u32[]{:S(2)}) collective-permute-start(bf16[96,512]{1,0:T(8,128)(2,1)S(1)} %get-tuple-element.34.refs_0_), channel_id=1, source_target_pairs={{0,8},{2,10},{4,12},{6,14},{8,0},{10,2},{12,4},{14,6},{16,24},{18,... | collective-permute-start | bytes 294920 | tf_op jit(solution)/shard_map/ppermute | solution.py:332
  34.6 5.7 %collective-permute-start.8 = (bf16[96,512]{1,0:T(8,128)(2,1)S(1)}, bf16[96,512]{1,0:T(8,128)(2,1)S(1)}, u32[]{:S(2)}, u32[]{:S(2)}) collective-permute-start(bf16[96,512]{1,0:T(8,128)(2,1)S(1)} %get-tuple-element.34.refs_0_), channel_id=1, source_target_pairs={{0,12},{2,14},{4,8},{6,10},{8,4},{10,6},{12,0},{14,2},{16,28},{18,... | collective-permute-start | bytes 294920 | tf_op jit(solution)/shard_map/ppermute | solution.py:332
  36.5 6.1 %collective-permute-start.15 = (bf16[96,512]{1,0:T(8,128)(2,1)S(1)}, bf16[96,512]{1,0:T(8,128)(2,1)S(1)}, u32[]{:S(2)}, u32[]{:S(2)}) collective-permute-start(bf16[96,512]{1,0:T(8,128)(2,1)S(1)} %get-tuple-element.38.refs_5_), channel_id=1, source_target_pairs={{0,4},{2,6},{4,0},{6,2},{8,12},{10,14},{12,8},{14,10},{16,20},{18,... | collective-permute-start | bytes 294920 | tf_op jit(solution)/shard_map/ppermute | solution.py:332
  39.0 5.6 %collective-permute-start.17 = (bf16[96,512]{1,0:T(8,128)(2,1)S(1)}, bf16[96,512]{1,0:T(8,128)(2,1)S(1)}, u32[]{:S(2)}, u32[]{:S(2)}) collective-permute-start(bf16[96,512]{1,0:T(8,128)(2,1)S(1)} %get-tuple-element.38.refs_5_), channel_id=1, source_target_pairs={{0,12},{2,14},{4,8},{6,10},{8,4},{10,6},{12,0},{14,2},{16,28},{18,... | collective-permute-start | bytes 294920 | tf_op jit(solution)/shard_map/ppermute | solution.py:332
  41.1 8.0 %collective-permute-start.9 = (bf16[384,512]{1,0:T(8,128)(2,1)}, bf16[384,512]{1,0:T(8,128)(2,1)S(1)}, u32[]{:S(2)}, u32[]{:S(2)}) collective-permute-start(bf16[384,512]{1,0:T(8,128)(2,1)} %pad_maximum_fusion.1), channel_id=1, source_target_pairs={{0,2},{2,0},{4,6},{6,4},{8,10},{10,8},{12,14},{14,12},{16,18},{18,... | collective-permute-start | bytes 1179656 | tf_op jit(solution)/shard_map/ppermute | solution.py:332
  45.4 8.0 %collective-permute-start.18 = (bf16[384,512]{1,0:T(8,128)(2,1)}, bf16[384,512]{1,0:T(8,128)(2,1)S(1)}, u32[]{:S(2)}, u32[]{:S(2)}) collective-permute-start(bf16[384,512]{1,0:T(8,128)(2,1)} %pad_maximum_fusion.2), channel_id=1, source_target_pairs={{0,2},{2,0},{4,6},{6,4},{8,10},{10,8},{12,14},{14,12},{16,18},{18,... | collective-permute-start | bytes 1179656 | tf_op jit(solution)/shard_map/ppermute | solution.py:332
  58.1 5.6 %collective-permute-start.25 = (bf16[96,512]{1,0:T(8,128)(2,1)S(1)}, bf16[96,512]{1,0:T(8,128)(2,1)S(1)}, u32[]{:S(2)}, u32[]{:S(2)}) collective-permute-start(bf16[96,512]{1,0:T(8,128)(2,1)S(1)} %get-tuple-element.48), channel_id=1, source_target_pairs={{0,12},{2,14},{4,8},{6,10},{8,4},{10,6},{12,0},{14,2},{16,28},{18,... | collective-permute-start | bytes 294920 | tf_op jit(solution)/shard_map/ppermute | solution.py:332
  59.7 5.4 %collective-permute-start.24 = (bf16[96,512]{1,0:T(8,128)(2,1)S(1)}, bf16[96,512]{1,0:T(8,128)(2,1)S(1)}, u32[]{:S(2)}, u32[]{:S(2)}) collective-permute-start(bf16[96,512]{1,0:T(8,128)(2,1)S(1)} %get-tuple-element.47), channel_id=1, source_target_pairs={{0,8},{2,10},{4,12},{6,14},{8,0},{10,2},{12,4},{14,6},{16,24},{18,... | collective-permute-start | bytes 294920 | tf_op jit(solution)/shard_map/ppermute | solution.py:332
  61.9 28.9 %collective-permute-start.28 = (bf16[512,1024]{1,0:T(8,128)(2,1)S(1)}, bf16[512,1024]{1,0:T(8,128)(2,1)S(1)}, u32[]{:S(2)}, u32[]{:S(2)}) collective-permute-start(bf16[512,1024]{1,0:T(8,128)(2,1)S(1)} %get-tuple-element.55), channel_id=1, source_target_pairs={{0,1},{1,0},{2,3},{3,2},{4,5},{5,4},{6,7},{7,6},{8,9},{9,8},{10,11... | collective-permute-start | bytes 3145736 | tf_op jit(solution)/shard_map/ppermute | solution.py:335
  61.9 7.0 %collective-permute-start.21 = (bf16[96,512]{1,0:T(8,128)(2,1)S(1)}, bf16[96,512]{1,0:T(8,128)(2,1)S(1)}, u32[]{:S(2)}, u32[]{:S(2)}) collective-permute-start(bf16[96,512]{1,0:T(8,128)(2,1)S(1)} %get-tuple-element.42), channel_id=1, source_target_pairs={{0,12},{2,14},{4,8},{6,10},{8,4},{10,6},{12,0},{14,2},{16,28},{18,... | collective-permute-start | bytes 294920 | tf_op jit(solution)/shard_map/ppermute | solution.py:332
  63.7 8.7 %collective-permute-start.20 = (bf16[96,512]{1,0:T(8,128)(2,1)S(1)}, bf16[96,512]{1,0:T(8,128)(2,1)S(1)}, u32[]{:S(2)}, u32[]{:S(2)}) collective-permute-start(bf16[96,512]{1,0:T(8,128)(2,1)S(1)} %get-tuple-element.41), channel_id=1, source_target_pairs={{0,8},{2,10},{4,12},{6,14},{8,0},{10,2},{12,4},{14,6},{16,24},{18,... | collective-permute-start | bytes 294920 | tf_op jit(solution)/shard_map/ppermute | solution.py:332
  65.0 7.3 %collective-permute-start.19 = (bf16[96,512]{1,0:T(8,128)(2,1)S(1)}, bf16[96,512]{1,0:T(8,128)(2,1)S(1)}, u32[]{:S(2)}, u32[]{:S(2)}) collective-permute-start(bf16[96,512]{1,0:T(8,128)(2,1)S(1)} %get-tuple-element.40), channel_id=1, source_target_pairs={{0,4},{2,6},{4,0},{6,2},{8,12},{10,14},{12,8},{14,10},{16,20},{18,... | collective-permute-start | bytes 294920 | tf_op jit(solution)/shard_map/ppermute | solution.py:332
  65.8 7.8 %collective-permute-start.26 = (bf16[96,512]{1,0:T(8,128)(2,1)S(1)}, bf16[96,512]{1,0:T(8,128)(2,1)S(1)}, u32[]{:S(2)}, u32[]{:S(2)}) collective-permute-start(bf16[96,512]{1,0:T(8,128)(2,1)S(1)} %add_convert_fusion.p_ref), channel_id=1, source_target_pairs={{0,16},{2,18},{4,20},{6,22},{8,24},{10,26},{12,28},{14,30},{16,0},... | collective-permute-start | bytes 294920 | tf_op jit(solution)/shard_map/ppermute | solution.py:332
  72.4 7.2 %collective-permute-start.22 = (bf16[96,512]{1,0:T(8,128)(2,1)S(1)}, bf16[96,512]{1,0:T(8,128)(2,1)S(1)}, u32[]{:S(2)}, u32[]{:S(2)}) collective-permute-start(bf16[96,512]{1,0:T(8,128)(2,1)S(1)} %add_convert_fusion.1.p_ref), channel_id=1, source_target_pairs={{0,16},{2,18},{4,20},{6,22},{8,24},{10,26},{12,28},{14,30},{16,0},... | collective-permute-start | bytes 294920 | tf_op jit(solution)/shard_map/ppermute | solution.py:332
  73.8 8.1 %collective-permute-start.29 = (bf16[96,512]{1,0:T(8,128)(2,1)S(1)}, bf16[96,512]{1,0:T(8,128)(2,1)S(1)}, u32[]{:S(2)}, u32[]{:S(2)}) collective-permute-start(bf16[96,512]{1,0:T(8,128)(2,1)S(1)} %update.7.refs_0_), channel_id=1, source_target_pairs={{0,4},{2,6},{4,0},{6,2},{8,12},{10,14},{12,8},{14,10},{16,20},{18,... | collective-permute-start | bytes 294920 | tf_op jit(solution)/shard_map/ppermute | solution.py:332
  74.9 7.0 %collective-permute-start.30 = (bf16[96,512]{1,0:T(8,128)(2,1)S(1)}, bf16[96,512]{1,0:T(8,128)(2,1)S(1)}, u32[]{:S(2)}, u32[]{:S(2)}) collective-permute-start(bf16[96,512]{1,0:T(8,128)(2,1)S(1)} %update.7.refs_0_), channel_id=1, source_target_pairs={{0,8},{2,10},{4,12},{6,14},{8,0},{10,2},{12,4},{14,6},{16,24},{18,... | collective-permute-start | bytes 294920 | tf_op jit(solution)/shard_map/ppermute | solution.py:332
  76.7 7.7 %collective-permute-start.31 = (bf16[96,512]{1,0:T(8,128)(2,1)S(1)}, bf16[96,512]{1,0:T(8,128)(2,1)S(1)}, u32[]{:S(2)}, u32[]{:S(2)}) collective-permute-start(bf16[96,512]{1,0:T(8,128)(2,1)S(1)} %update.7.refs_0_), channel_id=1, source_target_pairs={{0,12},{2,14},{4,8},{6,10},{8,4},{10,6},{12,0},{14,2},{16,28},{18,... | collective-permute-start | bytes 294920 | tf_op jit(solution)/shard_map/ppermute | solution.py:332
  81.9 6.5 %collective-permute-start.35 = (bf16[96,512]{1,0:T(8,128)(2,1)S(1)}, bf16[96,512]{1,0:T(8,128)(2,1)S(1)}, u32[]{:S(2)}, u32[]{:S(2)}) collective-permute-start(bf16[96,512]{1,0:T(8,128)(2,1)S(1)} %update.6.refs_5_), channel_id=1, source_target_pairs={{0,12},{2,14},{4,8},{6,10},{8,4},{10,6},{12,0},{14,2},{16,28},{18,... | collective-permute-start | bytes 294920 | tf_op jit(solution)/shard_map/ppermute | solution.py:332
  84.4 6.4 %collective-permute-start.27 = (bf16[512,512]{1,0:T(8,128)(2,1)S(1)}, bf16[512,512]{1,0:T(8,128)(2,1)S(1)}, u32[]{:S(2)}, u32[]{:S(2)}) collective-permute-start(bf16[512,512]{1,0:T(8,128)(2,1)S(1)} %apply.2.o_ref), channel_id=1, source_target_pairs={{0,1},{1,0},{2,3},{3,2},{4,5},{5,4},{6,7},{7,6},{8,9},{9,8},{10,11... | collective-permute-start | bytes 1572872 | tf_op jit(solution)/shard_map/ppermute | solution.py:335
  84.5 8.0 %collective-permute-start.32 = (bf16[384,512]{1,0:T(8,128)(2,1)S(1)}, bf16[384,512]{1,0:T(8,128)(2,1)S(1)}, u32[]{:S(2)}, u32[]{:S(2)}) collective-permute-start(bf16[384,512]{1,0:T(8,128)(2,1)S(1)} %pad_maximum_fusion.3), channel_id=1, source_target_pairs={{0,2},{2,0},{4,6},{6,4},{8,10},{10,8},{12,14},{14,12},{16,18},{18,... | collective-permute-start | bytes 1179656 | tf_op jit(solution)/shard_map/ppermute | solution.py:332
  88.5 8.2 %collective-permute-start.36 = (bf16[384,512]{1,0:T(8,128)(2,1)S(1)}, bf16[384,512]{1,0:T(8,128)(2,1)S(1)}, u32[]{:S(2)}, u32[]{:S(2)}) collective-permute-start(bf16[384,512]{1,0:T(8,128)(2,1)S(1)} %pad_maximum_fusion.4), channel_id=1, source_target_pairs={{0,2},{2,0},{4,6},{6,4},{8,10},{10,8},{12,14},{14,12},{16,18},{18,... | collective-permute-start | bytes 1179656 | tf_op jit(solution)/shard_map/ppermute | solution.py:332
  (13 other events, 118.3 us)

commit v5 on v4

--- a/solution.py
+++ b/solution.py
@@ -74,21 +74,22 @@
         db_s[span, :] = (dh * silu).astype(bf16)
 
 
-def first_grads_kernel(me_ref, k_hbm, v_hbm, r_ref, w_hbm, *refs):
+def first_grads_kernel(me_ref, k_hbm, v_hbm, r_hbm, w_hbm, *refs):
     out_refs, w0_refs = refs[: 2 * CHUNKS], refs[2 * CHUNKS : 3 * CHUNKS]
-    k_s, v_s, w, da_s, db_s, hid_s, dy_s, g_s, sems = refs[3 * CHUNKS :]
+    k_s, v_s, w, da_s, db_s, hid_s, dy_s, g_s, r_s, sems = refs[3 * CHUNKS :]
     copies = [pltpu.make_async_copy(k_hbm.at[0], k_s, sems.at[0]), pltpu.make_async_copy(v_hbm.at[0], v_s, sems.at[1])]
     copies += [pltpu.make_async_copy(w_hbm.at[m], w.at[m], sems.at[2 + m]) for m in range(3)]
-    for i in (0, 2, 3, 1, 4):
+    copies.append(pltpu.make_async_copy(r_hbm.at[0], r_s, sems.at[5]))
+    for i in (0, 2, 3, 5, 1, 4):
         copies[i].start()
     me = me_ref[0]
     tok, width = k_s.shape
-    rate_col = jnp.broadcast_to(r_ref[...], (8, tok)).T[:, :1]
 
     def ready(name):
-        for i in {"gate": (0, 2), "linear": (3,), "output": (1, 4)}[name]:
+        for i in {"gate": (0, 2), "linear": (3,), "output": (5, 1, 4)}[name]:
             copies[i].wait()
         if name == "output":
+            rate_col = jnp.broadcast_to(r_s[...], (8, tok)).T[:, :1]
             dy_s[...] = (rate_col * v_s[...].astype(f32)).astype(bf16)
 
     token_grads(k_s, dy_s, w, da_s, db_s, hid_s, 0, ready)
@@ -116,12 +117,11 @@
     weights = pltpu.VMEM((3, width, width), bf16)
     return pl.pallas_call(
         first_grads_kernel,
-        grid=(1,),
         out_shape=[jax.ShapeDtypeStruct((rows, width), bf16)] * (2 * CHUNKS)
         + [jax.ShapeDtypeStruct((rows // 4, width), bf16)] * CHUNKS,
-        in_specs=[SMEM, HBM, HBM, pl.BlockSpec((None, 1, tok), lambda i: (0, 0, 0)), HBM],
+        in_specs=[SMEM] + [HBM] * 4,
         out_specs=[VMEM] * (3 * CHUNKS),
-        scratch_shapes=[square, square, weights, square, square, square, square, weights, pltpu.SemaphoreType.DMA((5,))],
+        scratch_shapes=[square, square, weights, square, square, square, square, weights, pltpu.VMEM((1, tok), f32), pltpu.SemaphoreType.DMA((6,))],
         compiler_params=params(),
         name="first_grads",
     )(me, in_hbm(k), in_hbm(v), in_hbm(r), in_hbm(init))
@@ -181,22 +181,35 @@
     )(me, in_hbm(own), in_hbm(other), *w)
 
 
-def join_kernel(*refs):
-    rows = refs[0].shape[0]
-    for i, ref in enumerate(refs[:-1]):
-        refs[-1][i * rows : (i + 1) * rows, :] = ref[...]
-
-
-def join(pieces):
-    rows, width = pieces[0].shape
-    return pl.pallas_call(
-        join_kernel,
-        out_shape=jax.ShapeDtypeStruct((len(pieces) * rows, width), bf16),
-        in_specs=[VMEM] * len(pieces),
-        out_specs=VMEM,
-        compiler_params=params(),
-        name="join",
-    )(*pieces)
+def tokens_kernel(k_hbm, v_hbm, r_hbm, out, k_s, v_s, r_s, sems):
+    loads = [pltpu.make_async_copy(x.at[1], x_s, sems.at[i]) for i, (x, x_s) in enumerate(((v_hbm, v_s), (r_hbm, r_s), (k_hbm, k_s)))]
+    for load in loads:
+        load.start()
+    tok = v_s.shape[0]
+    loads[0].wait()
+    loads[1].wait()
+    rate_col = jnp.broadcast_to(r_s[...], (8, tok)).T[:, :1]
+    v_s[...] = (rate_col * v_s[...].astype(f32)).astype(bf16)
+    loads[2].wait()
+    stores = [pltpu.make_async_copy(x_s, out.at[i], sems.at[3 + i]) for i, x_s in enumerate((k_s, v_s))]
+    for store in stores:
+        store.start()
+    for store in stores:
+        store.wait()
+
+
+def next_tokens(k, v, r):
+    _, tok, width = k.shape
+    square = pltpu.VMEM((tok, width), bf16)
+    return pl.pallas_call(
+        tokens_kernel,
+        out_shape=pltpu.HBM((2, tok, width), bf16),
+        in_specs=[HBM] * 3,
+        out_specs=HBM,
+        scratch_shapes=[square, square, pltpu.VMEM((1, tok), f32), pltpu.SemaphoreType.DMA((5,))],
+        compiler_params=params(),
+        name="next_tokens",
+    )(in_hbm(k), in_hbm(v), in_hbm(r))
 
 
 def update_kernel(keep, p_ref, q_ref, w_ref, *refs):
@@ -278,27 +291,29 @@
     )(o, proj)
 
 
-def project_kernel(sum_ref, o_ref, proj_ref, *refs):
-    refs[-1][...] = (sum_ref[...] + dot(o_ref[...], proj_ref[...])).astype(bf16)
+def project_kernel(block, sum_ref, o_ref, proj_ref, *refs):
+    out, (out_s, sems) = refs[-3], refs[-2:]
+    rows = o_ref.shape[0] // 4
+    stores = []
+    for i in range(4):
+        span = slice(i * rows, (i + 1) * rows)
+        out_s[span, :] = (sum_ref[span, :] + dot(o_ref[span, :], proj_ref[...])).astype(bf16)
+        stores.append(pltpu.make_async_copy(out_s.at[span, :], out.at[block, span, :], sems.at[i]))
+        stores[-1].start()
+    for store in stores:
+        store.wait()
 
 
 def project(block, blocks, own, o_other, proj_other, into):
-    tok, width = o_other.shape
-    cols = proj_other.shape[1]
-    args = [own, o_other, proj_other]
-    specs = [pl.BlockSpec(x.shape, lambda i: (0, 0)) for x in args]
-    aliases = {}
-    if into is not None:
-        args.append(into)
-        specs.append(pl.BlockSpec(memory_space=pl.ANY))
-        aliases = {3: 0}
-    return pl.pallas_call(
-        project_kernel,
-        grid=(1,),
+    tok, cols = own.shape
+    args = [own, o_other, proj_other] + ([] if into is None else [into])
+    return pl.pallas_call(
+        functools.partial(project_kernel, block),
         out_shape=jax.ShapeDtypeStruct((blocks, tok, cols), bf16),
-        in_specs=specs,
-        out_specs=pl.BlockSpec((None, tok, cols), lambda i: (block, 0, 0)),
-        input_output_aliases=aliases,
+        in_specs=[VMEM] * 3 + [pl.BlockSpec(memory_space=pl.ANY)] * (len(args) - 3),
+        out_specs=pl.BlockSpec(memory_space=pl.ANY),
+        scratch_shapes=[pltpu.VMEM((tok, cols), bf16), pltpu.SemaphoreType.DMA((4,))],
+        input_output_aliases={} if into is None else {3: 0},
         compiler_params=params(),
         name="project",
     )(*args)
@@ -306,7 +321,6 @@
 
 SHARDS = 8
 CHUNKS = 2
-O = {'join': (0, 0), 't01': 0, 'flows': (0, 1, 2), 'aflows': (0, 1, 2), 'p0_after_t1': 0, 'p01': (0, 0), 'u01': (0, 0), 'tokdone': '', 'tok': 'p0', 'j01': (0, 0), 'app': 'wb', 'res': 'me', 's2': ((0, 0), (0, 0)), 'A': ((0, 0), (0, 0)), 'jf': (0, 0)}
 FLOWS = ((1, 2), (2, 4), (3, 6))
 
 
@@ -355,6 +369,7 @@
 
     def on_device(queries, key_vectors, value_vectors, token_rates, fast_init, out_proj):
         blocks, tok, _, width = queries.shape
+        assert blocks == 2
         flat = lambda x: x.reshape(blocks, tok, width)
         q, k, v = flat(queries), flat(key_vectors), flat(value_vectors)
         r = token_rates.reshape(blocks, 1, tok)
@@ -364,10 +379,6 @@
         me = jnp.where(head == 0, label, swap_low_bits(label)).reshape(1)
         half = proj_all.shape[1] // heads
         proj = lax.dynamic_slice_in_dim(proj_all, head * half, half, 1)
-        tokens = None
-        if blocks > 1:
-            dy = (r[1, 0][:, None] * v[1].astype(f32)).astype(bf16)
-            tokens = jnp.stack([k[1], dy])
         proj_other = swap_head(lax.dynamic_slice_in_dim(proj_all, (1 - head) * half, half, 1))
 
         def finish(c, me, w, into):
@@ -377,70 +388,36 @@
         result = None
         for c in range(blocks):
             last = c + 1 == blocks
-            jn = join if O["join"][c] else jnp.concatenate
             if c == 0:
                 grads = first_grads(me, k, v, r, init)
                 state = [[w0] for w0 in grads[2 * CHUNKS :]]
+                tokens = next_tokens(*together(k, v, r, grads[0])[:3])
                 received = [swap(grads[2 * h], 1) for h in range(CHUNKS)]
-                pieces = []
-                for h in range(CHUNKS):
-                    got = after(received[h], pieces[-1][0]) if h and O["t01"] else received[h]
-                    pieces.append(reduce_half(got, grads[2 * h + 1]))
+                pieces = [reduce_half(received[h], grads[2 * h + 1]) for h in range(CHUNKS)]
             else:
                 grads = next_grads(me, tokens, tokens_other, w)
                 pieces = [grads[4 * h : 4 * h + 4] for h in range(CHUNKS)]
-            flows = [FLOWS[i] for i in O["flows"]]
-            received = []
+            received = [[swap(pieces[h][i].astype(bf16), bits) for i, bits in FLOWS] for h in range(CHUNKS)]
+            sums = [reduce_pieces(pieces[h], received[h]) for h in range(CHUNKS)]
+            others = [last_exchange(p) for p in sums]
+            near = []
             for h in range(CHUNKS):
-                ps = pieces[h]
-                if O["s2"][c][h]:
-                    got = swap(jnp.concatenate([ps[1].astype(bf16), ps[3].astype(bf16)]), 2)
-                    n = got.shape[0] // 2
-                    mine, send = add(ps[0], got[:n]), add(ps[2], got[n:]).astype(bf16)
-                    pieces[h] = [mine]
-                    received.append([swap(send, 4)])
-                else:
-                    received.append([swap(ps[i].astype(bf16), bits) for i, bits in flows])
-            sums, near = [], []
-            if c == 0 and O["p0_after_t1"]:
-                received[0][0] = after(received[0][0], pieces[1][0])
-            for h in range(CHUNKS):
-                if h and O["p01"][c]:
-                    received[h][0] = after(received[h][0], sums[-1])
-                sums.append(reduce_pieces(pieces[h], received[h]))
-            others = [last_exchange(p) for p in sums]
-            for h in range(CHUNKS):
-                if h:
-                    extra = []
-                    if O["u01"][c]: extra.append(near[-1][0])
-                    if not last and O["tokdone"] == "q1": extra.append(tokens_other)
-                    if extra: others[h] = after(others[h], *extra)
                 wb, state[h] = update(sums[h], others[h], state[h], not last)
-                if O["A"][c][h]:
-                    z = swap(wb, 4)
-                    g = swap(jnp.concatenate([wb, z]), 2)
-                    n = wb.shape[0]
-                    near.append([wb, g[:n], z, g[n:]])
-                else:
-                    got = {FLOWS[i][1]: swap(wb, FLOWS[i][1]) for i in O["aflows"]}
-                    near.append([wb] + [got[bits] for bits in (2, 4, 6)])
+                got = {bits: swap(wb, bits) for _, bits in FLOWS}
+                near.append([wb] + [got[bits] for bits in (2, 4, 6)])
                 if not last and h == 0:
-                    dep = {"grads": grads[0], "p0": sums[0], "t1": pieces[1][0], "t0": pieces[0][0], "p1": sums[1], "wb0": wb, "keep": grads[1]}[O["tok"]]
-                    tokens_other = swap(after(tokens, dep), 1)
+                    tokens_other = swap(after(tokens, sums[0]), 1)
             joined, far = [], []
             for h in range(CHUNKS):
-                ps = list(near[h])
-                if h and O["j01"][c]: ps[0] = after(ps[0], joined[-1])
-                if h and not last and O["tokdone"] == "j1": ps[0] = after(ps[0], tokens_other)
-                if h and O["jf"][c]: ps[0] = after(ps[0], far[0])
-                joined.append(jn(ps))
+                parts = list(near[h])
+                if h and last:
+                    parts[0] = after(parts[0], joined[-1])
+                joined.append(jnp.concatenate(parts))
                 far.append(swap(joined[-1], 1))
             if c > 0:
-                deps = {"w1": [near[1][0]], "w0": [near[0][0]], "z": near[0][1:] + near[1][1:], "z1": near[1][1:], "z0": near[0][1:], "j": joined, "f0": far[:1], "f1": far[1:], "n": [], "wb": [near[1][0], near[0][0]], "p": sums}[O["app"]]
-                me_late = after(me, *deps) if deps else me
+                me_late = after(me, near[1][0])
                 result = finish(c - 1, me_late, grads[4 * CHUNKS :], result)
-                if O["res"] == "me":
-                    me, result = together(me, result)
+                me, result = together(me, result)
             w = [x for h in range(CHUNKS) for x in (*near[h], far[h])]
         return finish(blocks - 1, me, w, result)
 

time: 102 us -> 101 us (level)
  waiting for transfers between devices: 32.4 us -> 30.5 us
  Pallas kernels: 17 us -> 18.3 us
    ppermute x35, waiting for transfers between devices: 31.3 us -> 29.5 us  [swap(): return lax.ppermute(x, ('ctx', 'head'), pairs)]
    pallas_call x3 -> x4, Pallas kernels: 7.95 us -> 9.26 us  [the longest x1 3.99 us: first_grads(): pl.pallas_call(first_grads_kernel, out_shape=[jax.ShapeDtypeStruct((rows,...]
  transfers between devices with their start and end apart: 38 -> 38, of which waited for: 15 -> 16; matrix products, arithmetic and copies ran while one was open for 3% -> 2% of each run, Pallas kernels for 5% -> 7%
where the time goes in v5:
time: 101 us
  starting transfers between devices  49.1 us (49%)
  waiting for transfers between devices  30.5 us (30%)
  Pallas kernels  18.3 us (18%)
  other arithmetic  2.05 us (2%)
    ppermute x35, starting transfers between devices, swap(): return lax.ppermute(x, ('ctx', 'head'), pairs)  48.9 us
    ppermute x35, waiting for transfers between devices, swap(): return lax.ppermute(x, ('ctx', 'head'), pairs)  29.5 us
    pallas_call x1, Pallas kernels, next_grads(): pl.pallas_call(functools.partial(next_grads_kernel, len(w)), out_shape=[j...  4.65 us
    pallas_call x1, Pallas kernels, first_grads(): pl.pallas_call(first_grads_kernel, out_shape=[jax.ShapeDtypeStruct((rows,...  3.99 us
    pallas_call x2, Pallas kernels, project(): pl.pallas_call(functools.partial(project_kernel, block), out_shape=jax.Sh...  2.92 us
    pallas_call x1, Pallas kernels, next_tokens(): pl.pallas_call(tokens_kernel, out_shape=pltpu.HBM((2, tok, width), bf16),...  2.34 us
    pallas_call x2, Pallas kernels, fast_apply(): pl.pallas_call(functools.partial(apply_kernel, len(w)), grid=(1,), out_sh...  2.09 us
  transfers between devices with their start and end apart: 38, of which 16 were waited for; matrix products, arithmetic and copies ran while one was open for 2% of the time, Pallas kernels for 7%

profile of v5, /device:TPU:0, one launch (start us, length us, event | category | flops | bytes accessed | tf_op | source)
XLA Modules:
  0.0 100.6 jit_solution(11743460327210732597)
XLA Ops:
  0.0 4.0 %first_grads.1 = (bf16[384,512]{1,0:T(8,128)(2,1)S(1)}, bf16[384,512]{1,0:T(8,128)(2,1)S(1)}, bf16[384,512]{1,0:T(8,128)(2,1)S(1)}, bf16[384,512]{1,0:T(8,128)(2...) custom-call(s32[1]{0:T(128)} %bitcast.me_ref, bf16[2,512,512]{2,1,0:T(8,128)(2,1)} %bitcast.12, ...), custom_call_target="tpu_custom_call" | custom-call | tf_op jit(solution)/shard_map/first_grads/pallas_call | solution.py:118
  4.0 3.0 %collective-permute-start = (bf16[384,512]{1,0:T(8,128)(2,1)S(1)}, bf16[384,512]{1,0:T(8,128)(2,1)S(1)}, u32[]{:S(2)}, u32[]{:S(2)}) collective-permute-start(bf16[384,512]{1,0:T(8,128)(2,1)S(1)} %get-tuple-element.34), channel_id=1, source_target_pairs={{0,2},{2,0},{4,6},{6,4},{8,10},{10,8},{12,14},{14,12},{16,18},{18,... | collective-permute-start | bytes 1179656 | tf_op jit(solution)/shard_map/ppermute | solution.py:346
  7.1 2.3 %next_tokens.1.own_hbm = bf16[2,512,512]{2,1,0:T(8,128)(2,1)} custom-call(bf16[2,512,512]{2,1,0:T(8,128)(2,1)} %bitcast.13, bf16[2,512,512]{2,1,0:T(8,128)(2,1)} %bitcast.15, f32[2,1,512]{2,1,0:T(1,128)} %bitcast.18), custom_call_target="tpu_custom_call" | custom-call | tf_op jit(solution)/shard_map/next_tokens/pallas_call | solution.py:204
  9.4 3.3 %collective-permute-done = bf16[384,512]{1,0:T(8,128)(2,1)S(1)} collective-permute-done((bf16[384,512]{1,0:T(8,128)(2,1)S(1)}, bf16[384,512]{1,0:T(8,128)(2,1)S(1)}, u32[]{:S(2)}, u32[]{:S(2)}) %collective-permute-start) | collective-permute-done | bytes 393248 | tf_op jit(solution)/shard_map/ppermute | solution.py:346
  12.9 3.1 %collective-permute-start.3 = (bf16[96,512]{1,0:T(8,128)(2,1)S(1)}, bf16[96,512]{1,0:T(8,128)(2,1)S(1)}, u32[]{:S(2)}, u32[]{:S(2)}) collective-permute-start(bf16[96,512]{1,0:T(8,128)(2,1)S(1)} %get-tuple-element.73), channel_id=1, source_target_pairs={{0,12},{2,14},{4,8},{6,10},{8,4},{10,6},{12,0},{14,2},{16,28},{18,... | collective-permute-start | bytes 294920 | tf_op jit(solution)/shard_map/ppermute | solution.py:346
  16.7 1.9 %collective-permute-done.10 = bf16[384,512]{1,0:T(8,128)(2,1)S(1)} collective-permute-done((bf16[384,512]{1,0:T(8,128)(2,1)S(1)}, bf16[384,512]{1,0:T(8,128)(2,1)S(1)}, u32[]{:S(2)}, u32[]{:S(2)}) %collective-permute-start.10) | collective-permute-done | bytes 393248 | tf_op jit(solution)/shard_map/ppermute | solution.py:346
  18.8 3.6 %collective-permute-start.13 = (bf16[96,512]{1,0:T(8,128)(2,1)S(1)}, bf16[96,512]{1,0:T(8,128)(2,1)S(1)}, u32[]{:S(2)}, u32[]{:S(2)}) collective-permute-start(bf16[96,512]{1,0:T(8,128)(2,1)S(1)} %get-tuple-element.70), channel_id=1, source_target_pairs={{0,12},{2,14},{4,8},{6,10},{8,4},{10,6},{12,0},{14,2},{16,28},{18,... | collective-permute-start | bytes 294920 | tf_op jit(solution)/shard_map/ppermute | solution.py:346
  23.1 1.9 %collective-permute-start.4 = (bf16[2,512,512]{2,1,0:T(8,128)(2,1)S(1)}, bf16[2,512,512]{2,1,0:T(8,128)(2,1)}, u32[]{:S(2)}, u32[]{:S(2)}) collective-permute-start(bf16[2,512,512]{2,1,0:T(8,128)(2,1)S(1)} %copy-done.2), channel_id=1, source_target_pairs={{0,2},{2,0},{4,6},{6,4},{8,10},{10,8},{12,14},{14,12},{16,18},{18,... | collective-permute-start | bytes 3145736 | tf_op jit(solution)/shard_map/ppermute | solution.py:346
  25.0 2.6 %collective-permute-start.5 = (bf16[96,512]{1,0:T(8,128)(2,1)S(1)}, bf16[96,512]{1,0:T(8,128)(2,1)S(1)}, u32[]{:S(2)}, u32[]{:S(2)}) collective-permute-start(bf16[96,512]{1,0:T(8,128)(2,1)S(1)} %fusion.5.p_ref), channel_id=1, source_target_pairs={{0,16},{2,18},{4,20},{6,22},{8,24},{10,26},{12,28},{14,30},{16,0},... | collective-permute-start | bytes 294920 | tf_op jit(solution)/shard_map/ppermute | solution.py:346
  28.6 2.6 %collective-permute-start.14 = (bf16[96,512]{1,0:T(8,128)(2,1)S(1)}, bf16[96,512]{1,0:T(8,128)(2,1)S(1)}, u32[]{:S(2)}, u32[]{:S(2)}) collective-permute-start(bf16[96,512]{1,0:T(8,128)(2,1)S(1)} %fusion.2.p_ref), channel_id=1, source_target_pairs={{0,16},{2,18},{4,20},{6,22},{8,24},{10,26},{12,28},{14,30},{16,0},... | collective-permute-start | bytes 294920 | tf_op jit(solution)/shard_map/ppermute | solution.py:346
  32.5 1.5 %collective-permute-start.7 = (bf16[96,512]{1,0:T(8,128)(2,1)S(1)}, bf16[96,512]{1,0:T(8,128)(2,1)S(1)}, u32[]{:S(2)}, u32[]{:S(2)}) collective-permute-start(bf16[96,512]{1,0:T(8,128)(2,1)S(1)} %get-tuple-element.41.refs_0_), channel_id=1, source_target_pairs={{0,8},{2,10},{4,12},{6,14},{8,0},{10,2},{12,4},{14,6},{16,24},{18,... | collective-permute-start | bytes 294920 | tf_op jit(solution)/shard_map/ppermute | solution.py:346
  34.0 1.7 %collective-permute-start.8 = (bf16[96,512]{1,0:T(8,128)(2,1)S(1)}, bf16[96,512]{1,0:T(8,128)(2,1)S(1)}, u32[]{:S(2)}, u32[]{:S(2)}) collective-permute-start(bf16[96,512]{1,0:T(8,128)(2,1)S(1)} %get-tuple-element.41.refs_0_), channel_id=1, source_target_pairs={{0,12},{2,14},{4,8},{6,10},{8,4},{10,6},{12,0},{14,2},{16,28},{18,... | collective-permute-start | bytes 294920 | tf_op jit(solution)/shard_map/ppermute | solution.py:346
  36.8 1.6 %collective-permute-start.16 = (bf16[96,512]{1,0:T(8,128)(2,1)S(1)}, bf16[96,512]{1,0:T(8,128)(2,1)S(1)}, u32[]{:S(2)}, u32[]{:S(2)}) collective-permute-start(bf16[96,512]{1,0:T(8,128)(2,1)S(1)} %get-tuple-element.45.refs_5_), channel_id=1, source_target_pairs={{0,8},{2,10},{4,12},{6,14},{8,0},{10,2},{12,4},{14,6},{16,24},{18,... | collective-permute-start | bytes 294920 | tf_op jit(solution)/shard_map/ppermute | solution.py:346
  40.5 1.6 %collective-permute-start.9 = (bf16[384,512]{1,0:T(8,128)(2,1)}, bf16[384,512]{1,0:T(8,128)(2,1)S(1)}, u32[]{:S(2)}, u32[]{:S(2)}) collective-permute-start(bf16[384,512]{1,0:T(8,128)(2,1)} %pad_maximum_fusion), channel_id=1, source_target_pairs={{0,2},{2,0},{4,6},{6,4},{8,10},{10,8},{12,14},{14,12},{16,18},{18,... | collective-permute-start | bytes 1179656 | tf_op jit(solution)/shard_map/ppermute | solution.py:346
  42.1 2.0 %collective-permute-done.17.refs_8_ = bf16[96,512]{1,0:T(8,128)(2,1)S(1)} collective-permute-done((bf16[96,512]{1,0:T(8,128)(2,1)S(1)}, bf16[96,512]{1,0:T(8,128)(2,1)S(1)}, u32[]{:S(2)}, u32[]{:S(2)}) %collective-permute-start.17) | collective-permute-done | bytes 98336 | tf_op jit(solution)/shard_map/ppermute | solution.py:346
  46.1 2.3 %collective-permute-done.9.refs_4_ = bf16[384,512]{1,0:T(8,128)(2,1)S(1)} collective-permute-done((bf16[384,512]{1,0:T(8,128)(2,1)}, bf16[384,512]{1,0:T(8,128)(2,1)S(1)}, u32[]{:S(2)}, u32[]{:S(2)}) %collective-permute-start.9) | collective-permute-done | bytes 393248 | tf_op jit(solution)/shard_map/ppermute | solution.py:346
  48.5 4.4 %collective-permute-done.18.refs_9_ = bf16[384,512]{1,0:T(8,128)(2,1)S(1)} collective-permute-done((bf16[384,512]{1,0:T(8,128)(2,1)}, bf16[384,512]{1,0:T(8,128)(2,1)S(1)}, u32[]{:S(2)}, u32[]{:S(2)}) %collective-permute-start.18) | collective-permute-done | bytes 393248 | tf_op jit(solution)/shard_map/ppermute | solution.py:346
  52.8 4.7 %next_grads.1 = (bf16[96,512]{1,0:T(8,128)(2,1)S(1)}, bf16[96,512]{1,0:T(8,128)(2,1)S(1)}, bf16[96,512]{1,0:T(8,128)(2,1)S(1)}, bf16[96,512]{1,0:T(8,128)(2,1)S(...) custom-call(s32[1]{0:T(128)} %bitcast.me_ref, ...), custom_call_target="tpu_custom_call" | custom-call | tf_op jit(solution)/shard_map/next_grads/pallas_call | solution.py:171
  57.5 1.6 %collective-permute-start.27 = (bf16[96,512]{1,0:T(8,128)(2,1)S(1)}, bf16[96,512]{1,0:T(8,128)(2,1)S(1)}, u32[]{:S(2)}, u32[]{:S(2)}) collective-permute-start(bf16[96,512]{1,0:T(8,128)(2,1)S(1)} %get-tuple-element.58), channel_id=1, source_target_pairs={{0,12},{2,14},{4,8},{6,10},{8,4},{10,6},{12,0},{14,2},{16,28},{18,... | collective-permute-start | bytes 294920 | tf_op jit(solution)/shard_map/ppermute | solution.py:346
  61.4 1.6 %collective-permute-start.21 = (bf16[96,512]{1,0:T(8,128)(2,1)S(1)}, bf16[96,512]{1,0:T(8,128)(2,1)S(1)}, u32[]{:S(2)}, u32[]{:S(2)}) collective-permute-start(bf16[96,512]{1,0:T(8,128)(2,1)S(1)} %get-tuple-element.49), channel_id=1, source_target_pairs={{0,12},{2,14},{4,8},{6,10},{8,4},{10,6},{12,0},{14,2},{16,28},{18,... | collective-permute-start | bytes 294920 | tf_op jit(solution)/shard_map/ppermute | solution.py:346
  63.1 1.3 %collective-permute-start.20 = (bf16[96,512]{1,0:T(8,128)(2,1)S(1)}, bf16[96,512]{1,0:T(8,128)(2,1)S(1)}, u32[]{:S(2)}, u32[]{:S(2)}) collective-permute-start(bf16[96,512]{1,0:T(8,128)(2,1)S(1)} %get-tuple-element.48), channel_id=1, source_target_pairs={{0,8},{2,10},{4,12},{6,14},{8,0},{10,2},{12,4},{14,6},{16,24},{18,... | collective-permute-start | bytes 294920 | tf_op jit(solution)/shard_map/ppermute | solution.py:346
  65.2 3.2 %collective-permute-start.28 = (bf16[96,512]{1,0:T(8,128)(2,1)S(1)}, bf16[96,512]{1,0:T(8,128)(2,1)S(1)}, u32[]{:S(2)}, u32[]{:S(2)}) collective-permute-start(bf16[96,512]{1,0:T(8,128)(2,1)S(1)} %add_convert_fusion.p_ref), channel_id=1, source_target_pairs={{0,16},{2,18},{4,20},{6,22},{8,24},{10,26},{12,28},{14,30},{16,0},... | collective-permute-start | bytes 294920 | tf_op jit(solution)/shard_map/ppermute | solution.py:346
  68.4 3.4 %collective-permute-done.20 = bf16[96,512]{1,0:T(8,128)(2,1)S(1)} collective-permute-done((bf16[96,512]{1,0:T(8,128)(2,1)S(1)}, bf16[96,512]{1,0:T(8,128)(2,1)S(1)}, u32[]{:S(2)}, u32[]{:S(2)}) %collective-permute-start.20) | collective-permute-done | bytes 98336 | tf_op jit(solution)/shard_map/ppermute | solution.py:346
  74.3 1.8 %collective-permute-start.30 = (bf16[96,512]{1,0:T(8,128)(2,1)S(1)}, bf16[96,512]{1,0:T(8,128)(2,1)S(1)}, u32[]{:S(2)}, u32[]{:S(2)}) collective-permute-start(bf16[96,512]{1,0:T(8,128)(2,1)S(1)} %update.7.refs_0_), channel_id=1, source_target_pairs={{0,8},{2,10},{4,12},{6,14},{8,0},{10,2},{12,4},{14,6},{16,24},{18,... | collective-permute-start | bytes 294920 | tf_op jit(solution)/shard_map/ppermute | solution.py:346
  76.8 2.2 %collective-permute-done.22.q_ref = bf16[96,512]{1,0:T(8,128)(2,1)S(1)} collective-permute-done((bf16[96,512]{1,0:T(8,128)(2,1)S(1)}, bf16[96,512]{1,0:T(8,128)(2,1)S(1)}, u32[]{:S(2)}, u32[]{:S(2)}) %collective-permute-start.22) | collective-permute-done | bytes 98336 | tf_op jit(solution)/shard_map/ppermute | solution.py:346
  81.4 2.5 %collective-permute-start.35 = (bf16[96,512]{1,0:T(8,128)(2,1)S(1)}, bf16[96,512]{1,0:T(8,128)(2,1)S(1)}, u32[]{:S(2)}, u32[]{:S(2)}) collective-permute-start(bf16[96,512]{1,0:T(8,128)(2,1)S(1)} %update.6.refs_5_), channel_id=1, source_target_pairs={{0,12},{2,14},{4,8},{6,10},{8,4},{10,6},{12,0},{14,2},{16,28},{18,... | collective-permute-start | bytes 294920 | tf_op jit(solution)/shard_map/ppermute | solution.py:346
  84.6 1.7 %collective-permute-done.34.refs_7_ = bf16[96,512]{1,0:T(8,128)(2,1)S(1)} collective-permute-done((bf16[96,512]{1,0:T(8,128)(2,1)S(1)}, bf16[96,512]{1,0:T(8,128)(2,1)S(1)}, u32[]{:S(2)}, u32[]{:S(2)}) %collective-permute-start.34) | collective-permute-done | bytes 98336 | tf_op jit(solution)/shard_map/ppermute | solution.py:346
  86.3 1.5 %collective-permute-done.35.refs_8_ = bf16[96,512]{1,0:T(8,128)(2,1)S(1)} collective-permute-done((bf16[96,512]{1,0:T(8,128)(2,1)S(1)}, bf16[96,512]{1,0:T(8,128)(2,1)S(1)}, u32[]{:S(2)}, u32[]{:S(2)}) %collective-permute-start.35) | collective-permute-done | bytes 98336 | tf_op jit(solution)/shard_map/ppermute | solution.py:346
  87.8 1.6 %collective-permute-start.36 = (bf16[384,512]{1,0:T(8,128)(2,1)S(1)}, bf16[384,512]{1,0:T(8,128)(2,1)S(1)}, u32[]{:S(2)}, u32[]{:S(2)}) collective-permute-start(bf16[384,512]{1,0:T(8,128)(2,1)S(1)} %pad_maximum_fusion.3), channel_id=1, source_target_pairs={{0,2},{2,0},{4,6},{6,4},{8,10},{10,8},{12,14},{14,12},{16,18},{18,... | collective-permute-start | bytes 1179656 | tf_op jit(solution)/shard_map/ppermute | solution.py:346
  90.2 1.5 %project.2.refs_0_ = bf16[2,512,1024]{2,1,0:T(8,128)(2,1)} custom-call(f32[512,1024]{1,0:T(8,128)S(1)} %project_own.2.sum_ref, bf16[512,512]{1,0:T(8,128)(2,1)S(1)} %collective-permute-done.23.o_ref, bf16[512,1024]{1,0:T(8,128)(2,1)S(1)} %collective-permute-done.24.proj_ref), custom_call_target="tpu_custom_call" | custom-call | tf_op jit(solution)/shard_map/project/pallas_call | solution.py:310
  91.8 4.2 %collective-permute-done.36.refs_9_ = bf16[384,512]{1,0:T(8,128)(2,1)S(1)} collective-permute-done((bf16[384,512]{1,0:T(8,128)(2,1)S(1)}, bf16[384,512]{1,0:T(8,128)(2,1)S(1)}, u32[]{:S(2)}, u32[]{:S(2)}) %collective-permute-start.36) | collective-permute-done | bytes 393248 | tf_op jit(solution)/shard_map/ppermute | solution.py:346
  99.1 1.5 %project.3 = bf16[2,512,1024]{2,1,0:T(8,128)(2,1)} custom-call(f32[512,1024]{1,0:T(8,128)S(1)} %project_own.3.sum_ref, bf16[512,512]{1,0:T(8,128)(2,1)S(1)} %collective-permute-done.37.o_ref, bf16[512,1024]{1,0:T(8,128)(2,1)S(1)} %collective-permute-done.24.proj_ref, bf16[2,512,1024]{2,1,0:T(8,128)(2,1)} %project.2.refs_0_), custom_call_target="tpu_custom_call", output_to_operand_aliasing={{}: (3, {})} | custom-call | tf_op jit(solution)/shard_map/project/pallas_call | solution.py:310
  (78 shorter events, 22.8 us)
Async XLA Ops:
  4.0 8.8 %collective-permute-start = (bf16[384,512]{1,0:T(8,128)(2,1)S(1)}, bf16[384,512]{1,0:T(8,128)(2,1)S(1)}, u32[]{:S(2)}, u32[]{:S(2)}) collective-permute-start(bf16[384,512]{1,0:T(8,128)(2,1)S(1)} %get-tuple-element.34), channel_id=1, source_target_pairs={{0,2},{2,0},{4,6},{6,4},{8,10},{10,8},{12,14},{14,12},{16,18},{18,... | collective-permute-start | bytes 1179656 | tf_op jit(solution)/shard_map/ppermute | solution.py:346
  7.0 11.6 %collective-permute-start.10 = (bf16[384,512]{1,0:T(8,128)(2,1)S(1)}, bf16[384,512]{1,0:T(8,128)(2,1)S(1)}, u32[]{:S(2)}, u32[]{:S(2)}) collective-permute-start(bf16[384,512]{1,0:T(8,128)(2,1)S(1)} %get-tuple-element.43), channel_id=1, source_target_pairs={{0,2},{2,0},{4,6},{6,4},{8,10},{10,8},{12,14},{14,12},{16,18},{18,... | collective-permute-start | bytes 1179656 | tf_op jit(solution)/shard_map/ppermute | solution.py:346
  12.9 9.8 %collective-permute-start.3 = (bf16[96,512]{1,0:T(8,128)(2,1)S(1)}, bf16[96,512]{1,0:T(8,128)(2,1)S(1)}, u32[]{:S(2)}, u32[]{:S(2)}) collective-permute-start(bf16[96,512]{1,0:T(8,128)(2,1)S(1)} %get-tuple-element.73), channel_id=1, source_target_pairs={{0,12},{2,14},{4,8},{6,10},{8,4},{10,6},{12,0},{14,2},{16,28},{18,... | collective-permute-start | bytes 294920 | tf_op jit(solution)/shard_map/ppermute | solution.py:346
  16.1 6.9 %collective-permute-start.2 = (bf16[96,512]{1,0:T(8,128)(2,1)S(1)}, bf16[96,512]{1,0:T(8,128)(2,1)S(1)}, u32[]{:S(2)}, u32[]{:S(2)}) collective-permute-start(bf16[96,512]{1,0:T(8,128)(2,1)S(1)} %get-tuple-element.74), channel_id=1, source_target_pairs={{0,8},{2,10},{4,12},{6,14},{8,0},{10,2},{12,4},{14,6},{16,24},{18,... | collective-permute-start | bytes 294920 | tf_op jit(solution)/shard_map/ppermute | solution.py:346
  16.5 6.5 %collective-permute-start.1 = (bf16[96,512]{1,0:T(8,128)(2,1)S(1)}, bf16[96,512]{1,0:T(8,128)(2,1)S(1)}, u32[]{:S(2)}, u32[]{:S(2)}) collective-permute-start(bf16[96,512]{1,0:T(8,128)(2,1)S(1)} %get-tuple-element.72), channel_id=1, source_target_pairs={{0,4},{2,6},{4,0},{6,2},{8,12},{10,14},{12,8},{14,10},{16,20},{18,... | collective-permute-start | bytes 294920 | tf_op jit(solution)/shard_map/ppermute | solution.py:346
  18.8 8.8 %collective-permute-start.13 = (bf16[96,512]{1,0:T(8,128)(2,1)S(1)}, bf16[96,512]{1,0:T(8,128)(2,1)S(1)}, u32[]{:S(2)}, u32[]{:S(2)}) collective-permute-start(bf16[96,512]{1,0:T(8,128)(2,1)S(1)} %get-tuple-element.70), channel_id=1, source_target_pairs={{0,12},{2,14},{4,8},{6,10},{8,4},{10,6},{12,0},{14,2},{16,28},{18,... | collective-permute-start | bytes 294920 | tf_op jit(solution)/shard_map/ppermute | solution.py:346
  22.3 6.2 %collective-permute-start.12 = (bf16[96,512]{1,0:T(8,128)(2,1)S(1)}, bf16[96,512]{1,0:T(8,128)(2,1)S(1)}, u32[]{:S(2)}, u32[]{:S(2)}) collective-permute-start(bf16[96,512]{1,0:T(8,128)(2,1)S(1)} %get-tuple-element.71), channel_id=1, source_target_pairs={{0,8},{2,10},{4,12},{6,14},{8,0},{10,2},{12,4},{14,6},{16,24},{18,... | collective-permute-start | bytes 294920 | tf_op jit(solution)/shard_map/ppermute | solution.py:346
  22.8 5.8 %collective-permute-start.11 = (bf16[96,512]{1,0:T(8,128)(2,1)S(1)}, bf16[96,512]{1,0:T(8,128)(2,1)S(1)}, u32[]{:S(2)}, u32[]{:S(2)}) collective-permute-start(bf16[96,512]{1,0:T(8,128)(2,1)S(1)} %get-tuple-element.69), channel_id=1, source_target_pairs={{0,4},{2,6},{4,0},{6,2},{8,12},{10,14},{12,8},{14,10},{16,20},{18,... | collective-permute-start | bytes 294920 | tf_op jit(solution)/shard_map/ppermute | solution.py:346
  23.1 29.8 %collective-permute-start.4 = (bf16[2,512,512]{2,1,0:T(8,128)(2,1)S(1)}, bf16[2,512,512]{2,1,0:T(8,128)(2,1)}, u32[]{:S(2)}, u32[]{:S(2)}) collective-permute-start(bf16[2,512,512]{2,1,0:T(8,128)(2,1)S(1)} %copy-done.2), channel_id=1, source_target_pairs={{0,2},{2,0},{4,6},{6,4},{8,10},{10,8},{12,14},{14,12},{16,18},{18,... | collective-permute-start | bytes 3145736 | tf_op jit(solution)/shard_map/ppermute | solution.py:346
  25.0 7.0 %collective-permute-start.5 = (bf16[96,512]{1,0:T(8,128)(2,1)S(1)}, bf16[96,512]{1,0:T(8,128)(2,1)S(1)}, u32[]{:S(2)}, u32[]{:S(2)}) collective-permute-start(bf16[96,512]{1,0:T(8,128)(2,1)S(1)} %fusion.5.p_ref), channel_id=1, source_target_pairs={{0,16},{2,18},{4,20},{6,22},{8,24},{10,26},{12,28},{14,30},{16,0},... | collective-permute-start | bytes 294920 | tf_op jit(solution)/shard_map/ppermute | solution.py:346
  28.6 7.2 %collective-permute-start.14 = (bf16[96,512]{1,0:T(8,128)(2,1)S(1)}, bf16[96,512]{1,0:T(8,128)(2,1)S(1)}, u32[]{:S(2)}, u32[]{:S(2)}) collective-permute-start(bf16[96,512]{1,0:T(8,128)(2,1)S(1)} %fusion.2.p_ref), channel_id=1, source_target_pairs={{0,16},{2,18},{4,20},{6,22},{8,24},{10,26},{12,28},{14,30},{16,0},... | collective-permute-start | bytes 294920 | tf_op jit(solution)/shard_map/ppermute | solution.py:346
  32.5 5.9 %collective-permute-start.7 = (bf16[96,512]{1,0:T(8,128)(2,1)S(1)}, bf16[96,512]{1,0:T(8,128)(2,1)S(1)}, u32[]{:S(2)}, u32[]{:S(2)}) collective-permute-start(bf16[96,512]{1,0:T(8,128)(2,1)S(1)} %get-tuple-element.41.refs_0_), channel_id=1, source_target_pairs={{0,8},{2,10},{4,12},{6,14},{8,0},{10,2},{12,4},{14,6},{16,24},{18,... | collective-permute-start | bytes 294920 | tf_op jit(solution)/shard_map/ppermute | solution.py:346
  34.0 5.7 %collective-permute-start.8 = (bf16[96,512]{1,0:T(8,128)(2,1)S(1)}, bf16[96,512]{1,0:T(8,128)(2,1)S(1)}, u32[]{:S(2)}, u32[]{:S(2)}) collective-permute-start(bf16[96,512]{1,0:T(8,128)(2,1)S(1)} %get-tuple-element.41.refs_0_), channel_id=1, source_target_pairs={{0,12},{2,14},{4,8},{6,10},{8,4},{10,6},{12,0},{14,2},{16,28},{18,... | collective-permute-start | bytes 294920 | tf_op jit(solution)/shard_map/ppermute | solution.py:346
  36.0 6.1 %collective-permute-start.15 = (bf16[96,512]{1,0:T(8,128)(2,1)S(1)}, bf16[96,512]{1,0:T(8,128)(2,1)S(1)}, u32[]{:S(2)}, u32[]{:S(2)}) collective-permute-start(bf16[96,512]{1,0:T(8,128)(2,1)S(1)} %get-tuple-element.45.refs_5_), channel_id=1, source_target_pairs={{0,4},{2,6},{4,0},{6,2},{8,12},{10,14},{12,8},{14,10},{16,20},{18,... | collective-permute-start | bytes 294920 | tf_op jit(solution)/shard_map/ppermute | solution.py:346
  38.4 5.6 %collective-permute-start.17 = (bf16[96,512]{1,0:T(8,128)(2,1)S(1)}, bf16[96,512]{1,0:T(8,128)(2,1)S(1)}, u32[]{:S(2)}, u32[]{:S(2)}) collective-permute-start(bf16[96,512]{1,0:T(8,128)(2,1)S(1)} %get-tuple-element.45.refs_5_), channel_id=1, source_target_pairs={{0,12},{2,14},{4,8},{6,10},{8,4},{10,6},{12,0},{14,2},{16,28},{18,... | collective-permute-start | bytes 294920 | tf_op jit(solution)/shard_map/ppermute | solution.py:346
  40.5 8.0 %collective-permute-start.9 = (bf16[384,512]{1,0:T(8,128)(2,1)}, bf16[384,512]{1,0:T(8,128)(2,1)S(1)}, u32[]{:S(2)}, u32[]{:S(2)}) collective-permute-start(bf16[384,512]{1,0:T(8,128)(2,1)} %pad_maximum_fusion), channel_id=1, source_target_pairs={{0,2},{2,0},{4,6},{6,4},{8,10},{10,8},{12,14},{14,12},{16,18},{18,... | collective-permute-start | bytes 1179656 | tf_op jit(solution)/shard_map/ppermute | solution.py:346
  44.8 8.0 %collective-permute-start.18 = (bf16[384,512]{1,0:T(8,128)(2,1)}, bf16[384,512]{1,0:T(8,128)(2,1)S(1)}, u32[]{:S(2)}, u32[]{:S(2)}) collective-permute-start(bf16[384,512]{1,0:T(8,128)(2,1)} %pad_maximum_fusion.1), channel_id=1, source_target_pairs={{0,2},{2,0},{4,6},{6,4},{8,10},{10,8},{12,14},{14,12},{16,18},{18,... | collective-permute-start | bytes 1179656 | tf_op jit(solution)/shard_map/ppermute | solution.py:346
  57.5 5.6 %collective-permute-start.27 = (bf16[96,512]{1,0:T(8,128)(2,1)S(1)}, bf16[96,512]{1,0:T(8,128)(2,1)S(1)}, u32[]{:S(2)}, u32[]{:S(2)}) collective-permute-start(bf16[96,512]{1,0:T(8,128)(2,1)S(1)} %get-tuple-element.58), channel_id=1, source_target_pairs={{0,12},{2,14},{4,8},{6,10},{8,4},{10,6},{12,0},{14,2},{16,28},{18,... | collective-permute-start | bytes 294920 | tf_op jit(solution)/shard_map/ppermute | solution.py:346
  59.1 5.3 %collective-permute-start.26 = (bf16[96,512]{1,0:T(8,128)(2,1)S(1)}, bf16[96,512]{1,0:T(8,128)(2,1)S(1)}, u32[]{:S(2)}, u32[]{:S(2)}) collective-permute-start(bf16[96,512]{1,0:T(8,128)(2,1)S(1)} %get-tuple-element.57), channel_id=1, source_target_pairs={{0,8},{2,10},{4,12},{6,14},{8,0},{10,2},{12,4},{14,6},{16,24},{18,... | collective-permute-start | bytes 294920 | tf_op jit(solution)/shard_map/ppermute | solution.py:346
  61.3 28.9 %collective-permute-start.24 = (bf16[512,1024]{1,0:T(8,128)(2,1)S(1)}, bf16[512,1024]{1,0:T(8,128)(2,1)S(1)}, u32[]{:S(2)}, u32[]{:S(2)}) collective-permute-start(bf16[512,1024]{1,0:T(8,128)(2,1)S(1)} %get-tuple-element.63), channel_id=1, source_target_pairs={{0,1},{1,0},{2,3},{3,2},{4,5},{5,4},{6,7},{7,6},{8,9},{9,8},{10,11... | collective-permute-start | bytes 3145736 | tf_op jit(solution)/shard_map/ppermute | solution.py:349
  61.4 7.0 %collective-permute-start.21 = (bf16[96,512]{1,0:T(8,128)(2,1)S(1)}, bf16[96,512]{1,0:T(8,128)(2,1)S(1)}, u32[]{:S(2)}, u32[]{:S(2)}) collective-permute-start(bf16[96,512]{1,0:T(8,128)(2,1)S(1)} %get-tuple-element.49), channel_id=1, source_target_pairs={{0,12},{2,14},{4,8},{6,10},{8,4},{10,6},{12,0},{14,2},{16,28},{18,... | collective-permute-start | bytes 294920 | tf_op jit(solution)/shard_map/ppermute | solution.py:346
  63.1 8.7 %collective-permute-start.20 = (bf16[96,512]{1,0:T(8,128)(2,1)S(1)}, bf16[96,512]{1,0:T(8,128)(2,1)S(1)}, u32[]{:S(2)}, u32[]{:S(2)}) collective-permute-start(bf16[96,512]{1,0:T(8,128)(2,1)S(1)} %get-tuple-element.48), channel_id=1, source_target_pairs={{0,8},{2,10},{4,12},{6,14},{8,0},{10,2},{12,4},{14,6},{16,24},{18,... | collective-permute-start | bytes 294920 | tf_op jit(solution)/shard_map/ppermute | solution.py:346
  64.4 7.3 %collective-permute-start.19 = (bf16[96,512]{1,0:T(8,128)(2,1)S(1)}, bf16[96,512]{1,0:T(8,128)(2,1)S(1)}, u32[]{:S(2)}, u32[]{:S(2)}) collective-permute-start(bf16[96,512]{1,0:T(8,128)(2,1)S(1)} %get-tuple-element.47), channel_id=1, source_target_pairs={{0,4},{2,6},{4,0},{6,2},{8,12},{10,14},{12,8},{14,10},{16,20},{18,... | collective-permute-start | bytes 294920 | tf_op jit(solution)/shard_map/ppermute | solution.py:346
  65.2 7.8 %collective-permute-start.28 = (bf16[96,512]{1,0:T(8,128)(2,1)S(1)}, bf16[96,512]{1,0:T(8,128)(2,1)S(1)}, u32[]{:S(2)}, u32[]{:S(2)}) collective-permute-start(bf16[96,512]{1,0:T(8,128)(2,1)S(1)} %add_convert_fusion.p_ref), channel_id=1, source_target_pairs={{0,16},{2,18},{4,20},{6,22},{8,24},{10,26},{12,28},{14,30},{16,0},... | collective-permute-start | bytes 294920 | tf_op jit(solution)/shard_map/ppermute | solution.py:346
  71.8 7.2 %collective-permute-start.22 = (bf16[96,512]{1,0:T(8,128)(2,1)S(1)}, bf16[96,512]{1,0:T(8,128)(2,1)S(1)}, u32[]{:S(2)}, u32[]{:S(2)}) collective-permute-start(bf16[96,512]{1,0:T(8,128)(2,1)S(1)} %add_convert_fusion.1.p_ref), channel_id=1, source_target_pairs={{0,16},{2,18},{4,20},{6,22},{8,24},{10,26},{12,28},{14,30},{16,0},... | collective-permute-start | bytes 294920 | tf_op jit(solution)/shard_map/ppermute | solution.py:346
  73.2 8.0 %collective-permute-start.29 = (bf16[96,512]{1,0:T(8,128)(2,1)S(1)}, bf16[96,512]{1,0:T(8,128)(2,1)S(1)}, u32[]{:S(2)}, u32[]{:S(2)}) collective-permute-start(bf16[96,512]{1,0:T(8,128)(2,1)S(1)} %update.7.refs_0_), channel_id=1, source_target_pairs={{0,4},{2,6},{4,0},{6,2},{8,12},{10,14},{12,8},{14,10},{16,20},{18,... | collective-permute-start | bytes 294920 | tf_op jit(solution)/shard_map/ppermute | solution.py:346
  74.3 7.0 %collective-permute-start.30 = (bf16[96,512]{1,0:T(8,128)(2,1)S(1)}, bf16[96,512]{1,0:T(8,128)(2,1)S(1)}, u32[]{:S(2)}, u32[]{:S(2)}) collective-permute-start(bf16[96,512]{1,0:T(8,128)(2,1)S(1)} %update.7.refs_0_), channel_id=1, source_target_pairs={{0,8},{2,10},{4,12},{6,14},{8,0},{10,2},{12,4},{14,6},{16,24},{18,... | collective-permute-start | bytes 294920 | tf_op jit(solution)/shard_map/ppermute | solution.py:346
  76.1 7.7 %collective-permute-start.31 = (bf16[96,512]{1,0:T(8,128)(2,1)S(1)}, bf16[96,512]{1,0:T(8,128)(2,1)S(1)}, u32[]{:S(2)}, u32[]{:S(2)}) collective-permute-start(bf16[96,512]{1,0:T(8,128)(2,1)S(1)} %update.7.refs_0_), channel_id=1, source_target_pairs={{0,12},{2,14},{4,8},{6,10},{8,4},{10,6},{12,0},{14,2},{16,28},{18,... | collective-permute-start | bytes 294920 | tf_op jit(solution)/shard_map/ppermute | solution.py:346
  81.4 6.4 %collective-permute-start.35 = (bf16[96,512]{1,0:T(8,128)(2,1)S(1)}, bf16[96,512]{1,0:T(8,128)(2,1)S(1)}, u32[]{:S(2)}, u32[]{:S(2)}) collective-permute-start(bf16[96,512]{1,0:T(8,128)(2,1)S(1)} %update.6.refs_5_), channel_id=1, source_target_pairs={{0,12},{2,14},{4,8},{6,10},{8,4},{10,6},{12,0},{14,2},{16,28},{18,... | collective-permute-start | bytes 294920 | tf_op jit(solution)/shard_map/ppermute | solution.py:346
  83.8 6.4 %collective-permute-start.23 = (bf16[512,512]{1,0:T(8,128)(2,1)S(1)}, bf16[512,512]{1,0:T(8,128)(2,1)S(1)}, u32[]{:S(2)}, u32[]{:S(2)}) collective-permute-start(bf16[512,512]{1,0:T(8,128)(2,1)S(1)} %apply.2.o_ref), channel_id=1, source_target_pairs={{0,1},{1,0},{2,3},{3,2},{4,5},{5,4},{6,7},{7,6},{8,9},{9,8},{10,11... | collective-permute-start | bytes 1572872 | tf_op jit(solution)/shard_map/ppermute | solution.py:349
  83.9 7.9 %collective-permute-start.32 = (bf16[384,512]{1,0:T(8,128)(2,1)S(1)}, bf16[384,512]{1,0:T(8,128)(2,1)S(1)}, u32[]{:S(2)}, u32[]{:S(2)}) collective-permute-start(bf16[384,512]{1,0:T(8,128)(2,1)S(1)} %pad_maximum_fusion.2), channel_id=1, source_target_pairs={{0,2},{2,0},{4,6},{6,4},{8,10},{10,8},{12,14},{14,12},{16,18},{18,... | collective-permute-start | bytes 1179656 | tf_op jit(solution)/shard_map/ppermute | solution.py:346
  87.8 8.2 %collective-permute-start.36 = (bf16[384,512]{1,0:T(8,128)(2,1)S(1)}, bf16[384,512]{1,0:T(8,128)(2,1)S(1)}, u32[]{:S(2)}, u32[]{:S(2)}) collective-permute-start(bf16[384,512]{1,0:T(8,128)(2,1)S(1)} %pad_maximum_fusion.3), channel_id=1, source_target_pairs={{0,2},{2,0},{4,6},{6,4},{8,10},{10,8},{12,14},{14,12},{16,18},{18,... | collective-permute-start | bytes 1179656 | tf_op jit(solution)/shard_map/ppermute | solution.py:346
  (10 other events, 89.7 us)

commit v6 on v5

--- a/solution.py
+++ b/solution.py
@@ -131,7 +131,7 @@
     w_refs, out_refs, w_out = refs[:n_w], refs[n_w : n_w + 4 * CHUNKS], refs[n_w + 4 * CHUNKS]
     tok_s, da_s, db_s, hid_s, g_s, w, sems = refs[n_w + 4 * CHUNKS + 1 :]
     loads = [
-        [pltpu.make_async_copy(ref.at[j], tok_s.at[i, j], sems.at[2 * i + j]) for j in range(2)]
+        [pltpu.make_async_copy(ref.at[j], tok_s.at[j, pl.ds(i * own_hbm.shape[1], own_hbm.shape[1])], sems.at[2 * i + j]) for j in range(2)]
         for i, ref in enumerate((own_hbm, other_hbm))
     ]
     for pair in loads:
@@ -140,7 +140,7 @@
     me = me_ref[0]
     assemble(me, w_refs, w)
     keep_w = pltpu.make_async_copy(w, w_out, sems.at[4])
-    tok, width = tok_s.shape[2:]
+    tok, width = own_hbm.shape[1:]
     half = width // 2
     for i, pair in enumerate(loads):
 
@@ -148,14 +148,13 @@
             if name != "linear":
                 pair[name == "output"].wait()
 
-        token_grads(tok_s.at[i, 0], tok_s.at[i, 1], w, da_s, db_s, hid_s, i * tok, ready)
+        token_grads(tok_s.at[0, pl.ds(i * tok, tok)], tok_s.at[1, pl.ds(i * tok, tok)], w, da_s, db_s, hid_s, i * tok, ready)
     keep_w.start()
     mine = pl.ds(pl.multiple_of((me % 2) * half, half), half)
     over_tokens = ((0,), (0,))
-    spans = ((0, slice(0, tok)), (1, slice(tok, 2 * tok)))
-    for m, d_s in ((0, da_s), (1, db_s)):
-        g_s[m] = sum(dot(tok_s[i, 0, :, mine], d_s[span, :], over_tokens) for i, span in spans).astype(bf16)
-    g_s[2] = sum(dot(hid_s[span, mine], tok_s[i, 1], over_tokens) for i, span in spans).astype(bf16)
+    g_s[0] = dot(tok_s[0, :, mine], da_s[...], over_tokens).astype(bf16)
+    g_s[1] = dot(tok_s[0, :, mine], db_s[...], over_tokens).astype(bf16)
+    g_s[2] = dot(hid_s[:, mine], tok_s[1], over_tokens).astype(bf16)
     rows = width // SHARDS // CHUNKS
     for h in range(CHUNKS):
         for i, r in enumerate((0, 2, 4, 6)):
@@ -173,7 +172,7 @@
         out_shape=[jax.ShapeDtypeStruct((rows, width), bf16)] * (4 * CHUNKS) + [pltpu.HBM((3, width, width), bf16)],
         in_specs=[SMEM, HBM, HBM] + [VMEM] * len(w),
         out_specs=[VMEM] * (4 * CHUNKS) + [HBM],
-        scratch_shapes=[pltpu.VMEM((2, 2, tok, width), bf16)]
+        scratch_shapes=[pltpu.VMEM((2, 2 * tok, width), bf16)]
         + [pltpu.VMEM((2 * tok, width), bf16)] * 3
         + [pltpu.VMEM((3, width // 2, width), bf16), pltpu.VMEM((3, width, width), bf16), pltpu.SemaphoreType.DMA((5,))],
         compiler_params=params(),

time: 101 us -> 101 us (level)
  no operation moved by 1% of the time
where the time goes in v6:
time: 101 us
  starting transfers between devices  49 us (49%)
  waiting for transfers between devices  30.8 us (30%)
  Pallas kernels  18.3 us (18%)
  other arithmetic  2.05 us (2%)
    ppermute x35, starting transfers between devices, swap(): return lax.ppermute(x, ('ctx', 'head'), pairs)  48.8 us
    ppermute x35, waiting for transfers between devices, swap(): return lax.ppermute(x, ('ctx', 'head'), pairs)  29.6 us
    pallas_call x1, Pallas kernels, next_grads(): pl.pallas_call(functools.partial(next_grads_kernel, len(w)), out_shape=[j...  4.62 us
    pallas_call x1, Pallas kernels, first_grads(): pl.pallas_call(first_grads_kernel, out_shape=[jax.ShapeDtypeStruct((rows,...  3.99 us
    pallas_call x2, Pallas kernels, project(): pl.pallas_call(functools.partial(project_kernel, block), out_shape=jax.Sh...  2.93 us
    pallas_call x1, Pallas kernels, next_tokens(): pl.pallas_call(tokens_kernel, out_shape=pltpu.HBM((2, tok, width), bf16),...  2.34 us
    pallas_call x2, Pallas kernels, fast_apply(): pl.pallas_call(functools.partial(apply_kernel, len(w)), grid=(1,), out_sh...  2.09 us
  transfers between devices with their start and end apart: 38, of which 16 were waited for; matrix products, arithmetic and copies ran while one was open for 2% of the time, Pallas kernels for 7%

profile of v6, /device:TPU:0, one launch (start us, length us, event | category | flops | bytes accessed | tf_op | source)
XLA Modules:
  0.0 100.6 jit_solution(7726155145358478963)
XLA Ops:
  0.0 4.0 %first_grads.1 = (bf16[384,512]{1,0:T(8,128)(2,1)S(1)}, bf16[384,512]{1,0:T(8,128)(2,1)S(1)}, bf16[384,512]{1,0:T(8,128)(2,1)S(1)}, bf16[384,512]{1,0:T(8,128)(2...) custom-call(s32[1]{0:T(128)} %bitcast.me_ref, bf16[2,512,512]{2,1,0:T(8,128)(2,1)} %bitcast.12, ...), custom_call_target="tpu_custom_call" | custom-call | tf_op jit(solution)/shard_map/first_grads/pallas_call | solution.py:118
  4.0 3.0 %collective-permute-start = (bf16[384,512]{1,0:T(8,128)(2,1)S(1)}, bf16[384,512]{1,0:T(8,128)(2,1)S(1)}, u32[]{:S(2)}, u32[]{:S(2)}) collective-permute-start(bf16[384,512]{1,0:T(8,128)(2,1)S(1)} %get-tuple-element.34), channel_id=1, source_target_pairs={{0,2},{2,0},{4,6},{6,4},{8,10},{10,8},{12,14},{14,12},{16,18},{18,... | collective-permute-start | bytes 1179656 | tf_op jit(solution)/shard_map/ppermute | solution.py:345
  7.1 2.3 %next_tokens.1.own_hbm = bf16[2,512,512]{2,1,0:T(8,128)(2,1)} custom-call(bf16[2,512,512]{2,1,0:T(8,128)(2,1)} %bitcast.13, bf16[2,512,512]{2,1,0:T(8,128)(2,1)} %bitcast.15, f32[2,1,512]{2,1,0:T(1,128)} %bitcast.18), custom_call_target="tpu_custom_call" | custom-call | tf_op jit(solution)/shard_map/next_tokens/pallas_call | solution.py:203
  9.4 3.3 %collective-permute-done = bf16[384,512]{1,0:T(8,128)(2,1)S(1)} collective-permute-done((bf16[384,512]{1,0:T(8,128)(2,1)S(1)}, bf16[384,512]{1,0:T(8,128)(2,1)S(1)}, u32[]{:S(2)}, u32[]{:S(2)}) %collective-permute-start) | collective-permute-done | bytes 393248 | tf_op jit(solution)/shard_map/ppermute | solution.py:345
  12.9 3.1 %collective-permute-start.3 = (bf16[96,512]{1,0:T(8,128)(2,1)S(1)}, bf16[96,512]{1,0:T(8,128)(2,1)S(1)}, u32[]{:S(2)}, u32[]{:S(2)}) collective-permute-start(bf16[96,512]{1,0:T(8,128)(2,1)S(1)} %get-tuple-element.73), channel_id=1, source_target_pairs={{0,12},{2,14},{4,8},{6,10},{8,4},{10,6},{12,0},{14,2},{16,28},{18,... | collective-permute-start | bytes 294920 | tf_op jit(solution)/shard_map/ppermute | solution.py:345
  16.7 1.9 %collective-permute-done.10 = bf16[384,512]{1,0:T(8,128)(2,1)S(1)} collective-permute-done((bf16[384,512]{1,0:T(8,128)(2,1)S(1)}, bf16[384,512]{1,0:T(8,128)(2,1)S(1)}, u32[]{:S(2)}, u32[]{:S(2)}) %collective-permute-start.10) | collective-permute-done | bytes 393248 | tf_op jit(solution)/shard_map/ppermute | solution.py:345
  18.8 3.6 %collective-permute-start.13 = (bf16[96,512]{1,0:T(8,128)(2,1)S(1)}, bf16[96,512]{1,0:T(8,128)(2,1)S(1)}, u32[]{:S(2)}, u32[]{:S(2)}) collective-permute-start(bf16[96,512]{1,0:T(8,128)(2,1)S(1)} %get-tuple-element.70), channel_id=1, source_target_pairs={{0,12},{2,14},{4,8},{6,10},{8,4},{10,6},{12,0},{14,2},{16,28},{18,... | collective-permute-start | bytes 294920 | tf_op jit(solution)/shard_map/ppermute | solution.py:345
  23.1 1.9 %collective-permute-start.4 = (bf16[2,512,512]{2,1,0:T(8,128)(2,1)S(1)}, bf16[2,512,512]{2,1,0:T(8,128)(2,1)}, u32[]{:S(2)}, u32[]{:S(2)}) collective-permute-start(bf16[2,512,512]{2,1,0:T(8,128)(2,1)S(1)} %copy-done.2), channel_id=1, source_target_pairs={{0,2},{2,0},{4,6},{6,4},{8,10},{10,8},{12,14},{14,12},{16,18},{18,... | collective-permute-start | bytes 3145736 | tf_op jit(solution)/shard_map/ppermute | solution.py:345
  25.0 2.6 %collective-permute-start.5 = (bf16[96,512]{1,0:T(8,128)(2,1)S(1)}, bf16[96,512]{1,0:T(8,128)(2,1)S(1)}, u32[]{:S(2)}, u32[]{:S(2)}) collective-permute-start(bf16[96,512]{1,0:T(8,128)(2,1)S(1)} %fusion.5.p_ref), channel_id=1, source_target_pairs={{0,16},{2,18},{4,20},{6,22},{8,24},{10,26},{12,28},{14,30},{16,0},... | collective-permute-start | bytes 294920 | tf_op jit(solution)/shard_map/ppermute | solution.py:345
  28.6 2.6 %collective-permute-start.14 = (bf16[96,512]{1,0:T(8,128)(2,1)S(1)}, bf16[96,512]{1,0:T(8,128)(2,1)S(1)}, u32[]{:S(2)}, u32[]{:S(2)}) collective-permute-start(bf16[96,512]{1,0:T(8,128)(2,1)S(1)} %fusion.2.p_ref), channel_id=1, source_target_pairs={{0,16},{2,18},{4,20},{6,22},{8,24},{10,26},{12,28},{14,30},{16,0},... | collective-permute-start | bytes 294920 | tf_op jit(solution)/shard_map/ppermute | solution.py:345
  32.5 1.5 %collective-permute-start.7 = (bf16[96,512]{1,0:T(8,128)(2,1)S(1)}, bf16[96,512]{1,0:T(8,128)(2,1)S(1)}, u32[]{:S(2)}, u32[]{:S(2)}) collective-permute-start(bf16[96,512]{1,0:T(8,128)(2,1)S(1)} %get-tuple-element.41.refs_0_), channel_id=1, source_target_pairs={{0,8},{2,10},{4,12},{6,14},{8,0},{10,2},{12,4},{14,6},{16,24},{18,... | collective-permute-start | bytes 294920 | tf_op jit(solution)/shard_map/ppermute | solution.py:345
  34.0 1.7 %collective-permute-start.8 = (bf16[96,512]{1,0:T(8,128)(2,1)S(1)}, bf16[96,512]{1,0:T(8,128)(2,1)S(1)}, u32[]{:S(2)}, u32[]{:S(2)}) collective-permute-start(bf16[96,512]{1,0:T(8,128)(2,1)S(1)} %get-tuple-element.41.refs_0_), channel_id=1, source_target_pairs={{0,12},{2,14},{4,8},{6,10},{8,4},{10,6},{12,0},{14,2},{16,28},{18,... | collective-permute-start | bytes 294920 | tf_op jit(solution)/shard_map/ppermute | solution.py:345
  36.8 1.6 %collective-permute-start.16 = (bf16[96,512]{1,0:T(8,128)(2,1)S(1)}, bf16[96,512]{1,0:T(8,128)(2,1)S(1)}, u32[]{:S(2)}, u32[]{:S(2)}) collective-permute-start(bf16[96,512]{1,0:T(8,128)(2,1)S(1)} %get-tuple-element.45.refs_5_), channel_id=1, source_target_pairs={{0,8},{2,10},{4,12},{6,14},{8,0},{10,2},{12,4},{14,6},{16,24},{18,... | collective-permute-start | bytes 294920 | tf_op jit(solution)/shard_map/ppermute | solution.py:345
  40.5 1.6 %collective-permute-start.9 = (bf16[384,512]{1,0:T(8,128)(2,1)}, bf16[384,512]{1,0:T(8,128)(2,1)S(1)}, u32[]{:S(2)}, u32[]{:S(2)}) collective-permute-start(bf16[384,512]{1,0:T(8,128)(2,1)} %pad_maximum_fusion), channel_id=1, source_target_pairs={{0,2},{2,0},{4,6},{6,4},{8,10},{10,8},{12,14},{14,12},{16,18},{18,... | collective-permute-start | bytes 1179656 | tf_op jit(solution)/shard_map/ppermute | solution.py:345
  42.1 2.0 %collective-permute-done.17.refs_8_ = bf16[96,512]{1,0:T(8,128)(2,1)S(1)} collective-permute-done((bf16[96,512]{1,0:T(8,128)(2,1)S(1)}, bf16[96,512]{1,0:T(8,128)(2,1)S(1)}, u32[]{:S(2)}, u32[]{:S(2)}) %collective-permute-start.17) | collective-permute-done | bytes 98336 | tf_op jit(solution)/shard_map/ppermute | solution.py:345
  46.1 2.3 %collective-permute-done.9.refs_4_ = bf16[384,512]{1,0:T(8,128)(2,1)S(1)} collective-permute-done((bf16[384,512]{1,0:T(8,128)(2,1)}, bf16[384,512]{1,0:T(8,128)(2,1)S(1)}, u32[]{:S(2)}, u32[]{:S(2)}) %collective-permute-start.9) | collective-permute-done | bytes 393248 | tf_op jit(solution)/shard_map/ppermute | solution.py:345
  48.5 4.4 %collective-permute-done.18.refs_9_ = bf16[384,512]{1,0:T(8,128)(2,1)S(1)} collective-permute-done((bf16[384,512]{1,0:T(8,128)(2,1)}, bf16[384,512]{1,0:T(8,128)(2,1)S(1)}, u32[]{:S(2)}, u32[]{:S(2)}) %collective-permute-start.18) | collective-permute-done | bytes 393248 | tf_op jit(solution)/shard_map/ppermute | solution.py:345
  52.8 4.6 %next_grads.1 = (bf16[96,512]{1,0:T(8,128)(2,1)S(1)}, bf16[96,512]{1,0:T(8,128)(2,1)S(1)}, bf16[96,512]{1,0:T(8,128)(2,1)S(1)}, bf16[96,512]{1,0:T(8,128)(2,1)S(...) custom-call(s32[1]{0:T(128)} %bitcast.me_ref, ...), custom_call_target="tpu_custom_call" | custom-call | tf_op jit(solution)/shard_map/next_grads/pallas_call | solution.py:170
  57.5 1.6 %collective-permute-start.27 = (bf16[96,512]{1,0:T(8,128)(2,1)S(1)}, bf16[96,512]{1,0:T(8,128)(2,1)S(1)}, u32[]{:S(2)}, u32[]{:S(2)}) collective-permute-start(bf16[96,512]{1,0:T(8,128)(2,1)S(1)} %get-tuple-element.58), channel_id=1, source_target_pairs={{0,12},{2,14},{4,8},{6,10},{8,4},{10,6},{12,0},{14,2},{16,28},{18,... | collective-permute-start | bytes 294920 | tf_op jit(solution)/shard_map/ppermute | solution.py:345
  61.3 1.6 %collective-permute-start.21 = (bf16[96,512]{1,0:T(8,128)(2,1)S(1)}, bf16[96,512]{1,0:T(8,128)(2,1)S(1)}, u32[]{:S(2)}, u32[]{:S(2)}) collective-permute-start(bf16[96,512]{1,0:T(8,128)(2,1)S(1)} %get-tuple-element.49), channel_id=1, source_target_pairs={{0,12},{2,14},{4,8},{6,10},{8,4},{10,6},{12,0},{14,2},{16,28},{18,... | collective-permute-start | bytes 294920 | tf_op jit(solution)/shard_map/ppermute | solution.py:345
  63.0 1.3 %collective-permute-start.20 = (bf16[96,512]{1,0:T(8,128)(2,1)S(1)}, bf16[96,512]{1,0:T(8,128)(2,1)S(1)}, u32[]{:S(2)}, u32[]{:S(2)}) collective-permute-start(bf16[96,512]{1,0:T(8,128)(2,1)S(1)} %get-tuple-element.48), channel_id=1, source_target_pairs={{0,8},{2,10},{4,12},{6,14},{8,0},{10,2},{12,4},{14,6},{16,24},{18,... | collective-permute-start | bytes 294920 | tf_op jit(solution)/shard_map/ppermute | solution.py:345
  65.2 3.2 %collective-permute-start.28 = (bf16[96,512]{1,0:T(8,128)(2,1)S(1)}, bf16[96,512]{1,0:T(8,128)(2,1)S(1)}, u32[]{:S(2)}, u32[]{:S(2)}) collective-permute-start(bf16[96,512]{1,0:T(8,128)(2,1)S(1)} %add_convert_fusion.p_ref), channel_id=1, source_target_pairs={{0,16},{2,18},{4,20},{6,22},{8,24},{10,26},{12,28},{14,30},{16,0},... | collective-permute-start | bytes 294920 | tf_op jit(solution)/shard_map/ppermute | solution.py:345
  68.3 3.4 %collective-permute-done.20 = bf16[96,512]{1,0:T(8,128)(2,1)S(1)} collective-permute-done((bf16[96,512]{1,0:T(8,128)(2,1)S(1)}, bf16[96,512]{1,0:T(8,128)(2,1)S(1)}, u32[]{:S(2)}, u32[]{:S(2)}) %collective-permute-start.20) | collective-permute-done | bytes 98336 | tf_op jit(solution)/shard_map/ppermute | solution.py:345
  74.3 1.8 %collective-permute-start.30 = (bf16[96,512]{1,0:T(8,128)(2,1)S(1)}, bf16[96,512]{1,0:T(8,128)(2,1)S(1)}, u32[]{:S(2)}, u32[]{:S(2)}) collective-permute-start(bf16[96,512]{1,0:T(8,128)(2,1)S(1)} %update.7.refs_0_), channel_id=1, source_target_pairs={{0,8},{2,10},{4,12},{6,14},{8,0},{10,2},{12,4},{14,6},{16,24},{18,... | collective-permute-start | bytes 294920 | tf_op jit(solution)/shard_map/ppermute | solution.py:345
  76.7 2.2 %collective-permute-done.22.q_ref = bf16[96,512]{1,0:T(8,128)(2,1)S(1)} collective-permute-done((bf16[96,512]{1,0:T(8,128)(2,1)S(1)}, bf16[96,512]{1,0:T(8,128)(2,1)S(1)}, u32[]{:S(2)}, u32[]{:S(2)}) %collective-permute-start.22) | collective-permute-done | bytes 98336 | tf_op jit(solution)/shard_map/ppermute | solution.py:345
  81.3 2.5 %collective-permute-start.35 = (bf16[96,512]{1,0:T(8,128)(2,1)S(1)}, bf16[96,512]{1,0:T(8,128)(2,1)S(1)}, u32[]{:S(2)}, u32[]{:S(2)}) collective-permute-start(bf16[96,512]{1,0:T(8,128)(2,1)S(1)} %update.6.refs_5_), channel_id=1, source_target_pairs={{0,12},{2,14},{4,8},{6,10},{8,4},{10,6},{12,0},{14,2},{16,28},{18,... | collective-permute-start | bytes 294920 | tf_op jit(solution)/shard_map/ppermute | solution.py:345
  84.6 1.7 %collective-permute-done.34.refs_7_ = bf16[96,512]{1,0:T(8,128)(2,1)S(1)} collective-permute-done((bf16[96,512]{1,0:T(8,128)(2,1)S(1)}, bf16[96,512]{1,0:T(8,128)(2,1)S(1)}, u32[]{:S(2)}, u32[]{:S(2)}) %collective-permute-start.34) | collective-permute-done | bytes 98336 | tf_op jit(solution)/shard_map/ppermute | solution.py:345
  86.3 1.4 %collective-permute-done.35.refs_8_ = bf16[96,512]{1,0:T(8,128)(2,1)S(1)} collective-permute-done((bf16[96,512]{1,0:T(8,128)(2,1)S(1)}, bf16[96,512]{1,0:T(8,128)(2,1)S(1)}, u32[]{:S(2)}, u32[]{:S(2)}) %collective-permute-start.35) | collective-permute-done | bytes 98336 | tf_op jit(solution)/shard_map/ppermute | solution.py:345
  87.7 1.6 %collective-permute-start.36 = (bf16[384,512]{1,0:T(8,128)(2,1)S(1)}, bf16[384,512]{1,0:T(8,128)(2,1)S(1)}, u32[]{:S(2)}, u32[]{:S(2)}) collective-permute-start(bf16[384,512]{1,0:T(8,128)(2,1)S(1)} %pad_maximum_fusion.3), channel_id=1, source_target_pairs={{0,2},{2,0},{4,6},{6,4},{8,10},{10,8},{12,14},{14,12},{16,18},{18,... | collective-permute-start | bytes 1179656 | tf_op jit(solution)/shard_map/ppermute | solution.py:345
  90.1 1.5 %project.2.refs_0_ = bf16[2,512,1024]{2,1,0:T(8,128)(2,1)} custom-call(f32[512,1024]{1,0:T(8,128)S(1)} %project_own.2.sum_ref, bf16[512,512]{1,0:T(8,128)(2,1)S(1)} %collective-permute-done.23.o_ref, bf16[512,1024]{1,0:T(8,128)(2,1)S(1)} %collective-permute-done.24.proj_ref), custom_call_target="tpu_custom_call" | custom-call | tf_op jit(solution)/shard_map/project/pallas_call | solution.py:309
  91.9 4.2 %collective-permute-done.36.refs_9_ = bf16[384,512]{1,0:T(8,128)(2,1)S(1)} collective-permute-done((bf16[384,512]{1,0:T(8,128)(2,1)S(1)}, bf16[384,512]{1,0:T(8,128)(2,1)S(1)}, u32[]{:S(2)}, u32[]{:S(2)}) %collective-permute-start.36) | collective-permute-done | bytes 393248 | tf_op jit(solution)/shard_map/ppermute | solution.py:345
  99.2 1.5 %project.3 = bf16[2,512,1024]{2,1,0:T(8,128)(2,1)} custom-call(f32[512,1024]{1,0:T(8,128)S(1)} %project_own.3.sum_ref, bf16[512,512]{1,0:T(8,128)(2,1)S(1)} %collective-permute-done.37.o_ref, bf16[512,1024]{1,0:T(8,128)(2,1)S(1)} %collective-permute-done.24.proj_ref, bf16[2,512,1024]{2,1,0:T(8,128)(2,1)} %project.2.refs_0_), custom_call_target="tpu_custom_call", output_to_operand_aliasing={{}: (3, {})} | custom-call | tf_op jit(solution)/shard_map/project/pallas_call | solution.py:309
  (78 shorter events, 22.8 us)
Async XLA Ops:
  4.0 8.8 %collective-permute-start = (bf16[384,512]{1,0:T(8,128)(2,1)S(1)}, bf16[384,512]{1,0:T(8,128)(2,1)S(1)}, u32[]{:S(2)}, u32[]{:S(2)}) collective-permute-start(bf16[384,512]{1,0:T(8,128)(2,1)S(1)} %get-tuple-element.34), channel_id=1, source_target_pairs={{0,2},{2,0},{4,6},{6,4},{8,10},{10,8},{12,14},{14,12},{16,18},{18,... | collective-permute-start | bytes 1179656 | tf_op jit(solution)/shard_map/ppermute | solution.py:345
  7.0 11.6 %collective-permute-start.10 = (bf16[384,512]{1,0:T(8,128)(2,1)S(1)}, bf16[384,512]{1,0:T(8,128)(2,1)S(1)}, u32[]{:S(2)}, u32[]{:S(2)}) collective-permute-start(bf16[384,512]{1,0:T(8,128)(2,1)S(1)} %get-tuple-element.43), channel_id=1, source_target_pairs={{0,2},{2,0},{4,6},{6,4},{8,10},{10,8},{12,14},{14,12},{16,18},{18,... | collective-permute-start | bytes 1179656 | tf_op jit(solution)/shard_map/ppermute | solution.py:345
  12.9 9.8 %collective-permute-start.3 = (bf16[96,512]{1,0:T(8,128)(2,1)S(1)}, bf16[96,512]{1,0:T(8,128)(2,1)S(1)}, u32[]{:S(2)}, u32[]{:S(2)}) collective-permute-start(bf16[96,512]{1,0:T(8,128)(2,1)S(1)} %get-tuple-element.73), channel_id=1, source_target_pairs={{0,12},{2,14},{4,8},{6,10},{8,4},{10,6},{12,0},{14,2},{16,28},{18,... | collective-permute-start | bytes 294920 | tf_op jit(solution)/shard_map/ppermute | solution.py:345
  16.1 6.9 %collective-permute-start.2 = (bf16[96,512]{1,0:T(8,128)(2,1)S(1)}, bf16[96,512]{1,0:T(8,128)(2,1)S(1)}, u32[]{:S(2)}, u32[]{:S(2)}) collective-permute-start(bf16[96,512]{1,0:T(8,128)(2,1)S(1)} %get-tuple-element.74), channel_id=1, source_target_pairs={{0,8},{2,10},{4,12},{6,14},{8,0},{10,2},{12,4},{14,6},{16,24},{18,... | collective-permute-start | bytes 294920 | tf_op jit(solution)/shard_map/ppermute | solution.py:345
  16.5 6.5 %collective-permute-start.1 = (bf16[96,512]{1,0:T(8,128)(2,1)S(1)}, bf16[96,512]{1,0:T(8,128)(2,1)S(1)}, u32[]{:S(2)}, u32[]{:S(2)}) collective-permute-start(bf16[96,512]{1,0:T(8,128)(2,1)S(1)} %get-tuple-element.72), channel_id=1, source_target_pairs={{0,4},{2,6},{4,0},{6,2},{8,12},{10,14},{12,8},{14,10},{16,20},{18,... | collective-permute-start | bytes 294920 | tf_op jit(solution)/shard_map/ppermute | solution.py:345
  18.8 8.8 %collective-permute-start.13 = (bf16[96,512]{1,0:T(8,128)(2,1)S(1)}, bf16[96,512]{1,0:T(8,128)(2,1)S(1)}, u32[]{:S(2)}, u32[]{:S(2)}) collective-permute-start(bf16[96,512]{1,0:T(8,128)(2,1)S(1)} %get-tuple-element.70), channel_id=1, source_target_pairs={{0,12},{2,14},{4,8},{6,10},{8,4},{10,6},{12,0},{14,2},{16,28},{18,... | collective-permute-start | bytes 294920 | tf_op jit(solution)/shard_map/ppermute | solution.py:345
  22.3 6.2 %collective-permute-start.12 = (bf16[96,512]{1,0:T(8,128)(2,1)S(1)}, bf16[96,512]{1,0:T(8,128)(2,1)S(1)}, u32[]{:S(2)}, u32[]{:S(2)}) collective-permute-start(bf16[96,512]{1,0:T(8,128)(2,1)S(1)} %get-tuple-element.71), channel_id=1, source_target_pairs={{0,8},{2,10},{4,12},{6,14},{8,0},{10,2},{12,4},{14,6},{16,24},{18,... | collective-permute-start | bytes 294920 | tf_op jit(solution)/shard_map/ppermute | solution.py:345
  22.8 5.8 %collective-permute-start.11 = (bf16[96,512]{1,0:T(8,128)(2,1)S(1)}, bf16[96,512]{1,0:T(8,128)(2,1)S(1)}, u32[]{:S(2)}, u32[]{:S(2)}) collective-permute-start(bf16[96,512]{1,0:T(8,128)(2,1)S(1)} %get-tuple-element.69), channel_id=1, source_target_pairs={{0,4},{2,6},{4,0},{6,2},{8,12},{10,14},{12,8},{14,10},{16,20},{18,... | collective-permute-start | bytes 294920 | tf_op jit(solution)/shard_map/ppermute | solution.py:345
  23.1 29.8 %collective-permute-start.4 = (bf16[2,512,512]{2,1,0:T(8,128)(2,1)S(1)}, bf16[2,512,512]{2,1,0:T(8,128)(2,1)}, u32[]{:S(2)}, u32[]{:S(2)}) collective-permute-start(bf16[2,512,512]{2,1,0:T(8,128)(2,1)S(1)} %copy-done.2), channel_id=1, source_target_pairs={{0,2},{2,0},{4,6},{6,4},{8,10},{10,8},{12,14},{14,12},{16,18},{18,... | collective-permute-start | bytes 3145736 | tf_op jit(solution)/shard_map/ppermute | solution.py:345
  25.0 7.0 %collective-permute-start.5 = (bf16[96,512]{1,0:T(8,128)(2,1)S(1)}, bf16[96,512]{1,0:T(8,128)(2,1)S(1)}, u32[]{:S(2)}, u32[]{:S(2)}) collective-permute-start(bf16[96,512]{1,0:T(8,128)(2,1)S(1)} %fusion.5.p_ref), channel_id=1, source_target_pairs={{0,16},{2,18},{4,20},{6,22},{8,24},{10,26},{12,28},{14,30},{16,0},... | collective-permute-start | bytes 294920 | tf_op jit(solution)/shard_map/ppermute | solution.py:345
  28.6 7.2 %collective-permute-start.14 = (bf16[96,512]{1,0:T(8,128)(2,1)S(1)}, bf16[96,512]{1,0:T(8,128)(2,1)S(1)}, u32[]{:S(2)}, u32[]{:S(2)}) collective-permute-start(bf16[96,512]{1,0:T(8,128)(2,1)S(1)} %fusion.2.p_ref), channel_id=1, source_target_pairs={{0,16},{2,18},{4,20},{6,22},{8,24},{10,26},{12,28},{14,30},{16,0},... | collective-permute-start | bytes 294920 | tf_op jit(solution)/shard_map/ppermute | solution.py:345
  32.5 5.9 %collective-permute-start.7 = (bf16[96,512]{1,0:T(8,128)(2,1)S(1)}, bf16[96,512]{1,0:T(8,128)(2,1)S(1)}, u32[]{:S(2)}, u32[]{:S(2)}) collective-permute-start(bf16[96,512]{1,0:T(8,128)(2,1)S(1)} %get-tuple-element.41.refs_0_), channel_id=1, source_target_pairs={{0,8},{2,10},{4,12},{6,14},{8,0},{10,2},{12,4},{14,6},{16,24},{18,... | collective-permute-start | bytes 294920 | tf_op jit(solution)/shard_map/ppermute | solution.py:345
  34.0 5.7 %collective-permute-start.8 = (bf16[96,512]{1,0:T(8,128)(2,1)S(1)}, bf16[96,512]{1,0:T(8,128)(2,1)S(1)}, u32[]{:S(2)}, u32[]{:S(2)}) collective-permute-start(bf16[96,512]{1,0:T(8,128)(2,1)S(1)} %get-tuple-element.41.refs_0_), channel_id=1, source_target_pairs={{0,12},{2,14},{4,8},{6,10},{8,4},{10,6},{12,0},{14,2},{16,28},{18,... | collective-permute-start | bytes 294920 | tf_op jit(solution)/shard_map/ppermute | solution.py:345
  36.0 6.1 %collective-permute-start.15 = (bf16[96,512]{1,0:T(8,128)(2,1)S(1)}, bf16[96,512]{1,0:T(8,128)(2,1)S(1)}, u32[]{:S(2)}, u32[]{:S(2)}) collective-permute-start(bf16[96,512]{1,0:T(8,128)(2,1)S(1)} %get-tuple-element.45.refs_5_), channel_id=1, source_target_pairs={{0,4},{2,6},{4,0},{6,2},{8,12},{10,14},{12,8},{14,10},{16,20},{18,... | collective-permute-start | bytes 294920 | tf_op jit(solution)/shard_map/ppermute | solution.py:345
  38.4 5.6 %collective-permute-start.17 = (bf16[96,512]{1,0:T(8,128)(2,1)S(1)}, bf16[96,512]{1,0:T(8,128)(2,1)S(1)}, u32[]{:S(2)}, u32[]{:S(2)}) collective-permute-start(bf16[96,512]{1,0:T(8,128)(2,1)S(1)} %get-tuple-element.45.refs_5_), channel_id=1, source_target_pairs={{0,12},{2,14},{4,8},{6,10},{8,4},{10,6},{12,0},{14,2},{16,28},{18,... | collective-permute-start | bytes 294920 | tf_op jit(solution)/shard_map/ppermute | solution.py:345
  40.5 8.0 %collective-permute-start.9 = (bf16[384,512]{1,0:T(8,128)(2,1)}, bf16[384,512]{1,0:T(8,128)(2,1)S(1)}, u32[]{:S(2)}, u32[]{:S(2)}) collective-permute-start(bf16[384,512]{1,0:T(8,128)(2,1)} %pad_maximum_fusion), channel_id=1, source_target_pairs={{0,2},{2,0},{4,6},{6,4},{8,10},{10,8},{12,14},{14,12},{16,18},{18,... | collective-permute-start | bytes 1179656 | tf_op jit(solution)/shard_map/ppermute | solution.py:345
  44.8 8.0 %collective-permute-start.18 = (bf16[384,512]{1,0:T(8,128)(2,1)}, bf16[384,512]{1,0:T(8,128)(2,1)S(1)}, u32[]{:S(2)}, u32[]{:S(2)}) collective-permute-start(bf16[384,512]{1,0:T(8,128)(2,1)} %pad_maximum_fusion.1), channel_id=1, source_target_pairs={{0,2},{2,0},{4,6},{6,4},{8,10},{10,8},{12,14},{14,12},{16,18},{18,... | collective-permute-start | bytes 1179656 | tf_op jit(solution)/shard_map/ppermute | solution.py:345
  57.5 5.6 %collective-permute-start.27 = (bf16[96,512]{1,0:T(8,128)(2,1)S(1)}, bf16[96,512]{1,0:T(8,128)(2,1)S(1)}, u32[]{:S(2)}, u32[]{:S(2)}) collective-permute-start(bf16[96,512]{1,0:T(8,128)(2,1)S(1)} %get-tuple-element.58), channel_id=1, source_target_pairs={{0,12},{2,14},{4,8},{6,10},{8,4},{10,6},{12,0},{14,2},{16,28},{18,... | collective-permute-start | bytes 294920 | tf_op jit(solution)/shard_map/ppermute | solution.py:345
  59.0 5.3 %collective-permute-start.26 = (bf16[96,512]{1,0:T(8,128)(2,1)S(1)}, bf16[96,512]{1,0:T(8,128)(2,1)S(1)}, u32[]{:S(2)}, u32[]{:S(2)}) collective-permute-start(bf16[96,512]{1,0:T(8,128)(2,1)S(1)} %get-tuple-element.57), channel_id=1, source_target_pairs={{0,8},{2,10},{4,12},{6,14},{8,0},{10,2},{12,4},{14,6},{16,24},{18,... | collective-permute-start | bytes 294920 | tf_op jit(solution)/shard_map/ppermute | solution.py:345
  61.2 28.8 %collective-permute-start.24 = (bf16[512,1024]{1,0:T(8,128)(2,1)S(1)}, bf16[512,1024]{1,0:T(8,128)(2,1)S(1)}, u32[]{:S(2)}, u32[]{:S(2)}) collective-permute-start(bf16[512,1024]{1,0:T(8,128)(2,1)S(1)} %get-tuple-element.63), channel_id=1, source_target_pairs={{0,1},{1,0},{2,3},{3,2},{4,5},{5,4},{6,7},{7,6},{8,9},{9,8},{10,11... | collective-permute-start | bytes 3145736 | tf_op jit(solution)/shard_map/ppermute | solution.py:348
  61.3 7.0 %collective-permute-start.21 = (bf16[96,512]{1,0:T(8,128)(2,1)S(1)}, bf16[96,512]{1,0:T(8,128)(2,1)S(1)}, u32[]{:S(2)}, u32[]{:S(2)}) collective-permute-start(bf16[96,512]{1,0:T(8,128)(2,1)S(1)} %get-tuple-element.49), channel_id=1, source_target_pairs={{0,12},{2,14},{4,8},{6,10},{8,4},{10,6},{12,0},{14,2},{16,28},{18,... | collective-permute-start | bytes 294920 | tf_op jit(solution)/shard_map/ppermute | solution.py:345
  63.0 8.7 %collective-permute-start.20 = (bf16[96,512]{1,0:T(8,128)(2,1)S(1)}, bf16[96,512]{1,0:T(8,128)(2,1)S(1)}, u32[]{:S(2)}, u32[]{:S(2)}) collective-permute-start(bf16[96,512]{1,0:T(8,128)(2,1)S(1)} %get-tuple-element.48), channel_id=1, source_target_pairs={{0,8},{2,10},{4,12},{6,14},{8,0},{10,2},{12,4},{14,6},{16,24},{18,... | collective-permute-start | bytes 294920 | tf_op jit(solution)/shard_map/ppermute | solution.py:345
  64.4 7.3 %collective-permute-start.19 = (bf16[96,512]{1,0:T(8,128)(2,1)S(1)}, bf16[96,512]{1,0:T(8,128)(2,1)S(1)}, u32[]{:S(2)}, u32[]{:S(2)}) collective-permute-start(bf16[96,512]{1,0:T(8,128)(2,1)S(1)} %get-tuple-element.47), channel_id=1, source_target_pairs={{0,4},{2,6},{4,0},{6,2},{8,12},{10,14},{12,8},{14,10},{16,20},{18,... | collective-permute-start | bytes 294920 | tf_op jit(solution)/shard_map/ppermute | solution.py:345
  65.2 7.8 %collective-permute-start.28 = (bf16[96,512]{1,0:T(8,128)(2,1)S(1)}, bf16[96,512]{1,0:T(8,128)(2,1)S(1)}, u32[]{:S(2)}, u32[]{:S(2)}) collective-permute-start(bf16[96,512]{1,0:T(8,128)(2,1)S(1)} %add_convert_fusion.p_ref), channel_id=1, source_target_pairs={{0,16},{2,18},{4,20},{6,22},{8,24},{10,26},{12,28},{14,30},{16,0},... | collective-permute-start | bytes 294920 | tf_op jit(solution)/shard_map/ppermute | solution.py:345
  71.8 7.2 %collective-permute-start.22 = (bf16[96,512]{1,0:T(8,128)(2,1)S(1)}, bf16[96,512]{1,0:T(8,128)(2,1)S(1)}, u32[]{:S(2)}, u32[]{:S(2)}) collective-permute-start(bf16[96,512]{1,0:T(8,128)(2,1)S(1)} %add_convert_fusion.1.p_ref), channel_id=1, source_target_pairs={{0,16},{2,18},{4,20},{6,22},{8,24},{10,26},{12,28},{14,30},{16,0},... | collective-permute-start | bytes 294920 | tf_op jit(solution)/shard_map/ppermute | solution.py:345
  73.2 8.0 %collective-permute-start.29 = (bf16[96,512]{1,0:T(8,128)(2,1)S(1)}, bf16[96,512]{1,0:T(8,128)(2,1)S(1)}, u32[]{:S(2)}, u32[]{:S(2)}) collective-permute-start(bf16[96,512]{1,0:T(8,128)(2,1)S(1)} %update.7.refs_0_), channel_id=1, source_target_pairs={{0,4},{2,6},{4,0},{6,2},{8,12},{10,14},{12,8},{14,10},{16,20},{18,... | collective-permute-start | bytes 294920 | tf_op jit(solution)/shard_map/ppermute | solution.py:345
  74.3 7.0 %collective-permute-start.30 = (bf16[96,512]{1,0:T(8,128)(2,1)S(1)}, bf16[96,512]{1,0:T(8,128)(2,1)S(1)}, u32[]{:S(2)}, u32[]{:S(2)}) collective-permute-start(bf16[96,512]{1,0:T(8,128)(2,1)S(1)} %update.7.refs_0_), channel_id=1, source_target_pairs={{0,8},{2,10},{4,12},{6,14},{8,0},{10,2},{12,4},{14,6},{16,24},{18,... | collective-permute-start | bytes 294920 | tf_op jit(solution)/shard_map/ppermute | solution.py:345
  76.1 7.7 %collective-permute-start.31 = (bf16[96,512]{1,0:T(8,128)(2,1)S(1)}, bf16[96,512]{1,0:T(8,128)(2,1)S(1)}, u32[]{:S(2)}, u32[]{:S(2)}) collective-permute-start(bf16[96,512]{1,0:T(8,128)(2,1)S(1)} %update.7.refs_0_), channel_id=1, source_target_pairs={{0,12},{2,14},{4,8},{6,10},{8,4},{10,6},{12,0},{14,2},{16,28},{18,... | collective-permute-start | bytes 294920 | tf_op jit(solution)/shard_map/ppermute | solution.py:345
  81.3 6.4 %collective-permute-start.35 = (bf16[96,512]{1,0:T(8,128)(2,1)S(1)}, bf16[96,512]{1,0:T(8,128)(2,1)S(1)}, u32[]{:S(2)}, u32[]{:S(2)}) collective-permute-start(bf16[96,512]{1,0:T(8,128)(2,1)S(1)} %update.6.refs_5_), channel_id=1, source_target_pairs={{0,12},{2,14},{4,8},{6,10},{8,4},{10,6},{12,0},{14,2},{16,28},{18,... | collective-permute-start | bytes 294920 | tf_op jit(solution)/shard_map/ppermute | solution.py:345
  83.8 6.2 %collective-permute-start.23 = (bf16[512,512]{1,0:T(8,128)(2,1)S(1)}, bf16[512,512]{1,0:T(8,128)(2,1)S(1)}, u32[]{:S(2)}, u32[]{:S(2)}) collective-permute-start(bf16[512,512]{1,0:T(8,128)(2,1)S(1)} %apply.2.o_ref), channel_id=1, source_target_pairs={{0,1},{1,0},{2,3},{3,2},{4,5},{5,4},{6,7},{7,6},{8,9},{9,8},{10,11... | collective-permute-start | bytes 1572872 | tf_op jit(solution)/shard_map/ppermute | solution.py:348
  83.9 8.0 %collective-permute-start.32 = (bf16[384,512]{1,0:T(8,128)(2,1)S(1)}, bf16[384,512]{1,0:T(8,128)(2,1)S(1)}, u32[]{:S(2)}, u32[]{:S(2)}) collective-permute-start(bf16[384,512]{1,0:T(8,128)(2,1)S(1)} %pad_maximum_fusion.2), channel_id=1, source_target_pairs={{0,2},{2,0},{4,6},{6,4},{8,10},{10,8},{12,14},{14,12},{16,18},{18,... | collective-permute-start | bytes 1179656 | tf_op jit(solution)/shard_map/ppermute | solution.py:345
  87.7 8.4 %collective-permute-start.36 = (bf16[384,512]{1,0:T(8,128)(2,1)S(1)}, bf16[384,512]{1,0:T(8,128)(2,1)S(1)}, u32[]{:S(2)}, u32[]{:S(2)}) collective-permute-start(bf16[384,512]{1,0:T(8,128)(2,1)S(1)} %pad_maximum_fusion.3), channel_id=1, source_target_pairs={{0,2},{2,0},{4,6},{6,4},{8,10},{10,8},{12,14},{14,12},{16,18},{18,... | collective-permute-start | bytes 1179656 | tf_op jit(solution)/shard_map/ppermute | solution.py:345
  (10 other events, 89.6 us)

commit v7 on v5

--- a/solution.py
+++ b/solution.py
@@ -397,11 +397,13 @@
             else:
                 grads = next_grads(me, tokens, tokens_other, w)
                 pieces = [grads[4 * h : 4 * h + 4] for h in range(CHUNKS)]
-            received = [[swap(pieces[h][i].astype(bf16), bits) for i, bits in FLOWS] for h in range(CHUNKS)]
+            received = {h: [swap(pieces[h][i].astype(bf16), bits) for i, bits in FLOWS] for h in range(CHUNKS)[:: -1 if last else 1]}
             sums = [reduce_pieces(pieces[h], received[h]) for h in range(CHUNKS)]
             others = [last_exchange(p) for p in sums]
             near = []
             for h in range(CHUNKS):
+                if h:
+                    others[h] = after(others[h], near[-1][0])
                 wb, state[h] = update(sums[h], others[h], state[h], not last)
                 got = {bits: swap(wb, bits) for _, bits in FLOWS}
                 near.append([wb] + [got[bits] for bits in (2, 4, 6)])

time: 101 us -> 101 us (level)
  no operation moved by 1% of the time
where the time goes in v7:
time: 101 us
  starting transfers between devices  49.1 us (49%)
  waiting for transfers between devices  30.5 us (30%)
  Pallas kernels  18.3 us (18%)
  other arithmetic  2.05 us (2%)
    ppermute x35, starting transfers between devices, swap(): return lax.ppermute(x, ('ctx', 'head'), pairs)  48.9 us
    ppermute x35, waiting for transfers between devices, swap(): return lax.ppermute(x, ('ctx', 'head'), pairs)  29.5 us
    pallas_call x1, Pallas kernels, next_grads(): pl.pallas_call(functools.partial(next_grads_kernel, len(w)), out_shape=[j...  4.65 us
    pallas_call x1, Pallas kernels, first_grads(): pl.pallas_call(first_grads_kernel, out_shape=[jax.ShapeDtypeStruct((rows,...  3.99 us
    pallas_call x2, Pallas kernels, project(): pl.pallas_call(functools.partial(project_kernel, block), out_shape=jax.Sh...  2.92 us
    pallas_call x1, Pallas kernels, next_tokens(): pl.pallas_call(tokens_kernel, out_shape=pltpu.HBM((2, tok, width), bf16),...  2.34 us
    pallas_call x2, Pallas kernels, fast_apply(): pl.pallas_call(functools.partial(apply_kernel, len(w)), grid=(1,), out_sh...  2.09 us
  transfers between devices with their start and end apart: 38, of which 16 were waited for; matrix products, arithmetic and copies ran while one was open for 2% of the time, Pallas kernels for 7%

profile of v7, /device:TPU:0, one launch (start us, length us, event | category | flops | bytes accessed | tf_op | source)
XLA Modules:
  0.0 100.6 jit_solution(11743460327210732597)
XLA Ops:
  0.0 4.0 %first_grads.1 = (bf16[384,512]{1,0:T(8,128)(2,1)S(1)}, bf16[384,512]{1,0:T(8,128)(2,1)S(1)}, bf16[384,512]{1,0:T(8,128)(2,1)S(1)}, bf16[384,512]{1,0:T(8,128)(2...) custom-call(s32[1]{0:T(128)} %bitcast.me_ref, bf16[2,512,512]{2,1,0:T(8,128)(2,1)} %bitcast.12, ...), custom_call_target="tpu_custom_call" | custom-call | tf_op jit(solution)/shard_map/first_grads/pallas_call | solution.py:118
  4.0 3.0 %collective-permute-start = (bf16[384,512]{1,0:T(8,128)(2,1)S(1)}, bf16[384,512]{1,0:T(8,128)(2,1)S(1)}, u32[]{:S(2)}, u32[]{:S(2)}) collective-permute-start(bf16[384,512]{1,0:T(8,128)(2,1)S(1)} %get-tuple-element.36), channel_id=1, source_target_pairs={{0,2},{2,0},{4,6},{6,4},{8,10},{10,8},{12,14},{14,12},{16,18},{18,... | collective-permute-start | bytes 1179656 | tf_op jit(solution)/shard_map/ppermute | solution.py:346
  7.1 2.3 %next_tokens.1.own_hbm = bf16[2,512,512]{2,1,0:T(8,128)(2,1)} custom-call(bf16[2,512,512]{2,1,0:T(8,128)(2,1)} %bitcast.13, bf16[2,512,512]{2,1,0:T(8,128)(2,1)} %bitcast.15, f32[2,1,512]{2,1,0:T(1,128)} %bitcast.18), custom_call_target="tpu_custom_call" | custom-call | tf_op jit(solution)/shard_map/next_tokens/pallas_call | solution.py:204
  9.4 3.3 %collective-permute-done = bf16[384,512]{1,0:T(8,128)(2,1)S(1)} collective-permute-done((bf16[384,512]{1,0:T(8,128)(2,1)S(1)}, bf16[384,512]{1,0:T(8,128)(2,1)S(1)}, u32[]{:S(2)}, u32[]{:S(2)}) %collective-permute-start) | collective-permute-done | bytes 393248 | tf_op jit(solution)/shard_map/ppermute | solution.py:346
  12.9 3.1 %collective-permute-start.3 = (bf16[96,512]{1,0:T(8,128)(2,1)S(1)}, bf16[96,512]{1,0:T(8,128)(2,1)S(1)}, u32[]{:S(2)}, u32[]{:S(2)}) collective-permute-start(bf16[96,512]{1,0:T(8,128)(2,1)S(1)} %get-tuple-element.77), channel_id=1, source_target_pairs={{0,12},{2,14},{4,8},{6,10},{8,4},{10,6},{12,0},{14,2},{16,28},{18,... | collective-permute-start | bytes 294920 | tf_op jit(solution)/shard_map/ppermute | solution.py:346
  16.7 1.9 %collective-permute-done.10 = bf16[384,512]{1,0:T(8,128)(2,1)S(1)} collective-permute-done((bf16[384,512]{1,0:T(8,128)(2,1)S(1)}, bf16[384,512]{1,0:T(8,128)(2,1)S(1)}, u32[]{:S(2)}, u32[]{:S(2)}) %collective-permute-start.10) | collective-permute-done | bytes 393248 | tf_op jit(solution)/shard_map/ppermute | solution.py:346
  18.8 3.6 %collective-permute-start.13 = (bf16[96,512]{1,0:T(8,128)(2,1)S(1)}, bf16[96,512]{1,0:T(8,128)(2,1)S(1)}, u32[]{:S(2)}, u32[]{:S(2)}) collective-permute-start(bf16[96,512]{1,0:T(8,128)(2,1)S(1)} %get-tuple-element.74), channel_id=1, source_target_pairs={{0,12},{2,14},{4,8},{6,10},{8,4},{10,6},{12,0},{14,2},{16,28},{18,... | collective-permute-start | bytes 294920 | tf_op jit(solution)/shard_map/ppermute | solution.py:346
  23.1 1.9 %collective-permute-start.4 = (bf16[2,512,512]{2,1,0:T(8,128)(2,1)S(1)}, bf16[2,512,512]{2,1,0:T(8,128)(2,1)}, u32[]{:S(2)}, u32[]{:S(2)}) collective-permute-start(bf16[2,512,512]{2,1,0:T(8,128)(2,1)S(1)} %copy-done.2), channel_id=1, source_target_pairs={{0,2},{2,0},{4,6},{6,4},{8,10},{10,8},{12,14},{14,12},{16,18},{18,... | collective-permute-start | bytes 3145736 | tf_op jit(solution)/shard_map/ppermute | solution.py:346
  25.0 2.6 %collective-permute-start.5 = (bf16[96,512]{1,0:T(8,128)(2,1)S(1)}, bf16[96,512]{1,0:T(8,128)(2,1)S(1)}, u32[]{:S(2)}, u32[]{:S(2)}) collective-permute-start(bf16[96,512]{1,0:T(8,128)(2,1)S(1)} %fusion.5.p_ref), channel_id=1, source_target_pairs={{0,16},{2,18},{4,20},{6,22},{8,24},{10,26},{12,28},{14,30},{16,0},... | collective-permute-start | bytes 294920 | tf_op jit(solution)/shard_map/ppermute | solution.py:346
  28.6 2.6 %collective-permute-start.14 = (bf16[96,512]{1,0:T(8,128)(2,1)S(1)}, bf16[96,512]{1,0:T(8,128)(2,1)S(1)}, u32[]{:S(2)}, u32[]{:S(2)}) collective-permute-start(bf16[96,512]{1,0:T(8,128)(2,1)S(1)} %fusion.2.p_ref), channel_id=1, source_target_pairs={{0,16},{2,18},{4,20},{6,22},{8,24},{10,26},{12,28},{14,30},{16,0},... | collective-permute-start | bytes 294920 | tf_op jit(solution)/shard_map/ppermute | solution.py:346
  32.5 1.5 %collective-permute-start.7 = (bf16[96,512]{1,0:T(8,128)(2,1)S(1)}, bf16[96,512]{1,0:T(8,128)(2,1)S(1)}, u32[]{:S(2)}, u32[]{:S(2)}) collective-permute-start(bf16[96,512]{1,0:T(8,128)(2,1)S(1)} %get-tuple-element.43.refs_0_), channel_id=1, source_target_pairs={{0,8},{2,10},{4,12},{6,14},{8,0},{10,2},{12,4},{14,6},{16,24},{18,... | collective-permute-start | bytes 294920 | tf_op jit(solution)/shard_map/ppermute | solution.py:346
  34.0 1.7 %collective-permute-start.8 = (bf16[96,512]{1,0:T(8,128)(2,1)S(1)}, bf16[96,512]{1,0:T(8,128)(2,1)S(1)}, u32[]{:S(2)}, u32[]{:S(2)}) collective-permute-start(bf16[96,512]{1,0:T(8,128)(2,1)S(1)} %get-tuple-element.43.refs_0_), channel_id=1, source_target_pairs={{0,12},{2,14},{4,8},{6,10},{8,4},{10,6},{12,0},{14,2},{16,28},{18,... | collective-permute-start | bytes 294920 | tf_op jit(solution)/shard_map/ppermute | solution.py:346
  36.8 1.6 %collective-permute-start.16 = (bf16[96,512]{1,0:T(8,128)(2,1)S(1)}, bf16[96,512]{1,0:T(8,128)(2,1)S(1)}, u32[]{:S(2)}, u32[]{:S(2)}) collective-permute-start(bf16[96,512]{1,0:T(8,128)(2,1)S(1)} %get-tuple-element.48.refs_5_), channel_id=1, source_target_pairs={{0,8},{2,10},{4,12},{6,14},{8,0},{10,2},{12,4},{14,6},{16,24},{18,... | collective-permute-start | bytes 294920 | tf_op jit(solution)/shard_map/ppermute | solution.py:346
  40.5 1.6 %collective-permute-start.9 = (bf16[384,512]{1,0:T(8,128)(2,1)}, bf16[384,512]{1,0:T(8,128)(2,1)S(1)}, u32[]{:S(2)}, u32[]{:S(2)}) collective-permute-start(bf16[384,512]{1,0:T(8,128)(2,1)} %pad_maximum_fusion), channel_id=1, source_target_pairs={{0,2},{2,0},{4,6},{6,4},{8,10},{10,8},{12,14},{14,12},{16,18},{18,... | collective-permute-start | bytes 1179656 | tf_op jit(solution)/shard_map/ppermute | solution.py:346
  42.1 2.0 %collective-permute-done.17.refs_8_ = bf16[96,512]{1,0:T(8,128)(2,1)S(1)} collective-permute-done((bf16[96,512]{1,0:T(8,128)(2,1)S(1)}, bf16[96,512]{1,0:T(8,128)(2,1)S(1)}, u32[]{:S(2)}, u32[]{:S(2)}) %collective-permute-start.17) | collective-permute-done | bytes 98336 | tf_op jit(solution)/shard_map/ppermute | solution.py:346
  46.1 2.3 %collective-permute-done.9.refs_4_ = bf16[384,512]{1,0:T(8,128)(2,1)S(1)} collective-permute-done((bf16[384,512]{1,0:T(8,128)(2,1)}, bf16[384,512]{1,0:T(8,128)(2,1)S(1)}, u32[]{:S(2)}, u32[]{:S(2)}) %collective-permute-start.9) | collective-permute-done | bytes 393248 | tf_op jit(solution)/shard_map/ppermute | solution.py:346
  48.5 4.4 %collective-permute-done.18.refs_9_ = bf16[384,512]{1,0:T(8,128)(2,1)S(1)} collective-permute-done((bf16[384,512]{1,0:T(8,128)(2,1)}, bf16[384,512]{1,0:T(8,128)(2,1)S(1)}, u32[]{:S(2)}, u32[]{:S(2)}) %collective-permute-start.18) | collective-permute-done | bytes 393248 | tf_op jit(solution)/shard_map/ppermute | solution.py:346
  52.8 4.7 %next_grads.1 = (bf16[96,512]{1,0:T(8,128)(2,1)S(1)}, bf16[96,512]{1,0:T(8,128)(2,1)S(1)}, bf16[96,512]{1,0:T(8,128)(2,1)S(1)}, bf16[96,512]{1,0:T(8,128)(2,1)S(...) custom-call(s32[1]{0:T(128)} %bitcast.me_ref, ...), custom_call_target="tpu_custom_call" | custom-call | tf_op jit(solution)/shard_map/next_grads/pallas_call | solution.py:171
  57.5 1.6 %collective-permute-start.25 = (bf16[96,512]{1,0:T(8,128)(2,1)S(1)}, bf16[96,512]{1,0:T(8,128)(2,1)S(1)}, u32[]{:S(2)}, u32[]{:S(2)}) collective-permute-start(bf16[96,512]{1,0:T(8,128)(2,1)S(1)} %get-tuple-element.56), channel_id=1, source_target_pairs={{0,12},{2,14},{4,8},{6,10},{8,4},{10,6},{12,0},{14,2},{16,28},{18,... | collective-permute-start | bytes 294920 | tf_op jit(solution)/shard_map/ppermute | solution.py:346
  61.4 1.6 %collective-permute-start.21 = (bf16[96,512]{1,0:T(8,128)(2,1)S(1)}, bf16[96,512]{1,0:T(8,128)(2,1)S(1)}, u32[]{:S(2)}, u32[]{:S(2)}) collective-permute-start(bf16[96,512]{1,0:T(8,128)(2,1)S(1)} %get-tuple-element.52), channel_id=1, source_target_pairs={{0,12},{2,14},{4,8},{6,10},{8,4},{10,6},{12,0},{14,2},{16,28},{18,... | collective-permute-start | bytes 294920 | tf_op jit(solution)/shard_map/ppermute | solution.py:346
  63.1 1.3 %collective-permute-start.20 = (bf16[96,512]{1,0:T(8,128)(2,1)S(1)}, bf16[96,512]{1,0:T(8,128)(2,1)S(1)}, u32[]{:S(2)}, u32[]{:S(2)}) collective-permute-start(bf16[96,512]{1,0:T(8,128)(2,1)S(1)} %get-tuple-element.51), channel_id=1, source_target_pairs={{0,8},{2,10},{4,12},{6,14},{8,0},{10,2},{12,4},{14,6},{16,24},{18,... | collective-permute-start | bytes 294920 | tf_op jit(solution)/shard_map/ppermute | solution.py:346
  65.2 3.2 %collective-permute-start.26 = (bf16[96,512]{1,0:T(8,128)(2,1)S(1)}, bf16[96,512]{1,0:T(8,128)(2,1)S(1)}, u32[]{:S(2)}, u32[]{:S(2)}) collective-permute-start(bf16[96,512]{1,0:T(8,128)(2,1)S(1)} %add_convert_fusion.p_ref), channel_id=1, source_target_pairs={{0,16},{2,18},{4,20},{6,22},{8,24},{10,26},{12,28},{14,30},{16,0},... | collective-permute-start | bytes 294920 | tf_op jit(solution)/shard_map/ppermute | solution.py:346
  68.4 3.4 %collective-permute-done.20 = bf16[96,512]{1,0:T(8,128)(2,1)S(1)} collective-permute-done((bf16[96,512]{1,0:T(8,128)(2,1)S(1)}, bf16[96,512]{1,0:T(8,128)(2,1)S(1)}, u32[]{:S(2)}, u32[]{:S(2)}) %collective-permute-start.20) | collective-permute-done | bytes 98336 | tf_op jit(solution)/shard_map/ppermute | solution.py:346
  74.3 1.8 %collective-permute-start.30 = (bf16[96,512]{1,0:T(8,128)(2,1)S(1)}, bf16[96,512]{1,0:T(8,128)(2,1)S(1)}, u32[]{:S(2)}, u32[]{:S(2)}) collective-permute-start(bf16[96,512]{1,0:T(8,128)(2,1)S(1)} %update.6.refs_0_), channel_id=1, source_target_pairs={{0,8},{2,10},{4,12},{6,14},{8,0},{10,2},{12,4},{14,6},{16,24},{18,... | collective-permute-start | bytes 294920 | tf_op jit(solution)/shard_map/ppermute | solution.py:346
  76.8 2.2 %collective-permute-done.22.q_ref = bf16[96,512]{1,0:T(8,128)(2,1)S(1)} collective-permute-done((bf16[96,512]{1,0:T(8,128)(2,1)S(1)}, bf16[96,512]{1,0:T(8,128)(2,1)S(1)}, u32[]{:S(2)}, u32[]{:S(2)}) %collective-permute-start.22) | collective-permute-done | bytes 98336 | tf_op jit(solution)/shard_map/ppermute | solution.py:346
  81.4 2.5 %collective-permute-start.35 = (bf16[96,512]{1,0:T(8,128)(2,1)S(1)}, bf16[96,512]{1,0:T(8,128)(2,1)S(1)}, u32[]{:S(2)}, u32[]{:S(2)}) collective-permute-start(bf16[96,512]{1,0:T(8,128)(2,1)S(1)} %update.7.refs_5_), channel_id=1, source_target_pairs={{0,12},{2,14},{4,8},{6,10},{8,4},{10,6},{12,0},{14,2},{16,28},{18,... | collective-permute-start | bytes 294920 | tf_op jit(solution)/shard_map/ppermute | solution.py:346
  84.6 1.7 %collective-permute-done.34.refs_7_ = bf16[96,512]{1,0:T(8,128)(2,1)S(1)} collective-permute-done((bf16[96,512]{1,0:T(8,128)(2,1)S(1)}, bf16[96,512]{1,0:T(8,128)(2,1)S(1)}, u32[]{:S(2)}, u32[]{:S(2)}) %collective-permute-start.34) | collective-permute-done | bytes 98336 | tf_op jit(solution)/shard_map/ppermute | solution.py:346
  86.3 1.5 %collective-permute-done.35.refs_8_ = bf16[96,512]{1,0:T(8,128)(2,1)S(1)} collective-permute-done((bf16[96,512]{1,0:T(8,128)(2,1)S(1)}, bf16[96,512]{1,0:T(8,128)(2,1)S(1)}, u32[]{:S(2)}, u32[]{:S(2)}) %collective-permute-start.35) | collective-permute-done | bytes 98336 | tf_op jit(solution)/shard_map/ppermute | solution.py:346
  87.8 1.6 %collective-permute-start.36 = (bf16[384,512]{1,0:T(8,128)(2,1)S(1)}, bf16[384,512]{1,0:T(8,128)(2,1)S(1)}, u32[]{:S(2)}, u32[]{:S(2)}) collective-permute-start(bf16[384,512]{1,0:T(8,128)(2,1)S(1)} %pad_maximum_fusion.3), channel_id=1, source_target_pairs={{0,2},{2,0},{4,6},{6,4},{8,10},{10,8},{12,14},{14,12},{16,18},{18,... | collective-permute-start | bytes 1179656 | tf_op jit(solution)/shard_map/ppermute | solution.py:346
  90.2 1.5 %project.2.refs_0_ = bf16[2,512,1024]{2,1,0:T(8,128)(2,1)} custom-call(f32[512,1024]{1,0:T(8,128)S(1)} %project_own.2.sum_ref, bf16[512,512]{1,0:T(8,128)(2,1)S(1)} %collective-permute-done.27.o_ref, bf16[512,1024]{1,0:T(8,128)(2,1)S(1)} %collective-permute-done.28.proj_ref), custom_call_target="tpu_custom_call" | custom-call | tf_op jit(solution)/shard_map/project/pallas_call | solution.py:310
  91.8 4.2 %collective-permute-done.36.refs_9_ = bf16[384,512]{1,0:T(8,128)(2,1)S(1)} collective-permute-done((bf16[384,512]{1,0:T(8,128)(2,1)S(1)}, bf16[384,512]{1,0:T(8,128)(2,1)S(1)}, u32[]{:S(2)}, u32[]{:S(2)}) %collective-permute-start.36) | collective-permute-done | bytes 393248 | tf_op jit(solution)/shard_map/ppermute | solution.py:346
  99.1 1.5 %project.3 = bf16[2,512,1024]{2,1,0:T(8,128)(2,1)} custom-call(f32[512,1024]{1,0:T(8,128)S(1)} %project_own.3.sum_ref, bf16[512,512]{1,0:T(8,128)(2,1)S(1)} %collective-permute-done.37.o_ref, bf16[512,1024]{1,0:T(8,128)(2,1)S(1)} %collective-permute-done.28.proj_ref, bf16[2,512,1024]{2,1,0:T(8,128)(2,1)} %project.2.refs_0_), custom_call_target="tpu_custom_call", output_to_operand_aliasing={{}: (3, {})} | custom-call | tf_op jit(solution)/shard_map/project/pallas_call | solution.py:310
  (78 shorter events, 22.8 us)
Async XLA Ops:
  4.0 8.8 %collective-permute-start = (bf16[384,512]{1,0:T(8,128)(2,1)S(1)}, bf16[384,512]{1,0:T(8,128)(2,1)S(1)}, u32[]{:S(2)}, u32[]{:S(2)}) collective-permute-start(bf16[384,512]{1,0:T(8,128)(2,1)S(1)} %get-tuple-element.36), channel_id=1, source_target_pairs={{0,2},{2,0},{4,6},{6,4},{8,10},{10,8},{12,14},{14,12},{16,18},{18,... | collective-permute-start | bytes 1179656 | tf_op jit(solution)/shard_map/ppermute | solution.py:346
  7.0 11.6 %collective-permute-start.10 = (bf16[384,512]{1,0:T(8,128)(2,1)S(1)}, bf16[384,512]{1,0:T(8,128)(2,1)S(1)}, u32[]{:S(2)}, u32[]{:S(2)}) collective-permute-start(bf16[384,512]{1,0:T(8,128)(2,1)S(1)} %get-tuple-element.45), channel_id=1, source_target_pairs={{0,2},{2,0},{4,6},{6,4},{8,10},{10,8},{12,14},{14,12},{16,18},{18,... | collective-permute-start | bytes 1179656 | tf_op jit(solution)/shard_map/ppermute | solution.py:346
  12.9 9.8 %collective-permute-start.3 = (bf16[96,512]{1,0:T(8,128)(2,1)S(1)}, bf16[96,512]{1,0:T(8,128)(2,1)S(1)}, u32[]{:S(2)}, u32[]{:S(2)}) collective-permute-start(bf16[96,512]{1,0:T(8,128)(2,1)S(1)} %get-tuple-element.77), channel_id=1, source_target_pairs={{0,12},{2,14},{4,8},{6,10},{8,4},{10,6},{12,0},{14,2},{16,28},{18,... | collective-permute-start | bytes 294920 | tf_op jit(solution)/shard_map/ppermute | solution.py:346
  16.1 6.9 %collective-permute-start.2 = (bf16[96,512]{1,0:T(8,128)(2,1)S(1)}, bf16[96,512]{1,0:T(8,128)(2,1)S(1)}, u32[]{:S(2)}, u32[]{:S(2)}) collective-permute-start(bf16[96,512]{1,0:T(8,128)(2,1)S(1)} %get-tuple-element.78), channel_id=1, source_target_pairs={{0,8},{2,10},{4,12},{6,14},{8,0},{10,2},{12,4},{14,6},{16,24},{18,... | collective-permute-start | bytes 294920 | tf_op jit(solution)/shard_map/ppermute | solution.py:346
  16.5 6.5 %collective-permute-start.1 = (bf16[96,512]{1,0:T(8,128)(2,1)S(1)}, bf16[96,512]{1,0:T(8,128)(2,1)S(1)}, u32[]{:S(2)}, u32[]{:S(2)}) collective-permute-start(bf16[96,512]{1,0:T(8,128)(2,1)S(1)} %get-tuple-element.76), channel_id=1, source_target_pairs={{0,4},{2,6},{4,0},{6,2},{8,12},{10,14},{12,8},{14,10},{16,20},{18,... | collective-permute-start | bytes 294920 | tf_op jit(solution)/shard_map/ppermute | solution.py:346
  18.8 8.8 %collective-permute-start.13 = (bf16[96,512]{1,0:T(8,128)(2,1)S(1)}, bf16[96,512]{1,0:T(8,128)(2,1)S(1)}, u32[]{:S(2)}, u32[]{:S(2)}) collective-permute-start(bf16[96,512]{1,0:T(8,128)(2,1)S(1)} %get-tuple-element.74), channel_id=1, source_target_pairs={{0,12},{2,14},{4,8},{6,10},{8,4},{10,6},{12,0},{14,2},{16,28},{18,... | collective-permute-start | bytes 294920 | tf_op jit(solution)/shard_map/ppermute | solution.py:346
  22.3 6.2 %collective-permute-start.12 = (bf16[96,512]{1,0:T(8,128)(2,1)S(1)}, bf16[96,512]{1,0:T(8,128)(2,1)S(1)}, u32[]{:S(2)}, u32[]{:S(2)}) collective-permute-start(bf16[96,512]{1,0:T(8,128)(2,1)S(1)} %get-tuple-element.75), channel_id=1, source_target_pairs={{0,8},{2,10},{4,12},{6,14},{8,0},{10,2},{12,4},{14,6},{16,24},{18,... | collective-permute-start | bytes 294920 | tf_op jit(solution)/shard_map/ppermute | solution.py:346
  22.8 5.8 %collective-permute-start.11 = (bf16[96,512]{1,0:T(8,128)(2,1)S(1)}, bf16[96,512]{1,0:T(8,128)(2,1)S(1)}, u32[]{:S(2)}, u32[]{:S(2)}) collective-permute-start(bf16[96,512]{1,0:T(8,128)(2,1)S(1)} %get-tuple-element.73), channel_id=1, source_target_pairs={{0,4},{2,6},{4,0},{6,2},{8,12},{10,14},{12,8},{14,10},{16,20},{18,... | collective-permute-start | bytes 294920 | tf_op jit(solution)/shard_map/ppermute | solution.py:346
  23.1 29.8 %collective-permute-start.4 = (bf16[2,512,512]{2,1,0:T(8,128)(2,1)S(1)}, bf16[2,512,512]{2,1,0:T(8,128)(2,1)}, u32[]{:S(2)}, u32[]{:S(2)}) collective-permute-start(bf16[2,512,512]{2,1,0:T(8,128)(2,1)S(1)} %copy-done.2), channel_id=1, source_target_pairs={{0,2},{2,0},{4,6},{6,4},{8,10},{10,8},{12,14},{14,12},{16,18},{18,... | collective-permute-start | bytes 3145736 | tf_op jit(solution)/shard_map/ppermute | solution.py:346
  25.0 7.0 %collective-permute-start.5 = (bf16[96,512]{1,0:T(8,128)(2,1)S(1)}, bf16[96,512]{1,0:T(8,128)(2,1)S(1)}, u32[]{:S(2)}, u32[]{:S(2)}) collective-permute-start(bf16[96,512]{1,0:T(8,128)(2,1)S(1)} %fusion.5.p_ref), channel_id=1, source_target_pairs={{0,16},{2,18},{4,20},{6,22},{8,24},{10,26},{12,28},{14,30},{16,0},... | collective-permute-start | bytes 294920 | tf_op jit(solution)/shard_map/ppermute | solution.py:346
  28.6 7.2 %collective-permute-start.14 = (bf16[96,512]{1,0:T(8,128)(2,1)S(1)}, bf16[96,512]{1,0:T(8,128)(2,1)S(1)}, u32[]{:S(2)}, u32[]{:S(2)}) collective-permute-start(bf16[96,512]{1,0:T(8,128)(2,1)S(1)} %fusion.2.p_ref), channel_id=1, source_target_pairs={{0,16},{2,18},{4,20},{6,22},{8,24},{10,26},{12,28},{14,30},{16,0},... | collective-permute-start | bytes 294920 | tf_op jit(solution)/shard_map/ppermute | solution.py:346
  32.5 5.9 %collective-permute-start.7 = (bf16[96,512]{1,0:T(8,128)(2,1)S(1)}, bf16[96,512]{1,0:T(8,128)(2,1)S(1)}, u32[]{:S(2)}, u32[]{:S(2)}) collective-permute-start(bf16[96,512]{1,0:T(8,128)(2,1)S(1)} %get-tuple-element.43.refs_0_), channel_id=1, source_target_pairs={{0,8},{2,10},{4,12},{6,14},{8,0},{10,2},{12,4},{14,6},{16,24},{18,... | collective-permute-start | bytes 294920 | tf_op jit(solution)/shard_map/ppermute | solution.py:346
  34.0 5.7 %collective-permute-start.8 = (bf16[96,512]{1,0:T(8,128)(2,1)S(1)}, bf16[96,512]{1,0:T(8,128)(2,1)S(1)}, u32[]{:S(2)}, u32[]{:S(2)}) collective-permute-start(bf16[96,512]{1,0:T(8,128)(2,1)S(1)} %get-tuple-element.43.refs_0_), channel_id=1, source_target_pairs={{0,12},{2,14},{4,8},{6,10},{8,4},{10,6},{12,0},{14,2},{16,28},{18,... | collective-permute-start | bytes 294920 | tf_op jit(solution)/shard_map/ppermute | solution.py:346
  36.0 6.1 %collective-permute-start.15 = (bf16[96,512]{1,0:T(8,128)(2,1)S(1)}, bf16[96,512]{1,0:T(8,128)(2,1)S(1)}, u32[]{:S(2)}, u32[]{:S(2)}) collective-permute-start(bf16[96,512]{1,0:T(8,128)(2,1)S(1)} %get-tuple-element.48.refs_5_), channel_id=1, source_target_pairs={{0,4},{2,6},{4,0},{6,2},{8,12},{10,14},{12,8},{14,10},{16,20},{18,... | collective-permute-start | bytes 294920 | tf_op jit(solution)/shard_map/ppermute | solution.py:346
  38.4 5.6 %collective-permute-start.17 = (bf16[96,512]{1,0:T(8,128)(2,1)S(1)}, bf16[96,512]{1,0:T(8,128)(2,1)S(1)}, u32[]{:S(2)}, u32[]{:S(2)}) collective-permute-start(bf16[96,512]{1,0:T(8,128)(2,1)S(1)} %get-tuple-element.48.refs_5_), channel_id=1, source_target_pairs={{0,12},{2,14},{4,8},{6,10},{8,4},{10,6},{12,0},{14,2},{16,28},{18,... | collective-permute-start | bytes 294920 | tf_op jit(solution)/shard_map/ppermute | solution.py:346
  40.5 8.0 %collective-permute-start.9 = (bf16[384,512]{1,0:T(8,128)(2,1)}, bf16[384,512]{1,0:T(8,128)(2,1)S(1)}, u32[]{:S(2)}, u32[]{:S(2)}) collective-permute-start(bf16[384,512]{1,0:T(8,128)(2,1)} %pad_maximum_fusion), channel_id=1, source_target_pairs={{0,2},{2,0},{4,6},{6,4},{8,10},{10,8},{12,14},{14,12},{16,18},{18,... | collective-permute-start | bytes 1179656 | tf_op jit(solution)/shard_map/ppermute | solution.py:346
  44.8 8.0 %collective-permute-start.18 = (bf16[384,512]{1,0:T(8,128)(2,1)}, bf16[384,512]{1,0:T(8,128)(2,1)S(1)}, u32[]{:S(2)}, u32[]{:S(2)}) collective-permute-start(bf16[384,512]{1,0:T(8,128)(2,1)} %pad_maximum_fusion.1), channel_id=1, source_target_pairs={{0,2},{2,0},{4,6},{6,4},{8,10},{10,8},{12,14},{14,12},{16,18},{18,... | collective-permute-start | bytes 1179656 | tf_op jit(solution)/shard_map/ppermute | solution.py:346
  57.5 5.6 %collective-permute-start.25 = (bf16[96,512]{1,0:T(8,128)(2,1)S(1)}, bf16[96,512]{1,0:T(8,128)(2,1)S(1)}, u32[]{:S(2)}, u32[]{:S(2)}) collective-permute-start(bf16[96,512]{1,0:T(8,128)(2,1)S(1)} %get-tuple-element.56), channel_id=1, source_target_pairs={{0,12},{2,14},{4,8},{6,10},{8,4},{10,6},{12,0},{14,2},{16,28},{18,... | collective-permute-start | bytes 294920 | tf_op jit(solution)/shard_map/ppermute | solution.py:346
  59.1 5.3 %collective-permute-start.24 = (bf16[96,512]{1,0:T(8,128)(2,1)S(1)}, bf16[96,512]{1,0:T(8,128)(2,1)S(1)}, u32[]{:S(2)}, u32[]{:S(2)}) collective-permute-start(bf16[96,512]{1,0:T(8,128)(2,1)S(1)} %get-tuple-element.55), channel_id=1, source_target_pairs={{0,8},{2,10},{4,12},{6,14},{8,0},{10,2},{12,4},{14,6},{16,24},{18,... | collective-permute-start | bytes 294920 | tf_op jit(solution)/shard_map/ppermute | solution.py:346
  61.3 28.9 %collective-permute-start.28 = (bf16[512,1024]{1,0:T(8,128)(2,1)S(1)}, bf16[512,1024]{1,0:T(8,128)(2,1)S(1)}, u32[]{:S(2)}, u32[]{:S(2)}) collective-permute-start(bf16[512,1024]{1,0:T(8,128)(2,1)S(1)} %get-tuple-element.67), channel_id=1, source_target_pairs={{0,1},{1,0},{2,3},{3,2},{4,5},{5,4},{6,7},{7,6},{8,9},{9,8},{10,11... | collective-permute-start | bytes 3145736 | tf_op jit(solution)/shard_map/ppermute | solution.py:349
  61.4 7.0 %collective-permute-start.21 = (bf16[96,512]{1,0:T(8,128)(2,1)S(1)}, bf16[96,512]{1,0:T(8,128)(2,1)S(1)}, u32[]{:S(2)}, u32[]{:S(2)}) collective-permute-start(bf16[96,512]{1,0:T(8,128)(2,1)S(1)} %get-tuple-element.52), channel_id=1, source_target_pairs={{0,12},{2,14},{4,8},{6,10},{8,4},{10,6},{12,0},{14,2},{16,28},{18,... | collective-permute-start | bytes 294920 | tf_op jit(solution)/shard_map/ppermute | solution.py:346
  63.1 8.7 %collective-permute-start.20 = (bf16[96,512]{1,0:T(8,128)(2,1)S(1)}, bf16[96,512]{1,0:T(8,128)(2,1)S(1)}, u32[]{:S(2)}, u32[]{:S(2)}) collective-permute-start(bf16[96,512]{1,0:T(8,128)(2,1)S(1)} %get-tuple-element.51), channel_id=1, source_target_pairs={{0,8},{2,10},{4,12},{6,14},{8,0},{10,2},{12,4},{14,6},{16,24},{18,... | collective-permute-start | bytes 294920 | tf_op jit(solution)/shard_map/ppermute | solution.py:346
  64.4 7.3 %collective-permute-start.19 = (bf16[96,512]{1,0:T(8,128)(2,1)S(1)}, bf16[96,512]{1,0:T(8,128)(2,1)S(1)}, u32[]{:S(2)}, u32[]{:S(2)}) collective-permute-start(bf16[96,512]{1,0:T(8,128)(2,1)S(1)} %get-tuple-element.50), channel_id=1, source_target_pairs={{0,4},{2,6},{4,0},{6,2},{8,12},{10,14},{12,8},{14,10},{16,20},{18,... | collective-permute-start | bytes 294920 | tf_op jit(solution)/shard_map/ppermute | solution.py:346
  65.2 7.8 %collective-permute-start.26 = (bf16[96,512]{1,0:T(8,128)(2,1)S(1)}, bf16[96,512]{1,0:T(8,128)(2,1)S(1)}, u32[]{:S(2)}, u32[]{:S(2)}) collective-permute-start(bf16[96,512]{1,0:T(8,128)(2,1)S(1)} %add_convert_fusion.p_ref), channel_id=1, source_target_pairs={{0,16},{2,18},{4,20},{6,22},{8,24},{10,26},{12,28},{14,30},{16,0},... | collective-permute-start | bytes 294920 | tf_op jit(solution)/shard_map/ppermute | solution.py:346
  71.8 7.2 %collective-permute-start.22 = (bf16[96,512]{1,0:T(8,128)(2,1)S(1)}, bf16[96,512]{1,0:T(8,128)(2,1)S(1)}, u32[]{:S(2)}, u32[]{:S(2)}) collective-permute-start(bf16[96,512]{1,0:T(8,128)(2,1)S(1)} %add_convert_fusion.1.p_ref), channel_id=1, source_target_pairs={{0,16},{2,18},{4,20},{6,22},{8,24},{10,26},{12,28},{14,30},{16,0},... | collective-permute-start | bytes 294920 | tf_op jit(solution)/shard_map/ppermute | solution.py:346
  73.2 8.0 %collective-permute-start.29 = (bf16[96,512]{1,0:T(8,128)(2,1)S(1)}, bf16[96,512]{1,0:T(8,128)(2,1)S(1)}, u32[]{:S(2)}, u32[]{:S(2)}) collective-permute-start(bf16[96,512]{1,0:T(8,128)(2,1)S(1)} %update.6.refs_0_), channel_id=1, source_target_pairs={{0,4},{2,6},{4,0},{6,2},{8,12},{10,14},{12,8},{14,10},{16,20},{18,... | collective-permute-start | bytes 294920 | tf_op jit(solution)/shard_map/ppermute | solution.py:346
  74.3 7.0 %collective-permute-start.30 = (bf16[96,512]{1,0:T(8,128)(2,1)S(1)}, bf16[96,512]{1,0:T(8,128)(2,1)S(1)}, u32[]{:S(2)}, u32[]{:S(2)}) collective-permute-start(bf16[96,512]{1,0:T(8,128)(2,1)S(1)} %update.6.refs_0_), channel_id=1, source_target_pairs={{0,8},{2,10},{4,12},{6,14},{8,0},{10,2},{12,4},{14,6},{16,24},{18,... | collective-permute-start | bytes 294920 | tf_op jit(solution)/shard_map/ppermute | solution.py:346
  76.1 7.7 %collective-permute-start.31 = (bf16[96,512]{1,0:T(8,128)(2,1)S(1)}, bf16[96,512]{1,0:T(8,128)(2,1)S(1)}, u32[]{:S(2)}, u32[]{:S(2)}) collective-permute-start(bf16[96,512]{1,0:T(8,128)(2,1)S(1)} %update.6.refs_0_), channel_id=1, source_target_pairs={{0,12},{2,14},{4,8},{6,10},{8,4},{10,6},{12,0},{14,2},{16,28},{18,... | collective-permute-start | bytes 294920 | tf_op jit(solution)/shard_map/ppermute | solution.py:346
  81.4 6.4 %collective-permute-start.35 = (bf16[96,512]{1,0:T(8,128)(2,1)S(1)}, bf16[96,512]{1,0:T(8,128)(2,1)S(1)}, u32[]{:S(2)}, u32[]{:S(2)}) collective-permute-start(bf16[96,512]{1,0:T(8,128)(2,1)S(1)} %update.7.refs_5_), channel_id=1, source_target_pairs={{0,12},{2,14},{4,8},{6,10},{8,4},{10,6},{12,0},{14,2},{16,28},{18,... | collective-permute-start | bytes 294920 | tf_op jit(solution)/shard_map/ppermute | solution.py:346
  83.8 6.4 %collective-permute-start.27 = (bf16[512,512]{1,0:T(8,128)(2,1)S(1)}, bf16[512,512]{1,0:T(8,128)(2,1)S(1)}, u32[]{:S(2)}, u32[]{:S(2)}) collective-permute-start(bf16[512,512]{1,0:T(8,128)(2,1)S(1)} %apply.2.o_ref), channel_id=1, source_target_pairs={{0,1},{1,0},{2,3},{3,2},{4,5},{5,4},{6,7},{7,6},{8,9},{9,8},{10,11... | collective-permute-start | bytes 1572872 | tf_op jit(solution)/shard_map/ppermute | solution.py:349
  83.9 7.9 %collective-permute-start.32 = (bf16[384,512]{1,0:T(8,128)(2,1)S(1)}, bf16[384,512]{1,0:T(8,128)(2,1)S(1)}, u32[]{:S(2)}, u32[]{:S(2)}) collective-permute-start(bf16[384,512]{1,0:T(8,128)(2,1)S(1)} %pad_maximum_fusion.2), channel_id=1, source_target_pairs={{0,2},{2,0},{4,6},{6,4},{8,10},{10,8},{12,14},{14,12},{16,18},{18,... | collective-permute-start | bytes 1179656 | tf_op jit(solution)/shard_map/ppermute | solution.py:346
  87.8 8.2 %collective-permute-start.36 = (bf16[384,512]{1,0:T(8,128)(2,1)S(1)}, bf16[384,512]{1,0:T(8,128)(2,1)S(1)}, u32[]{:S(2)}, u32[]{:S(2)}) collective-permute-start(bf16[384,512]{1,0:T(8,128)(2,1)S(1)} %pad_maximum_fusion.3), channel_id=1, source_target_pairs={{0,2},{2,0},{4,6},{6,4},{8,10},{10,8},{12,14},{14,12},{16,18},{18,... | collective-permute-start | bytes 1179656 | tf_op jit(solution)/shard_map/ppermute | solution.py:346
  (10 other events, 89.7 us)
